TPU v7x, 32 devices: a whole 2x2x4 slice. The times are simulated.
32 devices in a mesh: dp: 16 (over z, y, core), seq: 2 (over x).
Axes of the slice: x: 2, y: 2, z: 4, core: 2. Of those that a mesh axis runs over, the one named last changes fastest.
Arguments:
- latent: bfloat16 [16384, 1408], P(('dp', 'seq')), may hold values from -6 to 6
- skip_input: bfloat16 [16384, 1408], P(('dp', 'seq')), may hold values from -6 to 6
- clip_text: bfloat16 [64, 77, 1024], P('dp', None, 'seq'), may hold values from -6 to 6
- t5_text: bfloat16 [64, 256, 2048], P('dp', None, 'seq'), may hold values from -6 to 6
- bucket: int32 [16], P('dp'), may hold values from 0 to 1
- counts: int32 [64, 2], P('dp'), may hold values from 1 to 256, as said below
- language: int32 [64], P('dp'), may hold values 0 or 1
- timesteps: int32 [64], P('dp'), may hold values from 0 to 999
- cotangent: bfloat16 [16384, 1408], P(('dp', 'seq')), may hold values from -6 to 6
- skip_weight: bfloat16 [2816, 1408], P('seq'), may hold values from -0.109375 to 0.109375
- skip_gain: float32 [1408], replicated, may hold values from 0.1 to 1.9
- time_weight: bfloat16 [256, 1408], replicated, may hold values from -0.375 to 0.375
- shift_weight: bfloat16 [1408, 1408], P(None, 'seq'), may hold values from -0.15625 to 0.15625
- norm1_gain: float32 [1408], replicated, may hold values from 0.1 to 1.9
- qkv_weight: bfloat16 [1408, 3, 1408], P(None, None, 'seq'), may hold values from -0.15625 to 0.15625
- q_gain: float32 [88], replicated, may hold values from 0.1 to 1.9
- k_gain: float32 [88], replicated, may hold values from 0.1 to 1.9
- out_weight: bfloat16 [1408, 1408], P('seq'), may hold values from -2.5 to 2.5
- norm3_gain: float32 [1408], replicated, may hold values from 0.1 to 1.9
- cross_query: bfloat16 [1408, 1408], P(None, 'seq'), may hold values from -0.15625 to 0.15625
- cq_gain: float32 [88], replicated, may hold values from 0.1 to 1.9
- t5_weight: bfloat16 [2048, 1024], P('seq'), may hold values from -0.125 to 0.125
- lang_embed: bfloat16 [2, 1024], replicated, may hold values from -6 to 6
- cross_kv: bfloat16 [1024, 2, 1408], P(None, None, 'seq'), may hold values from -0.1875 to 0.1875
- ck_gain: float32 [88], replicated, may hold values from 0.1 to 1.9
- cross_out: bfloat16 [1408, 1408], P('seq'), may hold values from -1.25 to 1.25
- norm2_gain: float32 [1408], replicated, may hold values from 0.1 to 1.9
- fc1_weight: bfloat16 [1408, 6144], P(None, 'seq'), may hold values from -0.15625 to 0.15625
- fc2_weight: bfloat16 [6144, 1408], P('seq'), may hold values from -0.078125 to 0.078125
Outputs:
- block_output: bfloat16 [16384, 1408], P(('dp', 'seq'))
- grad_latent: float32 [16384, 1408], P(('dp', 'seq'))
- grad_skip_input: float32 [16384, 1408], P(('dp', 'seq'))
- grad_clip_text: float32 [64, 77, 1024], P('dp', None, 'seq')
- grad_t5_text: float32 [64, 256, 2048], P('dp', None, 'seq')
- grad_skip_weight: float32 [2816, 1408], P('seq', 'dp')
- grad_skip_gain: float32 [1408], replicated
- grad_time_weight: float32 [256, 1408], replicated
- grad_shift_weight: float32 [1408, 1408], P('dp', 'seq')
- grad_norm1_gain: float32 [1408], replicated
- grad_qkv_weight: float32 [1408, 3, 1408], P('dp', None, 'seq')
- grad_q_gain: float32 [88], replicated
- grad_k_gain: float32 [88], replicated
- grad_out_weight: float32 [1408, 1408], P('seq', 'dp')
- grad_norm3_gain: float32 [1408], replicated
- grad_cross_query: float32 [1408, 1408], P('dp', 'seq')
- grad_cq_gain: float32 [88], replicated
- grad_t5_weight: float32 [2048, 1024], P('seq', 'dp')
- grad_lang_embed: float32 [2, 1024], replicated
- grad_cross_kv: float32 [1024, 2, 1408], P('dp', None, 'seq')
- grad_ck_gain: float32 [88], replicated
- grad_cross_out: float32 [1408, 1408], P('seq', 'dp')
- grad_norm2_gain: float32 [1408], replicated
- grad_fc1_weight: float32 [1408, 6144], P('dp', 'seq')
- grad_fc2_weight: float32 [6144, 1408], P('seq', 'dp')
Inputs may be any that keep to these rules, and one draw needn't show every extreme that they name: counts[i, 0] valid leading CLIP tokens of slot i (1 to 77), counts[i, 1] valid leading mT5 tokens (1 to 256); some slot has 77 CLIP tokens, some slot one, some slot 256 mT5 tokens. `bucket`: 0: the group is one image of 32 x 32 patches; 1: 4 images of half that side. `language`: 0 for English, 1 for Chinese captions. `timesteps`: diffusion timestep of a slot.
All inputs are finite; a program needn't handle non-finite values. No bound on the sum of `language` on one device may be relied on, other than what follows from the above.
Results may differ from a plain program's by a relative error of at most 0.029.
Values may be sent and summed in bfloat16 or wider, within the bound.
No kernel may reach another device: no remote copies, remote signals or barrier semaphores. Data moves between devices by JAX's collectives and lax.ppermute only.
A program may use at most 448 MiB of HBM per device.

v0:
```python
import math

import jax
import jax.numpy as jnp
from jax import lax
from jax.sharding import PartitionSpec as P

HEAD_DIM = 88
SIDE = 32
SMALL_PER = 4


PRECISE = lax.Precision.HIGHEST
EPSILON = 1e-06
NEGATIVE = -1000000000.0


def layer_norm(values):
    centre = values - jnp.mean(values, -1, keepdims=True)
    return centre * lax.rsqrt(jnp.mean(centre * centre, -1, keepdims=True) + EPSILON)


def gelu_tanh(values):
    return (
        0.5
        * values
        * (1.0 + jnp.tanh(0.7978845608028654 * (values + 0.044715 * values * values * values)))
    )


def timestep_features(steps, width):
    halfway = width // 2
    rates = jnp.exp(-math.log(10000.0) * jnp.arange(halfway, dtype=jnp.float32) / halfway)
    angles = steps.astype(jnp.float32)[:, None] * rates[None, :]
    return jnp.concatenate([jnp.cos(angles), jnp.sin(angles)], 1)


def token_layout(small_group, side):
    tokens_group = side * side
    indices = jnp.arange(tokens_group, dtype=jnp.int32)
    quarter = tokens_group // 4
    slot_of = jnp.where(small_group, indices // quarter, 0)
    within = jnp.where(small_group, indices % quarter, indices)
    across = jnp.where(small_group, side // 2, side)
    return (slot_of, within // across, within % across)


def rotary(values, rows, cols):
    quarter = values.shape[-1] // 4
    rates = jnp.exp(-math.log(10000.0) * jnp.arange(quarter, dtype=jnp.float32) / quarter)
    pieces = []
    for offset, source in ((0, rows), (2 * quarter, cols)):
        angles = source.astype(jnp.float32)[:, None] * rates[None, :]
        cosine = jnp.cos(angles)
        sine_part = jnp.sin(angles)
        leading = values[..., offset : offset + quarter]
        trailing = values[..., offset + quarter : offset + 2 * quarter]
        pieces.append(leading * cosine - trailing * sine_part)
        pieces.append(trailing * cosine + leading * sine_part)
    return jnp.concatenate(pieces, -1)


def contract_rows(left, right):
    return lax.dot_general(
        left, right, (((0,), (0,)), ((), ())), preferred_element_type=jnp.float32
    )


def contract_cols(left, right):
    return lax.dot_general(
        left, right, (((1,), (1,)), ((), ())), preferred_element_type=jnp.float32
    )


def gather_rows(local_rows):
    return lax.all_gather(local_rows, "seq", axis=0, tiled=True)


def gather_grads(local_rows):
    return lax.all_gather(local_rows, "seq", axis=0, tiled=True)


def sum_rows(left, weight, rows_local):

    def partial_rows(offset, number):
        return jnp.dot(
            lax.dynamic_slice_in_dim(left, offset, number, 0),
            weight,
            preferred_element_type=jnp.float32,
        )

    return lax.psum_scatter(
        partial_rows(jnp.int32(0), rows_local * lax.axis_size("seq")),
        "seq",
        scatter_dimension=0,
        tiled=True,
    )


def sum_grads(left, weight, rows_local):

    def partial_rows(offset, number):
        return contract_cols(lax.dynamic_slice_in_dim(left, offset, number, 0), weight)

    return lax.psum_scatter(
        partial_rows(jnp.int32(0), rows_local * lax.axis_size("seq")).astype(jnp.bfloat16),
        "seq",
        scatter_dimension=0,
        tiled=True,
    ).astype(jnp.float32)


def block_count(length):
    number = max(1, length // 512)
    return (number, length // number)


def attend_forward(queries, key_matrix_rows, value_matrix_rows, query_segs, key_segs):
    batches, length, head_size = queries.shape
    number, rows_block = block_count(length)
    scaling = 1.0 / math.sqrt(head_size)
    query_blocks = queries.reshape(batches, number, rows_block, head_size).swapaxes(0, 1)
    seg_blocks = query_segs.reshape(number, rows_block)

    def one_block(inputs):
        query_portion, seg_part = inputs
        scores = (
            jnp.einsum(
                "mwu,mou->mwo", query_portion, key_matrix_rows, preferred_element_type=jnp.float32
            )
            * scaling
        )
        scores = jnp.where((seg_part[:, None] == key_segs[None, :])[None], scores, NEGATIVE)
        maximum = jnp.max(scores, -1, keepdims=True)
        weights = jnp.exp(scores - maximum)
        totals = jnp.sum(weights, -1, keepdims=True)
        attention_probs = (weights / totals).astype(jnp.bfloat16)
        outputs = jnp.einsum(
            "pty,pyr->ptr", attention_probs, value_matrix_rows, preferred_element_type=jnp.float32
        )
        return (outputs, (maximum + jnp.log(totals))[..., 0])

    outputs, log_totals = lax.map(one_block, (query_blocks, seg_blocks))
    return (
        outputs.swapaxes(0, 1).reshape(batches, length, head_size),
        log_totals.swapaxes(0, 1).reshape(batches, length),
    )


def attend_backward(
    queries, key_matrix_rows, value_matrix_rows, query_segs, key_segs, log_totals, grad_out
):
    batches, length, head_size = queries.shape
    number, rows_block = block_count(length)
    scaling = 1.0 / math.sqrt(head_size)

    def blocks_of(values):
        return values.reshape((batches, number, rows_block) + values.shape[2:]).swapaxes(0, 1)

    seg_blocks = query_segs.reshape(number, rows_block)

    def one_block(carry, inputs):
        key_grad, value_grad = carry
        query_portion, seg_part, total_part, gradient_portion = inputs
        scores = (
            jnp.einsum(
                "mwu,mou->mwo", query_portion, key_matrix_rows, preferred_element_type=jnp.float32
            )
            * scaling
        )
        scores = jnp.where((seg_part[:, None] == key_segs[None, :])[None], scores, NEGATIVE)
        attention_probs = jnp.exp(scores - total_part[..., None])
        grad_probs = jnp.einsum(
            "mwu,mou->mwo", gradient_portion, value_matrix_rows, preferred_element_type=jnp.float32
        )
        row_dot = jnp.sum(attention_probs * grad_probs, -1, keepdims=True)
        score_gradient = (attention_probs * (grad_probs - row_dot)).astype(jnp.bfloat16)
        query_grad = (
            jnp.einsum(
                "pty,pyr->ptr", score_gradient, key_matrix_rows, preferred_element_type=jnp.float32
            )
            * scaling
        )
        key_grad = (
            key_grad
            + jnp.einsum(
                "zpn,zpa->zna", score_gradient, query_portion, preferred_element_type=jnp.float32
            )
            * scaling
        )
        value_grad = value_grad + jnp.einsum(
            "zpn,zpa->zna",
            attention_probs.astype(jnp.bfloat16),
            gradient_portion,
            preferred_element_type=jnp.float32,
        )
        return ((key_grad, value_grad), query_grad)

    zero_grad = jnp.zeros(key_matrix_rows.shape, jnp.float32)
    (key_grad, value_grad), query_grads = lax.scan(
        one_block,
        (zero_grad, zero_grad),
        (blocks_of(queries), seg_blocks, blocks_of(log_totals), blocks_of(grad_out)),
    )
    return (query_grads.swapaxes(0, 1).reshape(batches, length, head_size), key_grad, value_grad)


def on_device(
    latent,
    skip_input,
    clip_text,
    t5_text,
    bucket,
    counts,
    language,
    timesteps,
    cotangent,
    skip_weight,
    skip_gain,
    time_weight,
    shift_weight,
    norm1_gain,
    qkv_weight,
    q_gain,
    k_gain,
    out_weight,
    norm3_gain,
    cross_query,
    cq_gain,
    t5_weight,
    lang_embed,
    cross_kv,
    ck_gain,
    cross_out,
    norm2_gain,
    fc1_weight,
    fc2_weight,
):
    position = lax.axis_index("seq")
    rows_local = latent.shape[0]
    model_width = latent.shape[1]
    local_width = out_weight.shape[0]
    local_heads = local_width // HEAD_DIM
    text_local = clip_text.shape[2]
    text_width = lang_embed.shape[1]
    clip_length = clip_text.shape[1]
    context_length = clip_length + t5_text.shape[1]
    context_rows = SMALL_PER * context_length
    small_group = bucket[0] == 1
    slot_of, row_pos, col_pos = token_layout(small_group, SIDE)
    tokens_group = SIDE * SIDE
    slot_mine = lax.dynamic_slice_in_dim(slot_of, position * rows_local, rows_local, 0)
    slot_pick = (slot_mine[:, None] == jnp.arange(SMALL_PER, dtype=jnp.int32)[None, :]).astype(
        jnp.bfloat16
    )

    def split_heads(values):
        return values.reshape(values.shape[0], local_heads, HEAD_DIM).transpose(1, 0, 2)

    def merge_heads(values):
        return values.transpose(1, 0, 2).reshape(values.shape[1], local_width)

    def plain_norm(values, gain):
        return layer_norm(values) * gain

    def head_norm(values, gain):
        return layer_norm(split_heads(values)) * gain

    features = timestep_features(timesteps, time_weight.shape[0]).astype(jnp.bfloat16)
    time_pre = jnp.dot(features, time_weight, preferred_element_type=jnp.float32)
    gate_in, silu_pull = jax.vjp(jax.nn.silu, time_pre)
    gate_low = gate_in.astype(jnp.bfloat16)
    shift_cols = jnp.dot(gate_low, shift_weight, preferred_element_type=jnp.float32).astype(
        jnp.bfloat16
    )
    project_terms = jnp.einsum(
        "slf,fc->slc", t5_text, t5_weight, preferred_element_type=jnp.float32
    )
    projected = lax.psum_scatter(
        project_terms.astype(jnp.bfloat16), "seq", scatter_dimension=2, tiled=True
    ).astype(jnp.float32)
    lang_mine = lax.dynamic_slice_in_dim(lang_embed, position * text_local, text_local, 1).astype(
        jnp.float32
    )
    chosen = jnp.where(language[:, None] == 1, lang_mine[1][None, :], lang_mine[0][None, :])
    context_mine = jnp.concatenate(
        [clip_text, (projected + chosen[:, None, :]).astype(jnp.bfloat16)], 1
    )
    context, shifts = (
        lax.all_gather(context_mine, "seq", axis=2, tiled=True),
        lax.all_gather(shift_cols, "seq", axis=1, tiled=True),
    )
    joined = jnp.concatenate([latent, skip_input], 1)
    joined_cols = lax.all_to_all(joined, "seq", split_axis=1, concat_axis=0, tiled=True)
    hidden = sum_rows(joined_cols, skip_weight, rows_local)
    shift_rows = jnp.dot(slot_pick, shifts, preferred_element_type=jnp.float32)

    def first_norms(hidden_rows, gain_skip, gain_one, shift_part):
        residual = layer_norm(hidden_rows) * gain_skip
        return (residual, layer_norm(residual) * gain_one + shift_part)

    (residual_one, normed), first_pull = jax.vjp(
        first_norms, hidden, skip_gain, norm1_gain, shift_rows
    )
    normed_all = gather_rows(normed.astype(jnp.bfloat16))
    qkv_rows = jnp.einsum("td,dce->tce", normed_all, qkv_weight, preferred_element_type=jnp.float32)

    def query_key(query_pre, key_pre, gain_query, gain_key):
        return (
            rotary(layer_norm(split_heads(query_pre)) * gain_query, row_pos, col_pos),
            rotary(layer_norm(split_heads(key_pre)) * gain_key, row_pos, col_pos),
        )

    (queries, key_matrix_rows), query_key_pull = jax.vjp(
        query_key, qkv_rows[:, 0], qkv_rows[:, 1], q_gain, k_gain
    )
    query_low = queries.astype(jnp.bfloat16)
    key_low = key_matrix_rows.astype(jnp.bfloat16)
    value_low = split_heads(qkv_rows[:, 2]).astype(jnp.bfloat16)
    self_heads, self_totals = attend_forward(query_low, key_low, value_low, slot_of, slot_of)
    self_merged = merge_heads(self_heads.astype(jnp.bfloat16))
    residual_two = residual_one + sum_rows(self_merged, out_weight, rows_local)
    normed_cross, cross_norm_pull = jax.vjp(plain_norm, residual_two, norm3_gain)
    cross_all = gather_rows(normed_cross.astype(jnp.bfloat16))
    cross_pre = jnp.dot(cross_all, cross_query, preferred_element_type=jnp.float32)
    cross_queries, cross_query_pull = jax.vjp(head_norm, cross_pre, cq_gain)
    context_kv = jnp.einsum("slc,cke->slke", context, cross_kv, preferred_element_type=jnp.float32)
    flat_kv = context_kv.reshape(context_rows, 2, local_width)
    cross_keys, cross_key_pull = jax.vjp(head_norm, flat_kv[:, 0], ck_gain)
    positions = jnp.arange(context_length, dtype=jnp.int32)[None, :]
    visible = jnp.where(
        positions < clip_length, positions < counts[:, :1], positions - clip_length < counts[:, 1:]
    )
    key_segs = jnp.where(visible, jnp.arange(SMALL_PER, dtype=jnp.int32)[:, None], -1).reshape(-1)
    cross_query_low = cross_queries.astype(jnp.bfloat16)
    cross_key_low = cross_keys.astype(jnp.bfloat16)
    cross_value_low = split_heads(flat_kv[:, 1]).astype(jnp.bfloat16)
    cross_heads, cross_totals = attend_forward(
        cross_query_low, cross_key_low, cross_value_low, slot_of, key_segs
    )
    cross_merged = merge_heads(cross_heads.astype(jnp.bfloat16))
    residual_three = residual_two + sum_rows(cross_merged, cross_out, rows_local)
    normed_mlp, mlp_norm_pull = jax.vjp(plain_norm, residual_three, norm2_gain)
    mlp_all = gather_rows(normed_mlp.astype(jnp.bfloat16))
    expanded = jnp.dot(mlp_all, fc1_weight, preferred_element_type=jnp.float32)
    activated, gelu_pull = jax.vjp(gelu_tanh, expanded)
    active_low = activated.astype(jnp.bfloat16)
    block_output = (residual_three + sum_rows(active_low, fc2_weight, rows_local)).astype(
        jnp.bfloat16
    )
    grad_all = gather_grads(cotangent)
    grad_fc2 = contract_rows(active_low, grad_all)
    (grad_expanded,) = gelu_pull(contract_cols(grad_all, fc2_weight))
    expanded_low = grad_expanded.astype(jnp.bfloat16)
    grad_fc1 = contract_rows(mlp_all, expanded_low)
    gradient_portion, second_norm_gradient = mlp_norm_pull(
        sum_grads(expanded_low, fc1_weight, rows_local)
    )
    grad_three = cotangent.astype(jnp.float32) + gradient_portion
    cross_grad_all = gather_grads(grad_three.astype(jnp.bfloat16))
    grad_cross_out = contract_rows(cross_merged, cross_grad_all)
    cross_heads_grad = split_heads(contract_cols(cross_grad_all, cross_out).astype(jnp.bfloat16))
    grad_cq_heads, grad_ck_heads, grad_cv_heads = attend_backward(
        cross_query_low,
        cross_key_low,
        cross_value_low,
        slot_of,
        key_segs,
        cross_totals,
        cross_heads_grad,
    )
    grad_cross_pre, grad_cq_gain = cross_query_pull(grad_cq_heads)
    cross_pre_low = grad_cross_pre.astype(jnp.bfloat16)
    grad_cross_query = contract_rows(cross_all, cross_pre_low)
    gradient_portion, grad_norm3 = cross_norm_pull(
        sum_grads(cross_pre_low, cross_query, rows_local)
    )
    grad_two = grad_three + gradient_portion
    grad_ck_flat, grad_ck_gain = cross_key_pull(grad_ck_heads)
    grad_kv_low = (
        jnp.stack([grad_ck_flat, merge_heads(grad_cv_heads)], 1)
        .reshape(SMALL_PER, context_length, 2, local_width)
        .astype(jnp.bfloat16)
    )
    grad_cross_kv = jnp.einsum(
        "slc,slke->cke", context, grad_kv_low, preferred_element_type=jnp.float32
    )
    context_terms = jnp.einsum(
        "slke,cke->slc", grad_kv_low, cross_kv, preferred_element_type=jnp.float32
    )
    self_grad_all = gather_grads(grad_two.astype(jnp.bfloat16))
    grad_out_weight = contract_rows(self_merged, self_grad_all)
    self_heads_grad = split_heads(contract_cols(self_grad_all, out_weight).astype(jnp.bfloat16))
    grad_q_heads, grad_k_heads, grad_v_heads = attend_backward(
        query_low, key_low, value_low, slot_of, slot_of, self_totals, self_heads_grad
    )
    grad_q_pre, grad_k_pre, grad_q_gain, grad_k_gain = query_key_pull((grad_q_heads, grad_k_heads))
    grad_qkv_low = jnp.stack([grad_q_pre, grad_k_pre, merge_heads(grad_v_heads)], 1).astype(
        jnp.bfloat16
    )
    grad_qkv = jnp.einsum(
        "td,tce->dce", normed_all, grad_qkv_low, preferred_element_type=jnp.float32
    )
    grad_normed = sum_grads(
        grad_qkv_low.reshape(tokens_group, 3 * local_width),
        qkv_weight.reshape(model_width, 3 * local_width),
        rows_local,
    )
    grad_hidden, grad_skip_gain, grad_norm1, grad_shift_rows = first_pull((grad_two, grad_normed))
    shift_terms = jnp.dot(slot_pick.astype(jnp.float32).T, grad_shift_rows, precision=PRECISE)
    hidden_all = gather_grads(grad_hidden.astype(jnp.bfloat16))
    grad_skip_weight = contract_rows(joined_cols, hidden_all)
    joined_grad = lax.all_to_all(
        contract_cols(hidden_all, skip_weight).astype(jnp.bfloat16),
        "seq",
        split_axis=0,
        concat_axis=1,
        tiled=True,
    ).astype(jnp.float32)
    context_grad, shift_grad = (
        lax.psum_scatter(
            context_terms.astype(jnp.bfloat16), "seq", scatter_dimension=2, tiled=True
        ).astype(jnp.float32),
        lax.psum_scatter(
            shift_terms.astype(jnp.bfloat16), "seq", scatter_dimension=1, tiled=True
        ).astype(jnp.float32),
    )
    grad_clip = context_grad[:, :clip_length]
    project_grad = context_grad[:, clip_length:]
    language_pick = (language[:, None] == jnp.arange(2, dtype=jnp.int32)[None, :]).astype(
        jnp.float32
    )
    lang_local = jnp.dot(language_pick.T, jnp.sum(project_grad, 1), precision=PRECISE)
    grad_lang = lax.dynamic_update_slice_in_dim(
        jnp.zeros((2, text_width), jnp.float32), lang_local, position * text_local, 1
    )
    project_all = lax.all_gather(project_grad.astype(jnp.bfloat16), "seq", axis=2, tiled=True)
    grad_t5 = jnp.einsum("slc,fc->slf", project_all, t5_weight, preferred_element_type=jnp.float32)
    grad_t5_weight = jnp.einsum(
        "slf,slc->fc", t5_text, project_all, preferred_element_type=jnp.float32
    )
    shift_low = shift_grad.astype(jnp.bfloat16)
    grad_shift_weight = contract_rows(gate_low, shift_low)
    (grad_time_pre,) = silu_pull(contract_cols(shift_low, shift_weight))
    grad_time_weight = jnp.dot(features.astype(jnp.float32).T, grad_time_pre, precision=PRECISE)
    gain_totals = lax.psum(
        (
            grad_skip_gain,
            grad_norm1,
            grad_q_gain,
            grad_k_gain,
            grad_norm3,
            grad_cq_gain,
            grad_ck_gain,
            second_norm_gradient,
            grad_lang,
            grad_time_weight,
        ),
        ("dp", "seq"),
    )
    big_totals = (
        lax.psum_scatter(
            grad_skip_weight.astype(jnp.bfloat16), "dp", scatter_dimension=1, tiled=True
        ).astype(jnp.float32),
        lax.psum_scatter(
            grad_shift_weight.astype(jnp.bfloat16), "dp", scatter_dimension=0, tiled=True
        ).astype(jnp.float32),
        lax.psum_scatter(
            grad_qkv.astype(jnp.bfloat16), "dp", scatter_dimension=0, tiled=True
        ).astype(jnp.float32),
        lax.psum_scatter(
            grad_out_weight.astype(jnp.bfloat16), "dp", scatter_dimension=1, tiled=True
        ).astype(jnp.float32),
        lax.psum_scatter(
            grad_cross_query.astype(jnp.bfloat16), "dp", scatter_dimension=0, tiled=True
        ).astype(jnp.float32),
        lax.psum_scatter(
            grad_t5_weight.astype(jnp.bfloat16), "dp", scatter_dimension=1, tiled=True
        ).astype(jnp.float32),
        lax.psum_scatter(
            grad_cross_kv.astype(jnp.bfloat16), "dp", scatter_dimension=0, tiled=True
        ).astype(jnp.float32),
        lax.psum_scatter(
            grad_cross_out.astype(jnp.bfloat16), "dp", scatter_dimension=1, tiled=True
        ).astype(jnp.float32),
        lax.psum_scatter(
            grad_fc1.astype(jnp.bfloat16), "dp", scatter_dimension=0, tiled=True
        ).astype(jnp.float32),
        lax.psum_scatter(
            grad_fc2.astype(jnp.bfloat16), "dp", scatter_dimension=1, tiled=True
        ).astype(jnp.float32),
    )
    return (
        block_output,
        joined_grad[:, :model_width],
        joined_grad[:, model_width:],
        grad_clip,
        grad_t5,
        big_totals[0],
        gain_totals[0],
        gain_totals[9],
        big_totals[1],
        gain_totals[1],
        big_totals[2],
        gain_totals[2],
        gain_totals[3],
        big_totals[3],
        gain_totals[4],
        big_totals[4],
        gain_totals[5],
        big_totals[5],
        gain_totals[8],
        big_totals[6],
        gain_totals[6],
        big_totals[7],
        gain_totals[7],
        big_totals[8],
        big_totals[9],
    )


def solution(mesh):
    return jax.shard_map(
        on_device,
        mesh=mesh,
        in_specs=(
            P(("dp", "seq"), None),
            P(("dp", "seq"), None),
            P("dp", None, "seq"),
            P("dp", None, "seq"),
            P("dp"),
            P("dp", None),
            P("dp"),
            P("dp"),
            P(("dp", "seq"), None),
            P("seq", None),
            P(),
            P(),
            P(None, "seq"),
            P(),
            P(None, None, "seq"),
            P(),
            P(),
            P("seq", None),
            P(),
            P(None, "seq"),
            P(),
            P("seq", None),
            P(),
            P(None, None, "seq"),
            P(),
            P("seq", None),
            P(),
            P(None, "seq"),
            P("seq", None),
        ),
        out_specs=(
            P(("dp", "seq"), None),
            P(("dp", "seq"), None),
            P(("dp", "seq"), None),
            P("dp", None, "seq"),
            P("dp", None, "seq"),
            P("seq", "dp"),
            P(),
            P(),
            P("dp", "seq"),
            P(),
            P("dp", None, "seq"),
            P(),
            P(),
            P("seq", "dp"),
            P(),
            P("dp", "seq"),
            P(),
            P("seq", "dp"),
            P(),
            P("dp", None, "seq"),
            P(),
            P("seq", "dp"),
            P(),
            P("dp", "seq"),
            P("seq", "dp"),
        ),
        check_vma=False,
    )
```

profile of v0, /device:TPU:15, one launch (start us, length us, event | category | flops | bytes accessed | tf_op | source)
XLA Modules:
  0.0 2464.7 jit_solution(15213698064557847228)
XLA Ops:
  14.5 35.3 %all_to_all.32 = bf16[512,2,1408]{0,2,1:T(8,128)(2,1)} all-to-all(bf16[512,2,1408]{0,2,1:T(8,128)(2,1)S(1)} %bitcast.390), channel_id=1, replica_groups=mesh['dp'=16,'seq'=2] {'seq'}, dimensions={1} | all-to-all | bytes 5767168 | tf_op jit(solution)/shard_map/all_to_all | solution.py:294
  72.6 63.6 %reduce-scatter.25.cloned.1.call-done = f32[512,1408]{1,0:T(8,128)} async-done(((f32[1024,1408]{1,0:T(8,128)}), f32[512,1408]{1,0:T(8,128)}) %reduce-scatter.25.cloned.1.call-update) | async-done | bytes 2883600 | tf_op jit(solution)/shard_map/reduce_scatter | solution.py:92
  156.9 30.9 %all-gather.11.cloned.1.call-done = bf16[1024,1408]{1,0:T(8,128)(2,1)} async-done(((bf16[512,1408]{1,0:T(8,128)(2,1)}), bf16[1024,1408]{1,0:T(8,128)(2,1)}) %all-gather.11.cloned.1.call-update) | async-done | bytes 2883600 | tf_op jit(solution)/shard_map/all_gather | solution.py:76
  228.5 34.9 %while.56 = (s32[]{:T(128)}, bf16[2,8,512,88]{2,3,1,0:T(8,128)(2,1)}, f32[2,8,512]{2,1,0:T(8,128)S(1)}, s32[2,512]{1,0:T(2,128)S(1)}, bf16[2,8,512,88]{2,3,1,0:T...) while((s32[]{:T(128)}, ...), condition=%wide.region_12.13_spmd.clone, body=%wide.region_9.12_spmd.clone.sunk | while | flops 1527256064 | bytes 74922192 | solution.py:143
  274.9 67.4 %reduce-scatter.27.cloned.1.call-done = f32[512,1408]{1,0:T(8,128)} async-done(((f32[1024,1408]{1,0:T(8,128)}), f32[512,1408]{1,0:T(8,128)}) %reduce-scatter.27.cloned.1.call-update) | async-done | bytes 2883600 | tf_op jit(solution)/shard_map/reduce_scatter | solution.py:92
  348.8 36.0 %all-gather.15.cloned.1.call-done = bf16[4,333,1024]{2,1,0:T(8,128)(2,1)} async-done(((bf16[4,333,512]{2,1,0:T(8,128)(2,1)}), bf16[4,333,1024]{2,1,0:T(8,128)(2,1)}) %all-gather.15.cloned.1.call-update) | async-done | bytes 2727952 | tf_op jit(solution)/shard_map/all_gather | solution.py:290
  450.3 67.6 %while.57 = (s32[]{:T(128)}, bf16[2,8,512,88]{2,3,1,0:T(8,128)(2,1)}, f32[2,8,512]{2,1,0:T(8,128)S(1)}, s32[2,512]{1,0:T(2,128)S(1)}, bf16[2,8,512,88]{2,3,1,0:T...) while((s32[]{:T(128)}, ...), condition=%wide.region_24.25_spmd.clone, body=%wide.region_21.24_spmd.clone.sunk | while | flops 1964797184 | bytes 92158664 | solution.py:143
  451.1 13.0 fusion.289
  484.8 13.0 fusion.289
  526.0 70.7 %reduce-scatter.31.cloned.1.call-done = f32[512,1408]{1,0:T(8,128)} async-done(((f32[1024,1408]{1,0:T(8,128)}), f32[512,1408]{1,0:T(8,128)}) %reduce-scatter.31.cloned.1.call-update) | async-done | bytes 2883600 | tf_op jit(solution)/shard_map/reduce_scatter | solution.py:92
  603.0 37.3 %all-gather.19.cloned.1.call-done = bf16[1024,1408]{1,0:T(8,128)(2,1)} async-done(((bf16[512,1408]{1,0:T(8,128)(2,1)}), bf16[1024,1408]{1,0:T(8,128)(2,1)}) %all-gather.19.cloned.1.call-update) | async-done | bytes 2883600 | tf_op jit(solution)/shard_map/all_gather | solution.py:80
  640.3 16.3 fusion.188
  656.6 27.8 %all-gather.17.cloned.1.call-done = bf16[1024,1408]{1,0:T(8,128)(2,1)} async-done(((bf16[512,1408]{1,0:T(8,128)(2,1)}), bf16[1024,1408]{1,0:T(8,128)(2,1)}) %all-gather.17.cloned.1.call-update) | async-done | bytes 2883600 | tf_op jit(solution)/shard_map/all_gather | solution.py:76
  684.5 25.3 %fusion.73 = (bf16[1024,3072]{1,0:T(8,128)(2,1)S(1)}, f32[1024,3072]{1,0:T(8,128)}) fusion(f32[1024,3072]{1,0:T(8,128)} %fusion.188, bf16[1024,1408]{1,0:T(8,128)(2,1)} %all-gather.17.cloned.1.call-done, bf16[1408,3072]{1,0:T(8,128)(2,1)} %param.64), kind=kOutput, calls=%fused_computation.111 | convolution fusion | flops 8933867520 | bytes 42991616 | tf_op jit(solution)/shard_map/dot_general | solution.py:345
  712.4 13.7 convolution_convert_fusion.4
  726.2 17.6 fusion.169
  743.9 22.9 reduce-scatter.35.cloned.1.call-done
  770.7 70.0 %reduce-scatter.33.cloned.1.call-done = f32[512,1408]{1,0:T(8,128)} async-done(((f32[1024,1408]{1,0:T(8,128)}), f32[512,1408]{1,0:T(8,128)}) %reduce-scatter.33.cloned.1.call-update) | async-done | bytes 2883600 | tf_op jit(solution)/shard_map/reduce_scatter | solution.py:92
  849.2 42.1 %all-gather.21.cloned.1.call-done = bf16[1024,1408]{1,0:T(8,128)(2,1)} async-done(((bf16[512,1408]{1,0:T(8,128)(2,1)}), bf16[1024,1408]{1,0:T(8,128)(2,1)}) %all-gather.21.cloned.1.call-update) | async-done | bytes 2883600 | tf_op jit(solution)/shard_map/all_gather | solution.py:80
  906.5 163.2 %while.58 = (s32[]{:T(128)}, f32[8,1332,88]{1,2,0:T(8,128)}, f32[8,1332,88]{1,2,0:T(8,128)}, f32[2,8,512,88]{2,3,1,0:T(8,128)}, s32[2,512]{1,0:T(2,128)S(1)}, /*...) while((s32[]{:T(128)}, f32[8,1332,88]{1,2,0:T(8,128)}, ...), condition=%wide.region_34.35_spmd.clone, body=%wide.region_32.34_spmd.clone.sunk | while | flops 4856002560 | bytes 203936976 | solution.py:200
  908.3 12.2 fusion.301
  920.5 19.0 multiply_reduce_fusion.22
  939.5 19.1 multiply_convert_fusion.14
  988.5 12.2 fusion.301
  1000.7 19.0 multiply_reduce_fusion.22
  1019.7 19.1 multiply_convert_fusion.14
  1038.8 12.8 select_add_fusion.9
  1088.6 33.3 %reduce-scatter.37.cloned.1.call-done = bf16[512,1408]{1,0:T(8,128)(2,1)} async-done(((bf16[1024,1408]{1,0:T(8,128)(2,1)}), bf16[512,1408]{1,0:T(8,128)(2,1)}) %reduce-scatter.37.cloned.1.call-update) | async-done | bytes 1441808 | tf_op jit(solution)/shard_map/reduce_scatter | solution.py:105
  1187.7 118.2 %while.59 = (s32[]{:T(128)}, f32[8,1024,88]{1,2,0:T(8,128)}, f32[8,1024,88]{1,2,0:T(8,128)}, f32[2,8,512,88]{2,3,1,0:T(8,128)}, s32[2,512]{1,0:T(2,128)S(1)}, /*...) while((s32[]{:T(128)}, f32[8,1024,88]{1,2,0:T(8,128)}, ...), condition=%wide.region_42.43_spmd.clone, body=%wide.region_40.42_spmd.clone.sunk | while | flops 3733230592 | bytes 198015248 | solution.py:200
  1198.5 13.0 multiply_reduce_fusion.23
  1211.5 15.0 multiply_convert_fusion.15
  1256.5 13.0 multiply_reduce_fusion.23
  1269.5 14.9 multiply_convert_fusion.15
  1335.3 37.8 %reduce-scatter.39.cloned.1.call-done = bf16[512,1408]{1,0:T(8,128)(2,1)} async-done(((bf16[1024,1408]{1,0:T(8,128)(2,1)}), bf16[512,1408]{1,0:T(8,128)(2,1)}) %reduce-scatter.39.cloned.1.call-update) | async-done | bytes 1441808 | tf_op jit(solution)/shard_map/reduce_scatter | solution.py:105
  1390.7 14.4 convolution_convert_fusion.1
  1405.6 15.6 convolution_convert_fusion
  1482.8 97.9 %reduce-scatter.55.cloned.1.call-done = bf16[88,3072]{1,0:T(8,128)(2,1)} async-done(((bf16[1408,3072]{1,0:T(8,128)(2,1)}), bf16[88,3072]{1,0:T(8,128)(2,1)}) %reduce-scatter.55.cloned.1.call-update) | async-done | bytes 540688 | tf_op jit(solution)/shard_map/reduce_scatter | solution.py:486
  1582.8 109.5 %reduce-scatter.57.cloned.1.call-done = bf16[3072,88]{0,1:T(8,128)(2,1)} async-done(((bf16[3072,1408]{0,1:T(8,128)(2,1)}), bf16[3072,88]{0,1:T(8,128)(2,1)}) %reduce-scatter.57.cloned.1.call-update) | async-done | bytes 540688 | tf_op jit(solution)/shard_map/reduce_scatter | solution.py:489
  1694.4 61.1 %reduce-scatter.47.cloned.1.call-done = bf16[88,704]{1,0:T(8,128)(2,1)} async-done(((bf16[1408,704]{1,0:T(8,128)(2,1)}), bf16[88,704]{1,0:T(8,128)(2,1)}) %reduce-scatter.47.cloned.1.call-update) | async-done | bytes 123920 | tf_op jit(solution)/shard_map/reduce_scatter | solution.py:474
  1757.2 63.2 %reduce-scatter.53.cloned.1.call-done = bf16[704,88]{0,1:T(8,128)(2,1)} async-done(((bf16[704,1408]{0,1:T(8,128)(2,1)}), bf16[704,88]{0,1:T(8,128)(2,1)}) %reduce-scatter.53.cloned.1.call-update) | async-done | bytes 123920 | tf_op jit(solution)/shard_map/reduce_scatter | solution.py:483
  1822.1 69.0 %reduce-scatter.51.cloned.1.call-done = bf16[64,2,704]{2,0,1:T(8,128)(2,1)} async-done(((bf16[1024,2,704]{2,0,1:T(8,128)(2,1)}), bf16[64,2,704]{2,0,1:T(8,128)(2,1)}) %reduce-scatter.51.cloned.1.call-update) | async-done | bytes 180240 | tf_op jit(solution)/shard_map/reduce_scatter | solution.py:480
  1916.6 39.0 %reduce-scatter.49.cloned.1.call-done = bf16[1024,64]{0,1:T(8,128)(2,1)} async-done(((bf16[1024,1024]{0,1:T(8,128)(2,1)}), bf16[1024,64]{0,1:T(8,128)(2,1)}) %reduce-scatter.49.cloned.1.call-update) | async-done | bytes 131088 | tf_op jit(solution)/shard_map/reduce_scatter | solution.py:477
  1957.2 62.6 %reduce-scatter.45.cloned.1.call-done = bf16[704,88]{0,1:T(8,128)(2,1)} async-done(((bf16[704,1408]{0,1:T(8,128)(2,1)}), bf16[704,88]{0,1:T(8,128)(2,1)}) %reduce-scatter.45.cloned.1.call-update) | async-done | bytes 123920 | tf_op jit(solution)/shard_map/reduce_scatter | solution.py:471
  2021.4 144.8 %all-reduce.16.cloned.1.call-done = bf16[1408,3,704]{2,0,1:T(8,128)(2,1)} async-done(((bf16[1408,3,704]{2,0,1:T(8,128)(2,1)}), bf16[1408,3,704]{2,0,1:T(8,128)(2,1)}) %all-reduce.16.cloned.1.call-update) | async-done | bytes 5947408
  2168.1 40.1 %all-reduce.10 = (f32[1408]{0:T(1024)}, f32[1408]{0:T(1024)}, f32[88]{0:T(128)}, f32[88]{0:T(128)}, f32[1408]{0:T(1024)}, /*index=5*/f32[88]{0:T(128)}, f32[2,1024]{1,0:T(2,128)}, f32[88]{0:T(128)}, f32[1408]{0:T(1024)}) all-reduce(f32[1408]{0:T(1024)S(1)} %get-tuple-element.616, ...), channel_id=1, replica_groups=mesh['dp'=16,'seq'=2] {'dp','seq'}, use_global_device_ids=true, to_apply=%region_57.58 | all-reduce | flops 8032 | bytes 64256 | tf_op jit(solution)/shard_map/psum | solution.py:446
  2212.2 18.8 reduce-scatter.43.cloned.1.call-done
  2238.1 80.5 %reduce-scatter.61.cloned.1.call-done = bf16[1408,88]{0,1:T(8,128)(2,1)} async-done(((bf16[1408,1408]{0,1:T(8,128)(2,1)}), bf16[1408,88]{0,1:T(8,128)(2,1)}) %reduce-scatter.61.cloned.1.call-update) | async-done | bytes 247824
  2320.4 134.7 %all-reduce.14.cloned.1.call-done = f32[256,1408]{1,0:T(8,128)} async-done(((f32[256,1408]{1,0:T(8,128)}), f32[256,1408]{1,0:T(8,128)}) %all-reduce.14.cloned.1.call-update) | async-done | bytes 1441808 | tf_op jit(solution)/shard_map/psum | solution.py:446
  (627 shorter events, 650.6 us)
Async XLA Ops:
  7.2 377.6 %copy-start = (bf16[1024,2,704]{0,2,1:T(8,128)(2,1)S(1)}, bf16[1024,2,704]{0,2,1:T(8,128)(2,1)}, u32[]{:S(2)}) copy-start(bf16[1024,2,704]{0,2,1:T(8,128)(2,1)} %param.60) | copy-start | bytes 8650756
  7.2 129.0 %reduce-scatter.25.cloned.1.call-start = ((), (), s32[]{:S(2)}) async-start(), calls=%async_computation.21 | async-start | bytes 8650752 | tf_op jit(solution)/shard_map/reduce_scatter | solution.py:92
  63.6 124.1 %all-gather.11.cloned.1.call-start = ((), (), s32[]{:S(2)}) async-start(), calls=%async_computation.22 | async-start | bytes 4325376 | tf_op jit(solution)/shard_map/all_gather | solution.py:76
  72.6 70.2 %copy-start.103 = (s32[512]{0:T(512)}, s32[512]{0:T(512)S(1)}, u32[]{:S(2)}) copy-start(s32[512]{0:T(512)S(1)} %dynamic_slice.45) | copy-start | bytes 6148
  72.6 68.1 %copy-start.81 = (f32[1408]{0:T(1024)S(1)}, f32[1408]{0:T(1024)}, u32[]{:S(2)}) copy-start(f32[1408]{0:T(1024)} %param.47) | copy-start | bytes 16900
  145.6 126.4 %reduce-scatter.29.cloned.1.call-start = ((), (), s32[]{:S(2)}) async-start(), calls=%async_computation.25 | async-start | bytes 3145728 | tf_op jit(solution)/shard_map/reduce_scatter | solution.py:279
  151.5 190.7 %reduce-scatter.27.cloned.1.call-start = ((), (), s32[]{:S(2)}) async-start(), calls=%async_computation.23 | async-start | bytes 8650752 | tf_op jit(solution)/shard_map/reduce_scatter | solution.py:92
  156.8 69.4 %copy-start.38 = (f32[1024,22]{0,1:T(8,128)}, f32[1024,22]{0,1:T(8,128)S(1)}, u32[]{:S(2)}) copy-start(f32[1024,22]{0,1:T(8,128)S(1)} %get-tuple-element.777) | copy-start | bytes 270340
  156.8 69.4 %copy-start.40 = (f32[1024,22]{0,1:T(8,128)}, f32[1024,22]{0,1:T(8,128)S(1)}, u32[]{:S(2)}) copy-start(f32[1024,22]{0,1:T(8,128)S(1)} %get-tuple-element.778) | copy-start | bytes 270340
  156.8 69.4 %copy-start.42 = (f32[1024,22]{0,1:T(8,128)}, f32[1024,22]{0,1:T(8,128)S(1)}, u32[]{:S(2)}) copy-start(f32[1024,22]{0,1:T(8,128)S(1)} %get-tuple-element.787) | copy-start | bytes 270340
  156.8 69.4 %copy-start.44 = (f32[1024,22]{0,1:T(8,128)}, f32[1024,22]{0,1:T(8,128)S(1)}, u32[]{:S(2)}) copy-start(f32[1024,22]{0,1:T(8,128)S(1)} %get-tuple-element.788) | copy-start | bytes 270340
  270.7 114.1 %all-gather.15.cloned.1.call-start = ((), (), s32[]{:S(2)}) async-start(), calls=%async_computation.26 | async-start | bytes 4128768 | tf_op jit(solution)/shard_map/all_gather | solution.py:290
  272.0 70.3 %copy-start.82 = (f32[1408]{0:T(1024)S(1)}, f32[1408]{0:T(1024)}, u32[]{:S(2)}) copy-start(f32[1408]{0:T(1024)} %param.47) | copy-start | bytes 16900
  272.0 70.3 %copy-start.89 = (f32[512]{0:T(512)S(1)}, f32[512]{0:T(512)}, u32[]{:S(2)}) copy-start(f32[512]{0:T(512)} %copy-done.88) | copy-start | bytes 6148
  272.0 70.3 %copy-start.95 = (f32[512]{0:T(512)S(1)}, f32[512]{0:T(512)}, u32[]{:S(2)}) copy-start(f32[512]{0:T(512)} %copy-done.94) | copy-start | bytes 6148
  274.8 154.1 %all-gather.13.cloned.1.call-start = ((), (), s32[]{:S(2)}) async-start(), calls=%async_computation.24 | async-start | bytes 4325376 | tf_op jit(solution)/shard_map/all_gather | solution.py:76
  348.8 248.0 %reduce-scatter.31.cloned.1.call-start = ((), (), s32[]{:S(2)}) async-start(), calls=%async_computation.27 | async-start | bytes 8650752 | tf_op jit(solution)/shard_map/reduce_scatter | solution.py:92
  525.2 115.1 %all-gather.19.cloned.1.call-start = ((), (), s32[]{:S(2)}) async-start(), calls=%async_computation.30 | async-start | bytes 4325376 | tf_op jit(solution)/shard_map/all_gather | solution.py:80
  526.0 158.5 %all-gather.17.cloned.1.call-start = ((), (), s32[]{:S(2)}) async-start(), calls=%async_computation.28 | async-start | bytes 4325376 | tf_op jit(solution)/shard_map/all_gather | solution.py:76
  603.0 163.8 %reduce-scatter.35.cloned.1.call-start = ((), (), s32[]{:S(2)}) async-start(), calls=%async_computation.31 | async-start | bytes 4325376 | tf_op jit(solution)/shard_map/reduce_scatter | solution.py:105
  726.2 114.5 %reduce-scatter.33.cloned.1.call-start = ((), (), s32[]{:S(2)}) async-start(), calls=%async_computation.29 | async-start | bytes 8650752 | tf_op jit(solution)/shard_map/reduce_scatter | solution.py:92
  743.8 147.4 %all-gather.21.cloned.1.call-start = ((), (), s32[]{:S(2)}) async-start(), calls=%async_computation.32 | async-start | bytes 4325376 | tf_op jit(solution)/shard_map/all_gather | solution.py:80
  849.1 272.9 %reduce-scatter.37.cloned.1.call-start = ((), (), s32[]{:S(2)}) async-start(), calls=%async_computation.33 | async-start | bytes 4325376 | tf_op jit(solution)/shard_map/reduce_scatter | solution.py:105
  1081.4 91.0 %all-gather.23.cloned.1.call-start = ((), (), s32[]{:S(2)}) async-start(), calls=%async_computation.34 | async-start | bytes 4325376 | tf_op jit(solution)/shard_map/all_gather | solution.py:80
  1130.2 202.3 %reduce-scatter.41.cloned.1.call-start = ((), (), s32[]{:S(2)}) async-start(), calls=%async_computation.37 | async-start | bytes 4128768 | tf_op jit(solution)/shard_map/reduce_scatter | solution.py:421
  1168.4 204.6 %reduce-scatter.39.cloned.1.call-start = ((), (), s32[]{:S(2)}) async-start(), calls=%async_computation.35 | async-start | bytes 4325376 | tf_op jit(solution)/shard_map/reduce_scatter | solution.py:105
  1332.4 111.0 %all-gather.27.cloned.1.call-start = ((), (), s32[]{:S(2)}) async-start(), calls=%async_computation.38 | async-start | bytes 3145728 | tf_op jit(solution)/shard_map/all_gather | solution.py:437
  1335.0 133.0 %reduce-scatter.59.cloned.1.call-start = ((), (), s32[]{:S(2)}) async-start(), calls=%async_computation.48 | async-start | bytes 540672
  1387.5 84.1 %all-gather.25.cloned.1.call-start = ((), (), s32[]{:S(2)}) async-start(), calls=%async_computation.36 | async-start | bytes 4325376 | tf_op jit(solution)/shard_map/all_gather | solution.py:80
  1390.7 190.0 %reduce-scatter.55.cloned.1.call-start = ((), (), s32[]{:S(2)}) async-start(), calls=%async_computation.46 | async-start | bytes 9191424 | tf_op jit(solution)/shard_map/reduce_scatter | solution.py:486
  1405.1 287.2 %reduce-scatter.57.cloned.1.call-start = ((), (), s32[]{:S(2)}) async-start(), calls=%async_computation.47 | async-start | bytes 9191424 | tf_op jit(solution)/shard_map/reduce_scatter | solution.py:489
  1421.2 334.4 %reduce-scatter.47.cloned.1.call-start = ((), (), s32[]{:S(2)}) async-start(), calls=%async_computation.42 | async-start | bytes 2297856 | tf_op jit(solution)/shard_map/reduce_scatter | solution.py:474
  1427.3 393.1 %reduce-scatter.53.cloned.1.call-start = ((), (), s32[]{:S(2)}) async-start(), calls=%async_computation.45 | async-start | bytes 2297856 | tf_op jit(solution)/shard_map/reduce_scatter | solution.py:483
  1433.5 457.5 %reduce-scatter.51.cloned.1.call-start = ((), (), s32[]{:S(2)}) async-start(), calls=%async_computation.44 | async-start | bytes 3342336 | tf_op jit(solution)/shard_map/reduce_scatter | solution.py:480
  1443.4 512.2 %reduce-scatter.49.cloned.1.call-start = ((), (), s32[]{:S(2)}) async-start(), calls=%async_computation.43 | async-start | bytes 2228224 | tf_op jit(solution)/shard_map/reduce_scatter | solution.py:477
  1449.4 570.4 %reduce-scatter.45.cloned.1.call-start = ((), (), s32[]{:S(2)}) async-start(), calls=%async_computation.41 | async-start | bytes 2297856 | tf_op jit(solution)/shard_map/reduce_scatter | solution.py:471
  1455.6 710.6 %all-reduce.16.cloned.1.call-start = ((), (), s32[]{:S(2)}) async-start(), calls=%async_computation.49 | async-start | bytes 12976128
  1467.7 763.2 %reduce-scatter.43.cloned.1.call-start = ((), (), s32[]{:S(2)}) async-start(), calls=%async_computation.40 | async-start | bytes 2297856 | tf_op jit(solution)/shard_map/reduce_scatter | solution.py:465
  1471.5 847.1 %reduce-scatter.61.cloned.1.call-start = ((), (), s32[]{:S(2)}) async-start(), calls=%async_computation.50 | async-start | bytes 4212736
  1903.9 328.7 %all-to-all-start.1 = ((bf16[2,512,1408]{2,1,0:T(8,128)(2,1)}), bf16[2,512,1408]{2,1,0:T(8,128)(2,1)}, u32[]{:S(2)}, u32[]{:S(2)}) async-start(bf16[2,512,1408]{2,1,0:T(8,128)(2,1)} %bitcast.398), calls=%async_computation.9 | async-start | bytes 5767168 | tf_op jit(solution)/shard_map/all_to_all | solution.py:413
  1909.5 545.6 %all-reduce.14.cloned.1.call-start = ((), (), s32[]{:S(2)}) async-start(), calls=%async_computation.39 | async-start | bytes 2883584 | tf_op jit(solution)/shard_map/psum | solution.py:446
  1909.8 258.4 %copy-start.99 = (f32[1408]{0:T(1024)S(1)}, f32[1408]{0:T(1024)}, u32[]{:S(2)}) copy-start(f32[1408]{0:T(1024)} %get-tuple-element.620) | copy-start | bytes 16900
  1909.8 258.4 %copy-start.100 = (f32[1408]{0:T(1024)S(1)}, f32[1408]{0:T(1024)}, u32[]{:S(2)}) copy-start(f32[1408]{0:T(1024)} %get-tuple-element.618) | copy-start | bytes 16900
  1909.8 258.4 %copy-start.125 = (f32[88]{0:T(128)S(1)}, f32[88]{0:T(128)}, u32[]{:S(2)}) copy-start(f32[88]{0:T(128)} %get-tuple-element.614) | copy-start | bytes 1060
  1909.8 258.4 %copy-start.126 = (f32[88]{0:T(128)S(1)}, f32[88]{0:T(128)}, u32[]{:S(2)}) copy-start(f32[88]{0:T(128)} %get-tuple-element.608) | copy-start | bytes 1060
  1909.8 298.5 %copy-start.62 = (bf16[704,4]{1,0:T(8,128)(2,1)S(1)}, bf16[704,4]{1,0:T(8,128)(2,1)}, u32[]{:S(2)}) copy-start(bf16[704,4]{1,0:T(8,128)(2,1)} %reduce-scatter.59.cloned.1.call-done) | copy-start | bytes 16900
  1916.6 293.7 %copy-start.114 = (bf16[4,128]{1,0:T(4,128)(2,1)S(1)}, bf16[4,128]{1,0:T(4,128)(2,1)}, u32[]{:S(2)}) copy-start(bf16[4,128]{1,0:T(4,128)(2,1)} %copy-done.113) | copy-start | bytes 3076
  1916.6 293.7 %copy-start.116 = (bf16[4,128]{1,0:T(4,128)(2,1)S(1)}, bf16[4,128]{1,0:T(4,128)(2,1)}, u32[]{:S(2)}) copy-start(bf16[4,128]{1,0:T(4,128)(2,1)} %copy-done.115) | copy-start | bytes 3076
  (134 other events, 800.6 us)
Sparse Core Ops, SparseCore 0:
  63.8 72.4 reduce-scatter.24
  145.7 41.9 all-gather.10
  190.7 31.8 reduce-scatter.28
  270.9 71.3 reduce-scatter.26
  344.3 40.4 all-gather.14
  386.9 41.9 all-gather.12
  525.4 71.3 reduce-scatter.30
  598.3 41.9 all-gather.18
  642.5 41.9 all-gather.16
  726.3 40.4 reduce-scatter.34
  769.2 71.3 reduce-scatter.32
  849.2 41.9 all-gather.20
  1081.5 40.4 reduce-scatter.36
  1130.3 41.9 all-gather.22
  1174.6 38.9 reduce-scatter.40
  1332.6 40.4 reduce-scatter.38
  1375.1 33.1 all-gather.26
  1411.1 12.7 reduce-scatter.58
  1426.0 41.9 all-gather.24
  1472.5 108.1 reduce-scatter.54
  1585.3 106.9 reduce-scatter.56
  1696.6 58.9 reduce-scatter.46
  1759.9 60.5 reduce-scatter.52
  1825.2 65.8 reduce-scatter.50
  1895.2 60.2 reduce-scatter.48
  1959.2 60.4 reduce-scatter.44
  2023.3 142.8 all-reduce.15
  2171.0 59.8 reduce-scatter.42
  2235.3 83.2 reduce-scatter.60
  2325.2 129.8 all-reduce.13
where the time goes:
time: 2480 us; the launch traced here: 2460 us
  waiting for transfers between devices  1430 us (58%)
  matrix products  543 us (22%)
  other arithmetic  235 us (9%)
  local copies, waits for them, and re-layouts  152 us (6%)
  blocking collectives  78.7 us (3%)
    reduce_scatter x4, waiting for transfers between devices, sum_rows(): lax.psum_scatter(partial_rows(jnp.int32(0), rows_local * lax.axis_size('s...  272 us
    unnamed x33, waiting for transfers between devices  226 us
    psum x1, waiting for transfers between devices, on_device(): lax.psum((grad_skip_gain, grad_norm1, grad_q_gain, grad_k_gain, grad_norm...  135 us
    reduce_scatter x1, waiting for transfers between devices, on_device(): lax.psum_scatter(grad_fc2.astype(jnp.bfloat16), 'dp', scatter_dimension=1...  109 us
    dot_general x8, matrix products, one_block(): jnp.einsum('mwu,mou->mwo', query_portion, key_matrix_rows, preferred_elem...  100 us
    reduce_scatter x1, waiting for transfers between devices, on_device(): lax.psum_scatter(grad_fc1.astype(jnp.bfloat16), 'dp', scatter_dimension=0...  97.9 us
    reduce_scatter x3, waiting for transfers between devices, sum_grads(): lax.psum_scatter(partial_rows(jnp.int32(0), rows_local * lax.axis_size('s...  94.1 us
    all_gather x4, waiting for transfers between devices, gather_grads(): return lax.all_gather(local_rows, 'seq', axis=0, tiled=True)  83.2 us
  transfers between devices with their start and end apart: 31, of which 25 were waited for; matrix products, arithmetic and copies ran while one was open for 22% of the time, Pallas kernels for 0%

commit v1 on v0

v1 whole, which is shorter than its diff:
```python
import functools
import math

import jax
import jax.numpy as jnp
from jax import lax
from jax.experimental import pallas as pl
from jax.experimental.pallas import tpu as pltpu
from jax.sharding import PartitionSpec as P

HEAD_DIM = 88
SIDE = 32
SMALL_PER = 4
LANES = 128
KEY_ROWS = 384

PRECISE = lax.Precision.HIGHEST
EPSILON = 1e-06
HIDE = -30000.0
SCALE = 1.0 / math.sqrt(HEAD_DIM)
QUERY_SCALE = SCALE * math.log2(math.e)
KEY_BACK = math.log(2.0)
VMEM = 56 * 1024 * 1024

ROW_TIMES_ROW = (((1,), (1,)), ((), ()))
COL_TIMES_COL = (((0,), (0,)), ((), ()))


def params(*semantics):
    return pltpu.CompilerParams(dimension_semantics=semantics, vmem_limit_bytes=VMEM)


def lanes_of(shape):
    return lax.broadcasted_iota(jnp.int32, shape, len(shape) - 1)


def widen(values):
    fill = jnp.zeros((values.shape[0], LANES - HEAD_DIM), values.dtype)
    return jnp.concatenate([values, fill], 1)


def lane_mean(values, exact):
    high = values.astype(jnp.bfloat16)
    if exact:
        low = (values - high.astype(jnp.float32)).astype(jnp.bfloat16)
        high = jnp.concatenate([high, low], 1)
    ones = jnp.full((high.shape[1], LANES), 1.0, jnp.bfloat16)
    return jnp.dot(high, ones, preferred_element_type=jnp.float32) * (1.0 / HEAD_DIM)


def head_norm(values):
    inside = lanes_of(values.shape) < HEAD_DIM
    centre = jnp.where(inside, values - lane_mean(values, True), 0.0)
    spread = lax.rsqrt(lane_mean(centre * centre, False) + EPSILON)
    return centre * spread, spread


def by_parts(ref_rows, part, body):
    def step(number, carry):
        body(pl.ds(pl.multiple_of(number * part, part), part))
        return carry

    lax.fori_loop(0, ref_rows // part, step, 0)


def turn(values, rope):
    cosine, lead, trail = rope[:, :LANES], rope[:, LANES : 2 * LANES], rope[:, 2 * LANES :]
    quarter = HEAD_DIM // 4
    ahead = pltpu.roll(values, LANES - quarter, 1)
    behind = pltpu.roll(values, quarter, 1)
    return values * cosine + ahead * lead + behind * trail


def turn_back(values, rope):
    cosine, lead, trail = rope[:, :LANES], rope[:, LANES : 2 * LANES], rope[:, 2 * LANES :]
    quarter = HEAD_DIM // 4
    ahead = pltpu.roll(values, LANES - quarter, 1)
    behind = pltpu.roll(values, quarter, 1)
    return values * cosine - ahead * lead - behind * trail


def cut_kernel(*refs, kinds, columns, roped, chained):
    pre_ref, gain_ref = refs[:2]
    place = 2
    if roped:
        rope_ref = refs[place]
        place += 1
    extras = {}
    for kind in kinds:
        if kind != "v":
            extras[kind] = refs[place]
            place += 1
    if chained:
        place += len(kinds)
    outs = refs[place:]
    part = min(64, pre_ref.shape[0])
    lane = lanes_of((part, LANES))
    ones = jnp.where((lane == HEAD_DIM) | (lane == HEAD_DIM + 1), 1.0, 0.0)

    def rows_of(span):
        rope = rope_ref[span, :] if roped else None
        for number, kind in enumerate(kinds):
            for head, offset in enumerate(columns[number]):
                values = pre_ref[span, offset : offset + HEAD_DIM].astype(jnp.float32)
                values = widen(values)
                if kind == "v":
                    outs[number][head, span, :] = (values + ones).astype(jnp.bfloat16)
                    continue
                normed, _ = head_norm(values)
                normed = normed * gain_ref[number : number + 1, :]
                if roped:
                    normed = turn(normed, rope)
                if kind == "q":
                    normed = normed * QUERY_SCALE
                outs[number][head, span, :] = (normed + extras[kind][span, :]).astype(jnp.bfloat16)

    by_parts(pre_ref.shape[0], part, rows_of)


def cut_heads(pre, gains, kinds, columns, extras, rope=None, block=0, blocks=1, earlier=None):
    rows, width = pre.shape
    tile = min(256, rows)
    tiles = rows // tile
    here = lambda i: (block * tiles + i, 0)
    operands = [pre, gains]
    in_specs = [
        pl.BlockSpec((tile, width), lambda i: (i, 0)),
        pl.BlockSpec((8, LANES), lambda i: (0, 0)),
    ]
    if rope is not None:
        operands.append(rope)
        in_specs.append(pl.BlockSpec((tile, 3 * LANES), here))
    for kind in kinds:
        if kind != "v":
            operands.append(extras[kind])
            in_specs.append(pl.BlockSpec((tile, LANES), here))
    aliases = {}
    if earlier is not None:
        for number, array in enumerate(earlier):
            aliases[len(operands)] = number
            operands.append(array)
            in_specs.append(pl.BlockSpec(memory_space=pl.ANY))
    out_shape = [
        jax.ShapeDtypeStruct((len(cols), blocks * rows, LANES), jnp.bfloat16) for cols in columns
    ]
    out_specs = [
        pl.BlockSpec((len(cols), tile, LANES), lambda i: (0, block * tiles + i, 0))
        for cols in columns
    ]
    heads = sum(len(cols) for cols in columns)
    return pl.pallas_call(
        functools.partial(
            cut_kernel,
            kinds=kinds,
            columns=columns,
            roped=rope is not None,
            chained=earlier is not None,
        ),
        grid=(tiles,),
        in_specs=in_specs,
        out_specs=out_specs,
        out_shape=out_shape,
        input_output_aliases=aliases,
        compiler_params=params("arbitrary"),
        cost_estimate=pl.CostEstimate(
            flops=heads * rows * LANES * 40,
            bytes_accessed=rows * width * 4 + heads * rows * LANES * 2,
            transcendentals=0,
        ),
        name="cut_heads",
    )(*operands)


def join_kernel(*refs, kinds, columns, roped):
    pre_ref, gain_ref = refs[:2]
    place = 2
    if roped:
        rope_ref = refs[place]
        place += 1
    grads = refs[place : place + len(kinds)]
    out_ref, sum_ref = refs[place + len(kinds) :]
    part = min(256, pre_ref.shape[0])
    inside = lanes_of((part, LANES)) < HEAD_DIM

    @pl.when(pl.program_id(0) == 0)
    def _():
        sum_ref[...] = jnp.zeros_like(sum_ref)

    def rows_of(span):
        rope = rope_ref[span, :] if roped else None
        pieces = {}
        for number, kind in enumerate(kinds):
            total = jnp.zeros((part, LANES), jnp.float32)
            for head, offset in enumerate(columns[number]):
                slope = jnp.where(inside, grads[number][head, span, :], 0.0)
                if kind != "v":
                    slope = slope * (SCALE if kind == "q" else KEY_BACK)
                    if roped:
                        slope = turn_back(slope, rope)
                    values = pre_ref[span, offset : offset + HEAD_DIM].astype(jnp.float32)
                    normed, spread = head_norm(widen(values))
                    total = total + slope * normed
                    slope = slope * gain_ref[number : number + 1, :]
                    mean = lane_mean(slope, True)
                    mixed = lane_mean(slope * normed, False)
                    slope = (slope - mean - normed * mixed) * spread
                pieces[offset] = slope[:, :HEAD_DIM]
            if kind != "v":
                sum_ref[number : number + 1, :] += jnp.sum(total, 0, keepdims=True)
        out_ref[span, :] = jnp.concatenate(
            [pieces[offset] for offset in sorted(pieces)], 1
        ).astype(jnp.bfloat16)

    by_parts(pre_ref.shape[0], part, rows_of)


def join_heads(pre, gains, kinds, columns, grads, rope=None, block=0):
    rows, width = pre.shape
    tile = min(256, rows)
    tiles = rows // tile
    operands = [pre, gains]
    in_specs = [
        pl.BlockSpec((tile, width), lambda i: (i, 0)),
        pl.BlockSpec((8, LANES), lambda i: (0, 0)),
    ]
    if rope is not None:
        operands.append(rope)
        in_specs.append(pl.BlockSpec((tile, 3 * LANES), lambda i: (block * tiles + i, 0)))
    for array in grads:
        operands.append(array)
        in_specs.append(
            pl.BlockSpec((array.shape[0], tile, LANES), lambda i: (0, block * tiles + i, 0))
        )
    heads = sum(len(cols) for cols in columns)
    return pl.pallas_call(
        functools.partial(join_kernel, kinds=kinds, columns=columns, roped=rope is not None),
        grid=(tiles,),
        in_specs=in_specs,
        out_specs=[
            pl.BlockSpec((tile, width), lambda i: (i, 0)),
            pl.BlockSpec((8, LANES), lambda i: (0, 0)),
        ],
        out_shape=[
            jax.ShapeDtypeStruct((rows, width), jnp.bfloat16),
            jax.ShapeDtypeStruct((8, LANES), jnp.float32),
        ],
        compiler_params=params("arbitrary"),
        cost_estimate=pl.CostEstimate(
            flops=heads * rows * LANES * 60,
            bytes_accessed=rows * width * 6 + heads * rows * LANES * 4,
            transcendentals=0,
        ),
        name="join_heads",
    )(*operands)


def attend_kernel(pick, q_ref, k_ref, v_ref, o_ref, qx_ref, *, steps):
    step = pl.program_id(1)
    each, rows, _ = q_ref.shape
    part = min(256, rows)
    for start in range(0, rows, part):
        span = slice(start, start + part)
        merged = []
        for head in range(each):
            queries = q_ref[head, span, :]
            scores = lax.dot_general(
                queries, k_ref[head], ROW_TIMES_ROW, preferred_element_type=jnp.float32
            )
            weights = jnp.exp2(scores).astype(jnp.bfloat16)
            outputs = jnp.dot(weights, v_ref[head], preferred_element_type=jnp.float32)
            total = outputs[:, HEAD_DIM : HEAD_DIM + 1]
            merged.append((outputs * (1.0 / total))[:, :HEAD_DIM])
            level = -jnp.log2(total)
            high = level.astype(jnp.bfloat16).astype(jnp.float32)
            lane = lanes_of(outputs.shape)
            queries = queries.astype(jnp.float32)
            queries = jnp.where(lane == HEAD_DIM + 4, high, queries)
            queries = jnp.where(lane == HEAD_DIM + 5, level - high, queries)
            qx_ref[head, span, :] = queries.astype(jnp.bfloat16)
        merged = jnp.concatenate(merged, 1).astype(jnp.bfloat16)
        width = each * HEAD_DIM
        for number in range(steps):

            @pl.when(step == number)
            def _():
                o_ref[span, number * width : (number + 1) * width] = merged


def attend(queries, keys, values, pick, tile, key_rows, block=0, blocks=1):
    heads, rows_all, _ = queries.shape
    rows = rows_all // blocks
    tiles = rows // tile
    each = 2 if heads % 2 == 0 else 1
    there = lambda i, h, pick: (h, block * tiles + i, 0)
    keyed = lambda i, h, pick: (h, pick[i], 0)
    return pl.pallas_call(
        functools.partial(attend_kernel, steps=heads // each),
        grid_spec=pltpu.PrefetchScalarGridSpec(
            num_scalar_prefetch=1,
            grid=(tiles, heads // each),
            in_specs=[
                pl.BlockSpec((each, tile, LANES), there),
                pl.BlockSpec((each, key_rows, LANES), keyed),
                pl.BlockSpec((each, key_rows, LANES), keyed),
            ],
            out_specs=[
                pl.BlockSpec((tile, heads * HEAD_DIM), lambda i, h, pick: (i, 0)),
                pl.BlockSpec((each, tile, LANES), lambda i, h, pick: (h, i, 0)),
            ],
        ),
        out_shape=[
            jax.ShapeDtypeStruct((rows, heads * HEAD_DIM), jnp.bfloat16),
            jax.ShapeDtypeStruct((heads, rows, LANES), jnp.bfloat16),
        ],
        compiler_params=params("arbitrary", "arbitrary"),
        cost_estimate=pl.CostEstimate(
            flops=4 * heads * rows * key_rows * LANES,
            bytes_accessed=heads * (3 * rows + 2 * key_rows) * LANES * 2,
            transcendentals=heads * rows * key_rows,
        ),
        name="attend",
    )(pick, queries, keys, values)


def cut_grad_kernel(*refs, heads):
    grad_ref, o_ref = refs[:2]
    out_ref = refs[-1]
    rows = grad_ref.shape[0]
    lane = lanes_of((rows, LANES))
    for head in range(heads):
        span = slice(head * HEAD_DIM, (head + 1) * HEAD_DIM)
        slope = grad_ref[:, span].astype(jnp.bfloat16).astype(jnp.float32)
        level = -jnp.sum(slope * o_ref[:, span].astype(jnp.float32), 1, keepdims=True)
        high = level.astype(jnp.bfloat16).astype(jnp.float32)
        slope = widen(slope)
        slope = jnp.where(lane == HEAD_DIM, high, slope)
        slope = jnp.where(lane == HEAD_DIM + 1, level - high, slope)
        out_ref[head] = slope.astype(jnp.bfloat16)


def cut_grad(grad, outputs, block=0, blocks=1, earlier=None):
    rows, width = grad.shape
    heads = width // HEAD_DIM
    tile = min(256, rows)
    tiles = rows // tile
    operands = [grad, outputs]
    in_specs = [pl.BlockSpec((tile, width), lambda i: (i, 0))] * 2
    aliases = {}
    if earlier is not None:
        aliases = {2: 0}
        operands.append(earlier)
        in_specs.append(pl.BlockSpec(memory_space=pl.ANY))
    return pl.pallas_call(
        functools.partial(cut_grad_kernel, heads=heads),
        grid=(tiles,),
        in_specs=in_specs,
        out_specs=pl.BlockSpec((heads, tile, LANES), lambda i: (0, block * tiles + i, 0)),
        out_shape=jax.ShapeDtypeStruct((heads, blocks * rows, LANES), jnp.bfloat16),
        input_output_aliases=aliases,
        compiler_params=params("arbitrary"),
        cost_estimate=pl.CostEstimate(
            flops=heads * rows * LANES * 10,
            bytes_accessed=rows * width * 4 + heads * rows * LANES * 2,
            transcendentals=0,
        ),
        name="cut_grad",
    )(*operands)


def attend_back_kernel(pick, q_ref, k_ref, v_ref, g_ref, dq_ref, dk_ref, dv_ref, *, key_rows):
    tile = pl.program_id(1)
    queries, keys, slopes = q_ref[0], k_ref[0], g_ref[0]
    scores = lax.dot_general(keys, queries, ROW_TIMES_ROW, preferred_element_type=jnp.float32)
    weights = jnp.exp2(scores)
    pulls = lax.dot_general(v_ref[0], slopes, ROW_TIMES_ROW, preferred_element_type=jnp.float32)
    pulls = (weights * pulls).astype(jnp.bfloat16)
    value_grad = jnp.dot(weights.astype(jnp.bfloat16), slopes, preferred_element_type=jnp.float32)
    key_grad = jnp.dot(pulls, queries, preferred_element_type=jnp.float32)
    dq_ref[0] = lax.dot_general(pulls, keys, COL_TIMES_COL, preferred_element_type=jnp.float32)

    @pl.when(tile == 0)
    def _():
        dk_ref[...] = jnp.zeros_like(dk_ref)
        dv_ref[...] = jnp.zeros_like(dv_ref)

    start = pl.multiple_of(pick[tile] * key_rows, key_rows)
    dk_ref[0, pl.ds(start, key_rows), :] += key_grad
    dv_ref[0, pl.ds(start, key_rows), :] += value_grad


def attend_back(queries, keys, values, slopes, pick, tile, key_rows):
    heads, rows, _ = queries.shape
    all_keys = keys.shape[1]
    tiles = rows // tile
    there = lambda h, i, pick: (h, i, 0)
    keyed = lambda h, i, pick: (h, pick[i], 0)
    whole = lambda h, i, pick: (h, 0, 0)
    return pl.pallas_call(
        functools.partial(attend_back_kernel, key_rows=key_rows),
        grid_spec=pltpu.PrefetchScalarGridSpec(
            num_scalar_prefetch=1,
            grid=(heads, tiles),
            in_specs=[
                pl.BlockSpec((1, tile, LANES), there),
                pl.BlockSpec((1, key_rows, LANES), keyed),
                pl.BlockSpec((1, key_rows, LANES), keyed),
                pl.BlockSpec((1, tile, LANES), there),
            ],
            out_specs=[
                pl.BlockSpec((1, tile, LANES), there),
                pl.BlockSpec((1, all_keys, LANES), whole),
                pl.BlockSpec((1, all_keys, LANES), whole),
            ],
        ),
        out_shape=[
            jax.ShapeDtypeStruct((heads, rows, LANES), jnp.float32),
            jax.ShapeDtypeStruct((heads, all_keys, LANES), jnp.float32),
            jax.ShapeDtypeStruct((heads, all_keys, LANES), jnp.float32),
        ],
        compiler_params=params("arbitrary", "arbitrary"),
        cost_estimate=pl.CostEstimate(
            flops=10 * heads * rows * key_rows * LANES,
            bytes_accessed=heads * (2 * rows + 2 * key_rows) * LANES * 2
            + heads * (rows + 2 * all_keys) * LANES * 4,
            transcendentals=heads * rows * key_rows,
        ),
        name="attend_back",
    )(pick, queries, keys, values, slopes)


def dot_rows(left, right):
    return lax.dot_general(left, right, ROW_TIMES_ROW, preferred_element_type=jnp.float32)


def dot_sum(left, right):
    return lax.dot_general(left, right, COL_TIMES_COL, preferred_element_type=jnp.float32)


def dot_plain(left, right):
    return jnp.dot(left, right, preferred_element_type=jnp.float32)


def norm_rows(values):
    centre = values - jnp.mean(values, -1, keepdims=True)
    spread = lax.rsqrt(jnp.mean(centre * centre, -1, keepdims=True) + EPSILON)
    return centre * spread, spread


def norm_back(slope, normed, spread):
    mean = jnp.mean(slope, -1, keepdims=True)
    mixed = jnp.mean(slope * normed, -1, keepdims=True)
    return (slope - mean - normed * mixed) * spread


def low(values):
    return values.astype(jnp.bfloat16)


def wide(values):
    return values.astype(jnp.float32)


def after(values, *earlier):
    return lax.optimization_barrier((values,) + earlier)[0]


def from_back(values, step):
    size = lax.axis_size("seq")
    return lax.ppermute(values, "seq", [(i, (i + step) % size) for i in range(size)])


def to_back(values, step):
    size = lax.axis_size("seq")
    return lax.ppermute(values, "seq", [(i, (i - step) % size) for i in range(size)])


def gather_blocks(values):
    return [values] + [from_back(values, step) for step in range(1, lax.axis_size("seq"))]


def sum_blocks(terms):
    total = terms[0]
    for step in range(1, len(terms)):
        total = total + wide(to_back(low(terms[step]), step))
    return total


def sum_seq(values):
    if lax.axis_size("seq") == 2:
        return values + from_back(values, 1)
    return lax.psum(values, "seq")


def gather_weight(half):
    size = lax.axis_size("seq")
    if size == 1:
        return []
    parts = lax.axis_size("dp")
    rows = half.shape[0] // parts
    piece = lax.dynamic_slice_in_dim(half, lax.axis_index("dp") * rows, rows, 0)
    return [
        lax.all_gather(from_back(piece, step), "dp", axis=0, tiled=True) for step in range(1, size)
    ]


def scatter_sum(grad):
    parts = lax.axis_size("dp")
    rows, width = grad.shape[0] // parts, grad.shape[1]
    grad = low(grad)
    top = parts.bit_length() - 2
    if parts != 2 << top or top < 1:
        return wide(lax.psum_scatter(grad, "dp", scatter_dimension=0, tiled=True))
    place = lax.axis_index("dp")
    core = place & 1
    pairs = [[i, i + 1] for i in range(0, parts, 2)]
    held = lax.psum_scatter(
        grad, "dp", scatter_dimension=0, axis_index_groups=pairs, tiled=True
    )
    held = held.reshape((2,) * (top - 1) + (2 * rows, width))
    for bit in range(1, top):
        axis = top - 1 - bit
        mine = (place >> bit) & 1
        keep = lax.dynamic_index_in_dim(held, mine, axis, False)
        send = lax.dynamic_index_in_dim(held, 1 - mine, axis, False)
        came = lax.ppermute(send, "dp", [(i, i ^ (1 << bit)) for i in range(parts)])
        held = keep + came
    senders = [i for i in range(parts) if (i >> top) != (i & 1)]
    held = held + lax.ppermute(held, "dp", [(i, i ^ (1 << top)) for i in senders])
    owners = [i for i in range(parts) if (i >> top) == (i & 1)]
    send = lax.dynamic_slice_in_dim(held, (1 - core) * rows, rows, 0)
    came = lax.ppermute(send, "dp", [(i, i ^ 1) for i in owners])
    mine = lax.dynamic_slice_in_dim(held, core * rows, rows, 0)
    return wide(jnp.where((place >> top) == core, mine, came))


def rope_table(rows, cols):
    quarter = HEAD_DIM // 4
    lane = jnp.arange(LANES, dtype=jnp.int32)
    rates = jnp.exp(
        -math.log(10000.0) * (lane % quarter).astype(jnp.float32) / quarter
    )
    angles = jnp.arange(SIDE, dtype=jnp.float32)[:, None] * rates[None, :]
    cosine, sine = jnp.cos(angles), jnp.sin(angles)
    leading = (lane // quarter) % 2 == 0
    table = jnp.concatenate(
        [cosine, jnp.where(leading, -sine, 0.0), jnp.where(leading, 0.0, sine)], 1
    )
    lane = jnp.tile(lane, 3)
    by_row = jnp.where(lane < HEAD_DIM // 2, table, 0.0)
    by_col = jnp.where((lane >= HEAD_DIM // 2) & (lane < HEAD_DIM), table, 0.0)
    spots = jnp.arange(SIDE, dtype=jnp.int32)[None, :]
    picks = jnp.concatenate([rows[:, None] == spots, cols[:, None] == spots], 1)
    return jnp.dot(
        picks.astype(jnp.float32), jnp.concatenate([by_row, by_col], 0), precision=PRECISE
    )


def extra_lanes(columns):
    lane = jnp.arange(LANES, dtype=jnp.int32)[None, :]
    table = jnp.zeros((columns[0].shape[0], LANES), jnp.float32)
    for number, column in enumerate(columns):
        table = jnp.where(lane == HEAD_DIM + number, column[:, None], table)
    return table


def gain_rows(*gains):
    stacked = jnp.stack(gains)
    return jnp.pad(stacked, ((0, 8 - len(gains)), (0, LANES - HEAD_DIM)))


def timestep_features(steps, width):
    halfway = width // 2
    rates = jnp.exp(-math.log(10000.0) * jnp.arange(halfway, dtype=jnp.float32) / halfway)
    angles = steps.astype(jnp.float32)[:, None] * rates[None, :]
    return jnp.concatenate([jnp.cos(angles), jnp.sin(angles)], 1)


def gelu_and_slope(values):
    outer = 0.7978845608028654
    inner = 0.044715
    square = values * values
    bend = jnp.tanh(outer * (values + inner * square * values))
    half = 0.5 * (1.0 + bend)
    slope = half + 0.5 * values * (1.0 - bend * bend) * outer * (1.0 + 3.0 * inner * square)
    return low(values * half), slope


def on_device(
    latent,
    skip_input,
    clip_text,
    t5_text,
    bucket,
    counts,
    language,
    timesteps,
    cotangent,
    skip_weight,
    skip_gain,
    time_weight,
    shift_weight,
    norm1_gain,
    qkv_weight,
    q_gain,
    k_gain,
    out_weight,
    norm3_gain,
    cross_query,
    cq_gain,
    t5_weight,
    lang_embed,
    cross_kv,
    ck_gain,
    cross_out,
    norm2_gain,
    fc1_weight,
    fc2_weight,
):
    size = lax.axis_size("seq")
    me = lax.axis_index("seq")
    rows, width = latent.shape
    local_width = out_weight.shape[0]
    local_heads = local_width // HEAD_DIM
    all_heads = local_heads * size
    clip_length, text_local = clip_text.shape[1:]
    text_length = t5_text.shape[1]
    text_width = lang_embed.shape[1]
    tokens = rows * size
    small = (bucket[0] == 1).astype(jnp.int32)
    quarter = tokens // SMALL_PER
    tile = min(quarter, rows)
    slots = max(1, rows // quarter)

    def owner(step):
        return (me - step) % size

    def first_slot(device):
        return small * (device * rows // quarter)

    order = jnp.concatenate(
        [owner(step) * rows + jnp.arange(rows, dtype=jnp.int32) for step in range(size)]
    )
    slot_of = jnp.where(small == 1, order // quarter, 0)
    within = jnp.where(small == 1, order % quarter, order)
    across = jnp.where(small == 1, SIDE // 2, SIDE)
    rope = rope_table(within // across, within % across)
    own_slots = slot_of[:rows]
    self_extras = dict(
        q=extra_lanes([wide(slot_of == j) for j in range(SMALL_PER)]),
        k=extra_lanes(
            [jnp.where(slot_of == j, 0.0, HIDE) for j in range(SMALL_PER)]
            + [jnp.ones((tokens,), jnp.float32)] * 2
        ),
    )

    qkv_rows = qkv_weight.transpose(1, 2, 0).reshape(3 * local_width, width)
    cq_own = cross_query.T
    kv_own = cross_kv.transpose(1, 2, 0).reshape(2 * local_width, text_width)
    skip_blocks = [skip_weight] + gather_weight(skip_weight)
    cross_blocks = [jnp.concatenate([cq_own, cross_out], 0)]
    cross_blocks += gather_weight(cross_blocks[0])
    cq_full = jnp.concatenate([block[:local_width] for block in cross_blocks], 0)
    co_full = jnp.concatenate([block[local_width:] for block in cross_blocks], 0)
    kv_full = jnp.concatenate([kv_own] + gather_weight(kv_own), 0)

    features = low(timestep_features(timesteps, time_weight.shape[0]))
    gate = low(jax.nn.silu(dot_plain(features, time_weight)))
    shift_own = low(dot_plain(gate, shift_weight))
    shift_blocks = gather_blocks(shift_own)
    if size == 2:
        shifts = jnp.where(
            me == 0,
            jnp.concatenate(shift_blocks, 1),
            jnp.concatenate(shift_blocks[::-1], 1),
        )
    else:
        shifts = lax.all_gather(shift_own, "seq", axis=1, tiled=True)
    own_pick = own_slots[:, None] == jnp.arange(SMALL_PER, dtype=jnp.int32)[None, :]
    shift_rows = dot_plain(low(own_pick), shifts)

    partial = dot_plain(t5_text.reshape(-1, t5_text.shape[2]), t5_weight)
    partial = partial.reshape(SMALL_PER, text_length, text_width)

    def slots_for(values, device):
        return lax.dynamic_slice_in_dim(values, first_slot(device), slots, 0)

    projected = sum_blocks([slots_for(partial, owner(step)) for step in range(size)])
    clip_full = jnp.zeros((slots, clip_length, text_width), jnp.bfloat16)
    for step in range(size):
        block = slots_for(clip_text, (me + step) % size if step else me)
        block = from_back(block, step) if step else block
        clip_full = lax.dynamic_update_slice_in_dim(
            clip_full, block, owner(step) * text_local, 2
        )
    my_languages = lax.dynamic_slice_in_dim(language, first_slot(me), slots, 0)
    words = wide(lang_embed)
    chosen = jnp.where((my_languages == 1)[:, None], words[1][None, :], words[0][None, :])
    spare = KEY_ROWS - text_length - clip_length
    context = jnp.concatenate(
        [
            low(projected + chosen[:, None, :]),
            clip_full,
            jnp.zeros((slots, spare, text_width), jnp.bfloat16),
        ],
        1,
    ).reshape(slots * KEY_ROWS, text_width)
    my_counts = lax.dynamic_slice_in_dim(counts, first_slot(me), slots, 0)
    key_place = jnp.arange(KEY_ROWS, dtype=jnp.int32)[None, :]
    visible = jnp.where(
        key_place < text_length,
        key_place < my_counts[:, 1:],
        (key_place - text_length < my_counts[:, :1]) & (key_place < text_length + clip_length),
    ).reshape(-1)
    cross_key_extra = jnp.where(visible, 0.0, HIDE)
    ones_keys = jnp.ones((slots * KEY_ROWS,), jnp.float32)
    zeros_keys = jnp.zeros((slots * KEY_ROWS,), jnp.float32)
    cross_extras = dict(
        q=extra_lanes([jnp.ones((rows,), jnp.float32)]),
        k=extra_lanes([cross_key_extra, zeros_keys, zeros_keys, zeros_keys, ones_keys, ones_keys]),
    )
    context_kv = dot_rows(context, kv_full)
    kv_gains = gain_rows(ck_gain, ck_gain)
    key_columns = [
        2 * local_width * group + HEAD_DIM * head
        for group in range(size)
        for head in range(local_heads)
    ]
    kv_columns = [key_columns, [column + local_width for column in key_columns]]
    cross_keys, cross_values = cut_heads(
        context_kv, kv_gains, ("k", "v"), kv_columns, cross_extras
    )

    if size == 2:
        chunk = [
            jnp.where(me == 0, latent, skip_input),
            jnp.where(me == 0, skip_input, latent),
        ]
    else:
        joined = jnp.concatenate([latent, skip_input], 1)
        part = 2 * width // size
        chunk = [
            lax.dynamic_slice_in_dim(joined, owner(step) * part, part, 1) for step in range(size)
        ]
    hidden = dot_plain(chunk[0], skip_blocks[0])
    for step in range(1, size):
        hidden = hidden + dot_plain(chunk[step], skip_blocks[step])
    skip_normed, skip_spread = norm_rows(hidden)
    residual_one = skip_normed * skip_gain
    first_normed, first_spread = norm_rows(residual_one)
    normed = low(first_normed * norm1_gain + shift_rows)
    normed_blocks = gather_blocks(normed)

    self_kinds = ("q", "k", "v")
    self_columns = [
        [local_width * which + HEAD_DIM * head for head in range(local_heads)]
        for which in range(3)
    ]
    self_gains = gain_rows(q_gain, k_gain)
    qkv_blocks, cut = [], None
    for step in range(size):
        qkv_blocks.append(dot_rows(normed_blocks[step], qkv_rows))
        cut = cut_heads(
            qkv_blocks[step],
            self_gains,
            self_kinds,
            self_columns,
            self_extras,
            rope,
            step,
            size,
            cut,
        )
    queries, keys, values = cut
    no_pick = jnp.zeros((1,), jnp.int32)
    self_outputs, self_queries = [None] * size, [None] * size
    out_terms = [None] * size
    for step in list(range(1, size)) + [0]:
        self_outputs[step], self_queries[step] = attend(
            queries, keys, values, no_pick, rows, tokens, step, size
        )
        out_terms[step] = dot_plain(self_outputs[step], out_weight)
    residual_two = residual_one + sum_blocks(out_terms)

    third_normed, third_spread = norm_rows(residual_two)
    normed_cross = low(third_normed * norm3_gain)
    cross_pre = dot_rows(normed_cross, cq_full)
    query_gains = gain_rows(cq_gain)
    query_columns = [[HEAD_DIM * head for head in range(all_heads)]]
    (cross_queries,) = cut_heads(cross_pre, query_gains, ("q",), query_columns, cross_extras)
    cross_pick = small * (jnp.arange(rows // tile, dtype=jnp.int32) * tile // quarter)
    cross_outputs, cross_queries = attend(
        cross_queries, cross_keys, cross_values, cross_pick, tile, KEY_ROWS
    )
    residual_three = residual_two + dot_plain(cross_outputs, co_full)

    second_normed, second_spread = norm_rows(residual_three)
    mlp_blocks = gather_blocks(low(second_normed * norm2_gain))
    cotangent_blocks = gather_blocks(cotangent)
    active, expanded_grads, fc_terms, mlp_terms = [], [], [], []
    for step in range(size):
        gate_out, gate_slope = gelu_and_slope(dot_plain(mlp_blocks[step], fc1_weight))
        active.append(gate_out)
        expanded_grads.append(low(dot_rows(cotangent_blocks[step], fc2_weight) * gate_slope))
        mlp_terms.append(dot_rows(expanded_grads[step], fc1_weight))
    mlp_slope = sum_blocks(mlp_terms)
    for step in range(size):
        fc_terms.append(dot_plain(active[step], fc2_weight))
    block_output = low(residual_three + sum_blocks(fc_terms))
    active_all = jnp.concatenate(active, 0)
    expanded_all = jnp.concatenate(expanded_grads, 0)
    grad_fc2 = scatter_sum(dot_sum(jnp.concatenate(cotangent_blocks, 0), active_all)).T
    grad_fc1 = scatter_sum(dot_sum(jnp.concatenate(mlp_blocks, 0), expanded_all))

    grad_norm2 = jnp.sum(mlp_slope * second_normed, 0)
    grad_three = wide(cotangent) + norm_back(
        mlp_slope * norm2_gain, second_normed, second_spread
    )

    three_low = low(grad_three)
    cross_slopes = cut_grad(low(dot_rows(three_low, co_full)), cross_outputs)
    grad_cq, grad_ck, grad_cv = attend_back(
        cross_queries, cross_keys, cross_values, cross_slopes, cross_pick, tile, KEY_ROWS
    )
    cross_pre_grad, query_sums = join_heads(
        cross_pre, query_gains, ("q",), query_columns, (grad_cq,)
    )
    cross_slope = dot_plain(cross_pre_grad, cq_full)
    grad_norm3 = jnp.sum(cross_slope * third_normed, 0)
    grad_two = grad_three + norm_back(cross_slope * norm3_gain, third_normed, third_spread)
    two_blocks = gather_blocks(low(grad_two))
    context_kv_grad, key_sums = join_heads(
        context_kv, kv_gains, ("k", "v"), kv_columns, (grad_ck, grad_cv)
    )
    context_grad = dot_plain(context_kv_grad, kv_full).reshape(slots, KEY_ROWS, text_width)

    def own_part(summed):
        blocks = [
            summed[:, step * (summed.shape[1] // size) : (step + 1) * (summed.shape[1] // size)]
            for step in range(size)
        ]
        return sum_blocks(blocks)

    grad_cross = scatter_sum(
        jnp.concatenate(
            [dot_sum(normed_cross, cross_pre_grad), dot_sum(three_low, cross_outputs)], 1
        )
    )
    grad_cross_query = own_part(grad_cross[:, : all_heads * HEAD_DIM])
    grad_cross_out = own_part(grad_cross[:, all_heads * HEAD_DIM :]).T
    grad_cross_kv = own_part(scatter_sum(dot_sum(context, context_kv_grad)))
    grad_cross_kv = grad_cross_kv.reshape(-1, 2, local_width)

    def spread_slots(blocks):
        found = []
        for slot in range(SMALL_PER):
            total = 0.0
            for step, block in enumerate(blocks):
                offset = slot - first_slot((me + step) % size)
                inside = (offset >= 0) & (offset < slots)
                part = lax.dynamic_index_in_dim(
                    block, jnp.clip(offset, 0, slots - 1), 0, False
                )
                total = total + jnp.where(inside, wide(part), 0.0)
            found.append(total)
        return jnp.stack(found)

    text_grad = context_grad[:, :text_length]
    text_low = low(text_grad)
    text_blocks = [text_low] + [to_back(text_low, step) for step in range(1, size)]
    project_all = low(spread_slots(text_blocks)).reshape(SMALL_PER * text_length, text_width)
    clip_blocks = []
    for step in range(size):
        block = lax.dynamic_slice_in_dim(
            context_grad[:, text_length : text_length + clip_length],
            owner(step) * text_local,
            text_local,
            2,
        )
        clip_blocks.append(to_back(low(block), step) if step else block)
    grad_clip = spread_slots(clip_blocks)
    grad_t5 = dot_rows(project_all, t5_weight).reshape(t5_text.shape)
    grad_t5_weight = scatter_sum(
        dot_sum(project_all, t5_text.reshape(-1, t5_text.shape[2]))
    ).T
    tongues = wide(my_languages[None, :] == jnp.arange(2, dtype=jnp.int32)[:, None])
    grad_lang = jnp.dot(tongues, jnp.sum(text_grad, 1), precision=PRECISE)

    slopes = None
    for step in range(size):
        slopes = cut_grad(
            low(dot_rows(two_blocks[step], out_weight)), self_outputs[step], step, size, slopes
        )
    self_queries = jnp.concatenate(self_queries, 1)
    back_tile = min(512, tokens)
    head_grads = attend_back(
        self_queries,
        keys,
        values,
        slopes,
        jnp.zeros((tokens // back_tile,), jnp.int32),
        back_tile,
        tokens,
    )
    qkv_grads, normed_terms = [None] * size, [None] * size
    self_sums = 0.0
    for step in list(range(1, size)) + [0]:
        qkv_grads[step], sums = join_heads(
            qkv_blocks[step], self_gains, self_kinds, self_columns, head_grads, rope, step
        )
        self_sums = self_sums + sums
        normed_terms[step] = dot_plain(qkv_grads[step], qkv_rows)
    normed_slope = sum_blocks(normed_terms)
    normed_all = jnp.concatenate(normed_blocks, 0)
    grad_qkv = scatter_sum(dot_sum(normed_all, jnp.concatenate(qkv_grads, 0)))
    grad_qkv = grad_qkv.reshape(-1, 3, local_width)
    grad_out = scatter_sum(
        dot_sum(jnp.concatenate(two_blocks, 0), jnp.concatenate(self_outputs, 0))
    ).T

    grad_norm1 = jnp.sum(normed_slope * first_normed, 0)
    residual_slope = grad_two + norm_back(normed_slope * norm1_gain, first_normed, first_spread)
    grad_skip_gain = jnp.sum(residual_slope * skip_normed, 0)
    hidden_low = low(norm_back(residual_slope * skip_gain, skip_normed, skip_spread))
    hidden_blocks = gather_blocks(hidden_low)
    joined_blocks = [chunk[0]]
    for step in range(1, size):
        if size == 2:
            block = chunk[1]
        else:
            block = lax.dynamic_slice_in_dim(joined, (me + step) % size * part, part, 1)
        joined_blocks.append(from_back(block, step))
    grad_skip_weight = scatter_sum(
        dot_sum(jnp.concatenate(hidden_blocks, 0), jnp.concatenate(joined_blocks, 0))
    ).T
    joined_grads = [dot_rows(hidden_low, block) for block in skip_blocks]
    if size == 2:
        grad_latent = jnp.where(me == 0, joined_grads[0], joined_grads[1])
        grad_skip_input = jnp.where(me == 0, joined_grads[1], joined_grads[0])
    else:
        joined_grad = jnp.zeros((rows, 2 * width), jnp.float32)
        for step in range(size):
            joined_grad = lax.dynamic_update_slice_in_dim(
                joined_grad, joined_grads[step], owner(step) * part, 1
            )
        grad_latent, grad_skip_input = joined_grad[:, :width], joined_grad[:, width:]

    shift_terms = jnp.dot(wide(own_pick).T, normed_slope, precision=PRECISE)
    shift_low = low(sum_seq(shift_terms))
    shift_all = lax.all_gather(shift_low, "dp", axis=0, tiled=True)
    steps_all = lax.all_gather(timesteps, "dp", axis=0, tiled=True)
    features_all = low(timestep_features(steps_all, time_weight.shape[0]))
    gate_all, silu_pull = jax.vjp(jax.nn.silu, dot_plain(features_all, time_weight))
    shift_mine = lax.dynamic_slice_in_dim(shift_all, me * local_width, local_width, 1)
    parts = lax.axis_size("dp")
    gate_mine = lax.dynamic_slice_in_dim(
        low(gate_all), lax.axis_index("dp") * (width // parts), width // parts, 1
    )
    grad_shift = dot_sum(gate_mine, shift_mine)
    (time_slope,) = silu_pull(sum_seq(dot_rows(shift_mine, shift_weight)))
    grad_time = jnp.dot(wide(features_all).T, time_slope, precision=PRECISE)

    gains = [
        grad_skip_gain,
        grad_norm1,
        self_sums[0, :HEAD_DIM],
        self_sums[1, :HEAD_DIM],
        grad_norm3,
        query_sums[0, :HEAD_DIM],
        key_sums[0, :HEAD_DIM],
        grad_norm2,
        grad_lang.reshape(-1),
    ]
    packed = lax.psum(jnp.concatenate(gains), ("dp", "seq"))
    totals, start = [], 0
    for gain in gains:
        totals.append(packed[start : start + gain.shape[0]])
        start += gain.shape[0]
    return (
        block_output,
        grad_latent,
        grad_skip_input,
        grad_clip,
        grad_t5,
        grad_skip_weight,
        totals[0],
        grad_time,
        grad_shift,
        totals[1],
        grad_qkv,
        totals[2],
        totals[3],
        grad_out,
        totals[4],
        grad_cross_query,
        totals[5],
        grad_t5_weight,
        totals[8].reshape(lang_embed.shape),
        grad_cross_kv,
        totals[6],
        grad_cross_out,
        totals[7],
        grad_fc1,
        grad_fc2,
    )


def solution(mesh):
    return jax.shard_map(
        on_device,
        mesh=mesh,
        in_specs=(
            P(("dp", "seq"), None),
            P(("dp", "seq"), None),
            P("dp", None, "seq"),
            P("dp", None, "seq"),
            P("dp"),
            P("dp", None),
            P("dp"),
            P("dp"),
            P(("dp", "seq"), None),
            P("seq", None),
            P(),
            P(),
            P(None, "seq"),
            P(),
            P(None, None, "seq"),
            P(),
            P(),
            P("seq", None),
            P(),
            P(None, "seq"),
            P(),
            P("seq", None),
            P(),
            P(None, None, "seq"),
            P(),
            P("seq", None),
            P(),
            P(None, "seq"),
            P("seq", None),
        ),
        out_specs=(
            P(("dp", "seq"), None),
            P(("dp", "seq"), None),
            P(("dp", "seq"), None),
            P("dp", None, "seq"),
            P("dp", None, "seq"),
            P("seq", "dp"),
            P(),
            P(),
            P("dp", "seq"),
            P(),
            P("dp", None, "seq"),
            P(),
            P(),
            P("seq", "dp"),
            P(),
            P("dp", "seq"),
            P(),
            P("seq", "dp"),
            P(),
            P("dp", None, "seq"),
            P(),
            P("seq", "dp"),
            P(),
            P("dp", "seq"),
            P("seq", "dp"),
        ),
        check_vma=False,
    )
```

time: 2480 us -> 1280 us (0.52)
  waiting for transfers between devices: 1430 us -> 419 us
  matrix products: 543 us -> 289 us
  Pallas kernels: 0 us -> 218 us
  other arithmetic: 235 us -> 65.8 us
  starting transfers between devices: 7.99 us -> 77.1 us
  local copies, waits for them, and re-layouts: 152 us -> 84.6 us
    reduce_scatter x17 -> x8, waiting for transfers between devices: 887 us -> 0.09 us  [scatter_sum(): lax.psum_scatter(grad, 'dp', scatter_dimension=0, axis_index_groups=pairs...]
    ppermute x0 -> x55, waiting for transfers between devices: none -> 419 us  [the longest x16 200 us: scatter_sum(): came = lax.ppermute(send, 'dp', [(i, i ^ 1 << bit) for i in range(parts)])]
    dot_general x63 -> x46, matrix products: 543 us -> 289 us  [the longest x17 108 us: dot_plain(): return jnp.dot(left, right, preferred_element_type=jnp.float32)]
    unnamed x33 -> x11, waiting for transfers between devices: 226 us -> 0.18 us
    pallas_call x0 -> x16, Pallas kernels: none -> 218 us  [the longest x4 64 us: join_heads(): pl.pallas_call(functools.partial(join_kernel, kinds=kinds, columns=column...]
    all_gather x9 -> x3, waiting for transfers between devices: 180 us -> 0.01 us  [gather_weight(): lax.all_gather(from_back(piece, step), 'dp', axis=0, tiled=True)]
    psum x1 -> x0, waiting for transfers between devices: 135 us -> none  [on_device(): lax.psum((grad_skip_gain, grad_norm1, grad_q_gain, grad_k_gain, grad_norm...]
    reduce_sum x36 -> x7, other arithmetic: 106 us -> 6.59 us  [the longest x1 3.92 us: on_device(): grad_skip_gain = jnp.sum(residual_slope * skip_normed, 0)]
  transfers between devices with their start and end apart: 31 -> 66, of which waited for: 25 -> 31; matrix products, arithmetic and copies ran while one was open for 22% -> 29% of each run, Pallas kernels for 0% -> 13%
where the time goes in v1:
time: 1280 us; the launch traced here: 1260 us
  waiting for transfers between devices  419 us (33%)
  matrix products  289 us (23%)
  Pallas kernels  218 us (17%)
  blocking collectives  90.4 us (7%)
  local copies, waits for them, and re-layouts  84.6 us (7%)
  starting transfers between devices  77.1 us (6%)
  other arithmetic  65.8 us (5%)
  between operations  17.6 us (1%)
    ppermute x16, waiting for transfers between devices, scatter_sum(): came = lax.ppermute(send, 'dp', [(i, i ^ 1 << bit) for i in range(parts)])  200 us
    dot_general x17, matrix products, dot_plain(): return jnp.dot(left, right, preferred_element_type=jnp.float32)  108 us
    dot_general x15, matrix products, dot_rows(): lax.dot_general(left, right, ROW_TIMES_ROW, preferred_element_type=jnp.fl...  97.6 us
    ppermute x13, waiting for transfers between devices, from_back(): lax.ppermute(values, 'seq', [(i, (i + step) % size) for i in range(size)])  94.3 us
    ppermute x10, waiting for transfers between devices, to_back(): lax.ppermute(values, 'seq', [(i, (i - step) % size) for i in range(size)])  84.5 us
    dot_general x10, matrix products, dot_sum(): lax.dot_general(left, right, COL_TIMES_COL, preferred_element_type=jnp.fl...  75.6 us
    pallas_call x4, Pallas kernels, join_heads(): pl.pallas_call(functools.partial(join_kernel, kinds=kinds, columns=column...  64 us
    pallas_call x2, Pallas kernels, attend_back(): pl.pallas_call(functools.partial(attend_back_kernel, key_rows=key_rows),...  62.5 us
  transfers between devices with their start and end apart: 66, of which 31 were waited for; matrix products, arithmetic and copies ran while one was open for 29% of the time, Pallas kernels for 13%

profile of v1, /device:TPU:15, one launch (start us, length us, event | category | flops | bytes accessed | tf_op | source)
XLA Modules:
  0.0 1261.6 jit_solution(1547517762246845457)
XLA Ops:
  80.4 9.0 collective-permute-done.5
  93.5 8.5 fusion.155.refs_0_
  102.0 9.2 cut_heads.4
  111.2 9.1 collective-permute-done.2
  120.2 8.8 fusion.154.refs_0_
  129.0 8.5 cut_heads.5
  137.6 10.2 attend.4
  152.1 11.4 fusion.14.refs_0_
  163.5 10.9 cut_heads.7
  178.8 10.2 attend.3
  207.7 18.8 %attend.5 = (bf16[512,1408]{1,0:T(8,128)(2,1)}, bf16[16,512,128]{2,1,0:T(8,128)(2,1)}) custom-call(s32[2]{0:T(128)} %fusion.119.pick, bf16[16,512,128]{2,1,0:T(8,128)(2,1)} %cut_heads.6.q_ref, bf16[16,768,128]{2,1,0:T(8,128)(2,1)} %get-tuple-element.61.k_ref, bf16[16,768,128]{2,1,0:T(8,128)(2,1)} %get-tuple-element.62.v_ref), custom_call_target="tpu_custom_call" | custom-call | flops 1610612736 | bytes 9437184 | tf_op jit(solution)/shard_map/attend/pallas_call | solution.py:296
  233.1 12.4 multiply_convert_fusion.3
  245.6 12.8 %multiply_convert_fusion.1 = bf16[512,3072]{1,0:T(8,128)(2,1)} fusion(f32[512,3072]{1,0:T(8,128)} %get-tuple-element.270, bf16[512,1408]{1,0:T(8,128)(2,1)S(1)} %copy-done.108, bf16[3072,1408]{1,0:T(8,128)(2,1)} %param.57), kind=kOutput, calls=%fused_computation.20 | convolution fusion | flops 4457496576 | bytes 19529728 | tf_op jit(solution)/shard_map/dot_general | solution.py:432
  271.3 13.5 %multiply_convert_fusion = bf16[512,3072]{1,0:T(8,128)(2,1)} fusion(f32[512,3072]{1,0:T(8,128)} %get-tuple-element.272, bf16[512,1408]{1,0:T(8,128)(2,1)} %collective-permute-done.10, bf16[3072,1408]{1,0:T(8,128)(2,1)} %param.57), kind=kOutput, calls=%fused_computation.19 | convolution fusion | flops 4457496576 | bytes 19529728 | tf_op jit(solution)/shard_map/dot_general | solution.py:432
  293.0 8.7 convolution_convert_fusion.12
  302.1 19.7 %collective-permute-done.11 = bf16[512,1408]{1,0:T(8,128)(2,1)} collective-permute-done((bf16[512,1408]{1,0:T(8,128)(2,1)S(1)}, bf16[512,1408]{1,0:T(8,128)(2,1)}, u32[]{:S(2)}, u32[]{:S(2)}) %collective-permute-start.11) | collective-permute-done | bytes 1441824 | tf_op jit(solution)/shard_map/ppermute | solution.py:474
  321.8 9.3 multiply_reduce_fusion
  331.1 21.6 %collective-permute-done.9 = bf16[512,1408]{1,0:T(8,128)(2,1)} collective-permute-done((bf16[512,1408]{1,0:T(8,128)(2,1)}, bf16[512,1408]{1,0:T(8,128)(2,1)}, u32[]{:S(2)}, u32[]{:S(2)}) %collective-permute-start.9) | collective-permute-done | bytes 1441824 | tf_op jit(solution)/shard_map/ppermute | solution.py:474
  352.7 12.4 multiply_add_fusion.4
  378.1 31.9 %attend_back.2 = (f32[16,512,128]{2,1,0:T(8,128)}, f32[16,768,128]{2,1,0:T(8,128)}, f32[16,768,128]{2,1,0:T(8,128)}) custom-call(s32[2]{0:T(128)} %fusion.119.pick, bf16[16,512,128]{2,1,0:T(8,128)(2,1)} %get-tuple-element.64.q_ref, bf16[16,768,128]{2,1,0:T(8,128)(2,1)} %get-tuple-element.61.k_ref, bf16[16,768,128]{2,1,0:T(8,128)(2,1)} %get-tuple-element.62.v_ref, ...), custom_call_target="tpu_custom_call" | custom-call | flops 4026531840 | bytes 24117248 | tf_op jit(solution)/shard_map/attend_back/pallas_call | solution.py:398
  410.0 20.6 %join_heads.7 = (bf16[768,2816]{1,0:T(8,128)(2,1)}, f32[8,128]{1,0:T(8,128)}) custom-call(f32[768,2816]{1,0:T(8,128)} %fusion.14.refs_0_, f32[8,128]{1,0:T(8,128)} %select_maximum_fusion.refs_1_, f32[16,768,128]{2,1,0:T(8,128)} %get-tuple-element.74.refs_2_, f32[16,768,128]{2,1,0:T(8,128)} %get-tuple-element.75.refs_3_), custom_call_target="tpu_custom_call" | custom-call | flops 188743680 | bytes 25559040 | tf_op jit(solution)/shard_map/join_heads/pallas_call | solution.py:235
  440.7 19.2 %collective-permute-done.15 = bf16[2,256,1024]{2,1,0:T(8,128)(2,1)} collective-permute-done((bf16[2,256,1024]{2,1,0:T(8,128)(2,1)S(1)}, bf16[2,256,1024]{2,1,0:T(8,128)(2,1)}, u32[]{:S(2)}, u32[]{:S(2)}) %collective-permute-start.15) | collective-permute-done | bytes 1048608 | tf_op jit(solution)/shard_map/ppermute | solution.py:474
  467.7 14.3 %join_heads.4 = (bf16[512,1408]{1,0:T(8,128)(2,1)}, f32[8,128]{1,0:T(8,128)}) custom-call(f32[512,1408]{1,0:T(8,128)} %fusion.35.refs_0_, f32[8,128]{1,0:T(8,128)} %pad.12.refs_1_, f32[16,512,128]{2,1,0:T(8,128)} %get-tuple-element.65.refs_2_), custom_call_target="tpu_custom_call" | custom-call | flops 62914560 | bytes 8519680 | tf_op jit(solution)/shard_map/join_heads/pallas_call | solution.py:235
  491.5 26.8 %collective-permute-done.12 = bf16[512,1408]{1,0:T(8,128)(2,1)S(1)} collective-permute-done((bf16[512,1408]{1,0:T(8,128)(2,1)S(1)}, bf16[512,1408]{1,0:T(8,128)(2,1)S(1)}, u32[]{:S(2)}, u32[]{:S(2)}) %collective-permute-start.12) | collective-permute-done | bytes 1441824 | tf_op jit(solution)/shard_map/ppermute | solution.py:469
  523.3 8.9 convolution_convert_fusion.6
  549.8 30.6 %attend_back.3 = (f32[8,1024,128]{2,1,0:T(8,128)}, f32[8,1024,128]{2,1,0:T(8,128)}, f32[8,1024,128]{2,1,0:T(8,128)}) custom-call(s32[2]{0:T(128)} %broadcast.795.pick, bf16[8,1024,128]{2,1,0:T(8,128)(2,1)} %pad_maximum_fusion.10.q_ref, bf16[8,1024,128]{2,1,0:T(8,128)(2,1)} %get-tuple-element.57.k_ref, bf16[8,1024,128]{2,1,0:T(8,128)(2,1)} %get-tuple-element.58.v_ref, ...), custom_call_target="tpu_custom_call" | custom-call | flops 10737418240 | bytes 20971520 | tf_op jit(solution)/shard_map/attend_back/pallas_call | solution.py:398
  580.4 14.6 %join_heads.6 = (bf16[512,2112]{1,0:T(8,128)(2,1)}, f32[8,128]{1,0:T(8,128)}) custom-call(f32[512,2112]{1,0:T(8,128)} %fusion.154.refs_0_, f32[8,128]{1,0:T(8,128)} %select_maximum_fusion.1.refs_1_, f32[1024,384]{1,0:T(8,128)} %fusion.45.refs_2_, f32[8,1024,128]{2,1,0:T(8,128)} %get-tuple-element.69.refs_3_, f32[8,1024,128]{2,1,0:T(8,128)} %get-tuple-element.70.refs_4_, ...), custom_call_target="tpu_custom_call" | custom-call | flops 94371840 | bytes 12779520 | tf_op jit(solution)/shard_map/join_heads/pallas_call | solution.py:235
  605.2 14.4 %join_heads.5 = (bf16[512,2112]{1,0:T(8,128)(2,1)}, f32[8,128]{1,0:T(8,128)}) custom-call(f32[512,2112]{1,0:T(8,128)} %fusion.155.refs_0_, f32[8,128]{1,0:T(8,128)} %select_maximum_fusion.1.refs_1_, f32[1024,384]{1,0:T(8,128)} %fusion.45.refs_2_, f32[8,1024,128]{2,1,0:T(8,128)} %get-tuple-element.69.refs_3_, f32[8,1024,128]{2,1,0:T(8,128)} %get-tuple-element.70.refs_4_, ...), custom_call_target="tpu_custom_call" | custom-call | flops 94371840 | bytes 12779520 | tf_op jit(solution)/shard_map/join_heads/pallas_call | solution.py:235
  619.7 11.5 collective-permute-done.13
  645.8 16.2 %collective-permute-done.17 = bf16[512,1408]{1,0:T(8,128)(2,1)S(1)} collective-permute-done((bf16[512,1408]{1,0:T(8,128)(2,1)S(1)}, bf16[512,1408]{1,0:T(8,128)(2,1)S(1)}, u32[]{:S(2)}, u32[]{:S(2)}) %collective-permute-start.17) | collective-permute-done | bytes 1441824 | tf_op jit(solution)/shard_map/ppermute | solution.py:469
  662.0 30.9 %collective-permute-done.16 = bf16[512,1408]{1,0:T(8,128)(2,1)S(1)} collective-permute-done((bf16[512,1408]{1,0:T(8,128)(2,1)S(1)}, bf16[512,1408]{1,0:T(8,128)(2,1)S(1)}, u32[]{:S(2)}, u32[]{:S(2)}) %collective-permute-start.16) | collective-permute-done | bytes 1441824 | tf_op jit(solution)/shard_map/ppermute | solution.py:469
  700.7 11.7 convolution_convert_fusion.2
  732.3 11.6 copy.107
  745.3 13.8 %convolution_convert_fusion.1 = bf16[1408,3072]{1,0:T(8,128)(2,1)} fusion(bf16[512,3072]{1,0:T(8,128)(2,1)} %multiply_convert_fusion, bf16[512,3072]{1,0:T(8,128)(2,1)} %multiply_convert_fusion.1, bf16[512,1408]{1,0:T(8,128)(2,1)} %copy-done.113, bf16[512,1408]{1,0:T(8,128)(2,1)S(1)} %copy-done.27), kind=kOutput, calls=%fused_computation.1 | convolution fusion | flops 8881045504 | bytes 17825792 | tf_op jit(solution)/shard_map/dot_general | solution.py:436
  760.5 14.2 %convolution_convert_fusion = bf16[1408,3072]{1,0:T(8,128)(2,1)} fusion(bf16[512,3072]{1,0:T(8,128)(2,1)} %copy-done.119, bf16[512,3072]{1,0:T(8,128)(2,1)} %get-tuple-element.269, bf16[512,1408]{1,0:T(8,128)(2,1)} %collective-permute-done.10, bf16[512,1408]{1,0:T(8,128)(2,1)S(1)} %copy-done.109), kind=kOutput, calls=%fused_computation | convolution fusion | flops 8881045504 | bytes 17825792 | tf_op jit(solution)/shard_map/dot_general | solution.py:436
  776.9 23.3 %all-reduce.3 = s32[64]{0:T(128)S(1)} all-reduce(s32[64]{0:T(128)S(1)} %dynamic-update-slice), channel_id=1, replica_groups=mesh['dp'=16,'seq'=2] {'dp'}, use_global_device_ids=true, to_apply=%add.3 | all-reduce | flops 64 | bytes 512
  815.2 43.3 %psum.7 = f32[8032]{0:T(1024)S(1)} all-reduce(f32[8032]{0:T(1024)S(1)} %concatenate.194), channel_id=1, replica_groups=mesh['dp'=16,'seq'=2] {'dp','seq'}, use_global_device_ids=true, to_apply=%region_22.23 | all-reduce | flops 8032 | bytes 64256 | tf_op jit(solution)/shard_map/psum | solution.py:973
  875.9 23.9 %all-gather = bf16[16,4,1408]{2,1,0:T(4,128)(2,1)S(1)} all-gather(bf16[1,4,1408]{2,1,0:T(4,128)(2,1)S(1)} %fusion.83), channel_id=1, replica_groups=mesh['dp'=16,'seq'=2] {'dp'}, dimensions={0}, use_global_device_ids=true | all-gather | bytes 191488 | tf_op jit(solution)/shard_map/all_gather | solution.py:949
  941.1 10.3 collective-permute-done.41
  956.3 16.2 %collective-permute-done.18 = bf16[2,176,1408]{2,1,0:T(8,128)(2,1)S(1)} collective-permute-done((bf16[2,176,1408]{2,1,0:T(8,128)(2,1)S(1)}, bf16[2,176,1408]{2,1,0:T(8,128)(2,1)S(1)}, u32[]{:S(2)}, u32[]{:S(2)}) %collective-permute-start.18) | collective-permute-done | bytes 991264 | tf_op jit(solution)/shard_map/ppermute | solution.py:525
  978.1 11.7 collective-permute-done.19
  1011.3 19.7 %collective-permute-done.24 = bf16[2,176,2112]{2,1,0:T(8,128)(2,1)S(1)} collective-permute-done((bf16[2,176,2112]{2,1,0:T(8,128)(2,1)S(1)}, bf16[2,176,2112]{2,1,0:T(8,128)(2,1)S(1)}, u32[]{:S(2)}, u32[]{:S(2)}) %collective-permute-start.24) | collective-permute-done | bytes 1486880 | tf_op jit(solution)/shard_map/ppermute | solution.py:525
  1035.7 14.4 %collective-permute-done.25 = bf16[176,2112]{1,0:T(8,128)(2,1)} collective-permute-done((bf16[176,2112]{1,0:T(8,128)(2,1)S(1)}, bf16[176,2112]{1,0:T(8,128)(2,1)}, u32[]{:S(2)}, u32[]{:S(2)}) %collective-permute-start.25) | collective-permute-done | bytes 743456 | tf_op jit(solution)/shard_map/ppermute | solution.py:525
  1082.7 41.6 %collective-permute-done.47 = bf16[2,176,3072]{2,1,0:T(8,128)(2,1)} collective-permute-done((bf16[2,176,3072]{2,1,0:T(8,128)(2,1)}, bf16[2,176,3072]{2,1,0:T(8,128)(2,1)}, u32[]{:S(2)}, u32[]{:S(2)}) %collective-permute-start.47) | collective-permute-done | bytes 2162720 | tf_op jit(solution)/shard_map/ppermute | solution.py:525
  1129.0 41.6 %collective-permute-done.51 = bf16[2,176,3072]{2,1,0:T(8,128)(2,1)S(1)} collective-permute-done((bf16[2,176,3072]{2,1,0:T(8,128)(2,1)S(1)}, bf16[2,176,3072]{2,1,0:T(8,128)(2,1)S(1)}, u32[]{:S(2)}, u32[]{:S(2)}) %collective-permute-start.51) | collective-permute-done | bytes 2162720 | tf_op jit(solution)/shard_map/ppermute | solution.py:525
  1177.6 28.5 %collective-permute-done.52 = bf16[176,3072]{1,0:T(8,128)(2,1)S(1)} collective-permute-done((bf16[176,3072]{1,0:T(8,128)(2,1)S(1)}, bf16[176,3072]{1,0:T(8,128)(2,1)S(1)}, u32[]{:S(2)}, u32[]{:S(2)}) %collective-permute-start.52) | collective-permute-done | bytes 1081376 | tf_op jit(solution)/shard_map/ppermute | solution.py:525
  1218.2 13.4 %collective-permute-done.49 = bf16[176,3072]{1,0:T(8,128)(2,1)} collective-permute-done((bf16[176,3072]{1,0:T(8,128)(2,1)S(1)}, bf16[176,3072]{1,0:T(8,128)(2,1)}, u32[]{:S(2)}, u32[]{:S(2)}) %collective-permute-start.49) | collective-permute-done | bytes 1081376 | tf_op jit(solution)/shard_map/ppermute | solution.py:528
  1234.6 8.6 collective-permute-done.53
  (590 shorter events, 431.2 us)
Async XLA Ops:
  7.2 60.6 %all-gather.5.cloned.1.call-start = ((), (), s32[]{:S(2)}) async-start(), calls=%async_computation.8 | async-start | bytes 4212736 | tf_op jit(solution)/shard_map/all_gather | solution.py:502
  16.0 136.1 %all-gather.9.cloned.1.call-start = ((), (), s32[]{:S(2)}) async-start(), calls=%async_computation.10 | async-start | bytes 3063808 | tf_op jit(solution)/shard_map/all_gather | solution.py:502
  20.5 55.1 %collective-permute-start.1 = (bf16[4,704]{1,0:T(4,128)(2,1)}, bf16[4,704]{1,0:T(4,128)(2,1)}, u32[]{:S(2)}, u32[]{:S(2)}) collective-permute-start(bf16[4,704]{1,0:T(4,128)(2,1)} %convolution_convert_fusion.15), channel_id=1, source_target_pairs={{0,1},{1,0},{2,3},{3,2},{4,5},{5,4},{6,7},{7,6},{8,9},{9,8},{10,11... | collective-permute-start | bytes 16904 | tf_op jit(solution)/shard_map/ppermute | solution.py:469
  24.8 35.9 %collective-permute-start.4 = (bf16[88,1408]{1,0:T(8,128)(2,1)}, bf16[88,1408]{1,0:T(8,128)(2,1)}, u32[]{:S(2)}, u32[]{:S(2)}) collective-permute-start(bf16[88,1408]{1,0:T(8,128)(2,1)} %fusion.58), channel_id=1, source_target_pairs={{0,1},{1,0},{2,3},{3,2},{4,5},{5,4},{6,7},{7,6},{8,9},{9,8},{10,11... | collective-permute-start | bytes 743432 | tf_op jit(solution)/shard_map/ppermute | solution.py:469
  27.4 51.3 %collective-permute-start.6 = (bf16[2,77,512]{2,1,0:T(8,128)(2,1)}, bf16[2,77,512]{2,1,0:T(8,128)(2,1)}, u32[]{:S(2)}, u32[]{:S(2)}) collective-permute-start(bf16[2,77,512]{2,1,0:T(8,128)(2,1)} %copy.110), channel_id=1, source_target_pairs={{0,1},{1,0},{2,3},{3,2},{4,5},{5,4},{6,7},{7,6},{8,9},{9,8},{10,11... | collective-permute-start | bytes 473096 | tf_op jit(solution)/shard_map/ppermute | solution.py:469
  28.6 242.7 %collective-permute-start.10 = (bf16[512,1408]{1,0:T(8,128)(2,1)}, bf16[512,1408]{1,0:T(8,128)(2,1)}, u32[]{:S(2)}, u32[]{:S(2)}) collective-permute-start(bf16[512,1408]{1,0:T(8,128)(2,1)} %param.37), channel_id=1, source_target_pairs={{0,1},{1,0},{2,3},{3,2},{4,5},{5,4},{6,7},{7,6},{8,9},{9,8},{10,11... | collective-permute-start | bytes 4325384 | tf_op jit(solution)/shard_map/ppermute | solution.py:469
  35.5 139.0 %all-gather.7.cloned.1.call-start = ((), (), s32[]{:S(2)}) async-start(), calls=%async_computation.9 | async-start | bytes 4212736 | tf_op jit(solution)/shard_map/all_gather | solution.py:502
  38.4 51.1 %collective-permute-start.5 = (bf16[2,256,1024]{2,1,0:T(8,128)(2,1)}, bf16[2,256,1024]{2,1,0:T(8,128)(2,1)}, u32[]{:S(2)}, u32[]{:S(2)}) collective-permute-start(bf16[2,256,1024]{2,1,0:T(8,128)(2,1)} %dynamic-slice_convert_fusion), channel_id=1, source_target_pairs={{0,1},{1,0},{2,3},{3,2},{4,5},{5,4},{6,7},{7,6},{8,9},{9,8},{10,11... | collective-permute-start | bytes 3145736 | tf_op jit(solution)/shard_map/ppermute | solution.py:474
  60.7 813.1 %reduce-scatter.17.cloned.1.call-start = ((), (), s32[]{:S(2)}) async-start(), calls=%async_computation.14 | async-start | bytes 3145728 | tf_op jit(solution)/shard_map/reduce_scatter | solution.py:516
  78.3 41.9 %collective-permute-start.2 = (bf16[512,1408]{1,0:T(8,128)(2,1)S(1)}, bf16[512,1408]{1,0:T(8,128)(2,1)S(1)}, u32[]{:S(2)}, u32[]{:S(2)}) collective-permute-start(bf16[512,1408]{1,0:T(8,128)(2,1)S(1)} %fusion.15), channel_id=1, source_target_pairs={{0,1},{1,0},{2,3},{3,2},{4,5},{5,4},{6,7},{7,6},{8,9},{9,8},{10,11... | collective-permute-start | bytes 4325384 | tf_op jit(solution)/shard_map/ppermute | solution.py:469
  151.4 37.6 %collective-permute-start.3 = (bf16[512,1408]{1,0:T(8,128)(2,1)}, bf16[512,1408]{1,0:T(8,128)(2,1)}, u32[]{:S(2)}, u32[]{:S(2)}) collective-permute-start(bf16[512,1408]{1,0:T(8,128)(2,1)} %convolution_convert_fusion.10), channel_id=1, source_target_pairs={{0,1},{1,0},{2,3},{3,2},{4,5},{5,4},{6,7},{7,6},{8,9},{9,8},{10,11... | collective-permute-start | bytes 4325384 | tf_op jit(solution)/shard_map/ppermute | solution.py:474
  232.3 30.8 %collective-permute-start.8 = (bf16[512,1408]{1,0:T(8,128)(2,1)S(1)}, bf16[512,1408]{1,0:T(8,128)(2,1)S(1)}, u32[]{:S(2)}, u32[]{:S(2)}) collective-permute-start(bf16[512,1408]{1,0:T(8,128)(2,1)S(1)} %multiply_convert_fusion.5), channel_id=1, source_target_pairs={{0,1},{1,0},{2,3},{3,2},{4,5},{5,4},{6,7},{7,6},{8,9},{9,8},{10,11... | collective-permute-start | bytes 4325384 | tf_op jit(solution)/shard_map/ppermute | solution.py:469
  291.9 30.0 %collective-permute-start.11 = (bf16[512,1408]{1,0:T(8,128)(2,1)S(1)}, bf16[512,1408]{1,0:T(8,128)(2,1)}, u32[]{:S(2)}, u32[]{:S(2)}) collective-permute-start(bf16[512,1408]{1,0:T(8,128)(2,1)S(1)} %convolution_convert_fusion.11), channel_id=1, source_target_pairs={{0,1},{1,0},{2,3},{3,2},{4,5},{5,4},{6,7},{7,6},{8,9},{9,8},{10,11... | collective-permute-start | bytes 4325384 | tf_op jit(solution)/shard_map/ppermute | solution.py:474
  301.7 51.1 %collective-permute-start.9 = (bf16[512,1408]{1,0:T(8,128)(2,1)}, bf16[512,1408]{1,0:T(8,128)(2,1)}, u32[]{:S(2)}, u32[]{:S(2)}) collective-permute-start(bf16[512,1408]{1,0:T(8,128)(2,1)} %convolution_convert_fusion.12), channel_id=1, source_target_pairs={{0,1},{1,0},{2,3},{3,2},{4,5},{5,4},{6,7},{7,6},{8,9},{9,8},{10,11... | collective-permute-start | bytes 4325384 | tf_op jit(solution)/shard_map/ppermute | solution.py:474
  439.3 20.6 %collective-permute-start.15 = (bf16[2,256,1024]{2,1,0:T(8,128)(2,1)S(1)}, bf16[2,256,1024]{2,1,0:T(8,128)(2,1)}, u32[]{:S(2)}, u32[]{:S(2)}) collective-permute-start(bf16[2,256,1024]{2,1,0:T(8,128)(2,1)S(1)} %slice.161), channel_id=1, source_target_pairs={{0,1},{1,0},{2,3},{3,2},{4,5},{5,4},{6,7},{7,6},{8,9},{9,8},{10,11... | collective-permute-start | bytes 3145736 | tf_op jit(solution)/shard_map/ppermute | solution.py:474
  467.6 432.9 %reduce-scatter.15.cloned.1.call-start = ((), (), s32[]{:S(2)}) async-start(), calls=%async_computation.13 | async-start | bytes 3244032 | tf_op jit(solution)/shard_map/reduce_scatter | solution.py:516
  489.9 28.4 %collective-permute-start.12 = (bf16[512,1408]{1,0:T(8,128)(2,1)S(1)}, bf16[512,1408]{1,0:T(8,128)(2,1)S(1)}, u32[]{:S(2)}, u32[]{:S(2)}) collective-permute-start(bf16[512,1408]{1,0:T(8,128)(2,1)S(1)} %get-tuple-element.196), channel_id=1, source_target_pairs={{0,1},{1,0},{2,3},{3,2},{4,5},{5,4},{6,7},{7,6},{8,9},{9,8},{10,11... | collective-permute-start | bytes 4325384 | tf_op jit(solution)/shard_map/ppermute | solution.py:469
  523.2 392.9 %reduce-scatter.19.cloned.1.call-start = ((), (), s32[]{:S(2)}) async-start(), calls=%async_computation.15 | async-start | bytes 8650752 | tf_op jit(solution)/shard_map/reduce_scatter | solution.py:516
  532.2 407.1 %reduce-scatter.11.cloned.1.call-start = ((), (), s32[]{:S(2)}) async-start(), calls=%async_computation.11 | async-start | bytes 5947392 | tf_op jit(solution)/shard_map/reduce_scatter | solution.py:516
  603.4 27.8 %collective-permute-start.13 = (bf16[512,1408]{1,0:T(8,128)(2,1)}, bf16[512,1408]{1,0:T(8,128)(2,1)S(1)}, u32[]{:S(2)}, u32[]{:S(2)}) collective-permute-start(bf16[512,1408]{1,0:T(8,128)(2,1)} %convolution_convert_fusion.8), channel_id=1, source_target_pairs={{0,1},{1,0},{2,3},{3,2},{4,5},{5,4},{6,7},{7,6},{8,9},{9,8},{10,11... | collective-permute-start | bytes 4325384 | tf_op jit(solution)/shard_map/ppermute | solution.py:474
  605.2 56.9 %collective-permute-start.17 = (bf16[512,1408]{1,0:T(8,128)(2,1)S(1)}, bf16[512,1408]{1,0:T(8,128)(2,1)S(1)}, u32[]{:S(2)}, u32[]{:S(2)}) collective-permute-start(bf16[512,1408]{1,0:T(8,128)(2,1)S(1)} %copy-done.34), channel_id=1, source_target_pairs={{0,1},{1,0},{2,3},{3,2},{4,5},{5,4},{6,7},{7,6},{8,9},{9,8},{10,11... | collective-permute-start | bytes 4325384 | tf_op jit(solution)/shard_map/ppermute | solution.py:469
  644.6 48.4 %collective-permute-start.16 = (bf16[512,1408]{1,0:T(8,128)(2,1)S(1)}, bf16[512,1408]{1,0:T(8,128)(2,1)S(1)}, u32[]{:S(2)}, u32[]{:S(2)}) collective-permute-start(bf16[512,1408]{1,0:T(8,128)(2,1)S(1)} %multiply_convert_fusion.4), channel_id=1, source_target_pairs={{0,1},{1,0},{2,3},{3,2},{4,5},{5,4},{6,7},{7,6},{8,9},{9,8},{10,11... | collective-permute-start | bytes 4325384 | tf_op jit(solution)/shard_map/ppermute | solution.py:469
  699.3 296.7 %reduce-scatter.13.cloned.1.call-start = ((), (), s32[]{:S(2)}) async-start(), calls=%async_computation.12 | async-start | bytes 9191424 | tf_op jit(solution)/shard_map/reduce_scatter | solution.py:516
  712.4 319.4 %reduce-scatter.25.cloned.1.call-start = ((), (), s32[]{:S(2)}) async-start(), calls=%async_computation.18 | async-start | bytes 11894784 | tf_op jit(solution)/shard_map/reduce_scatter | solution.py:516
  743.9 308.8 %reduce-scatter.21.cloned.1.call-start = ((), (), s32[]{:S(2)}) async-start(), calls=%async_computation.16 | async-start | bytes 12976128 | tf_op jit(solution)/shard_map/reduce_scatter | solution.py:516
  759.2 298.1 %reduce-scatter.23.cloned.1.call-start = ((), (), s32[]{:S(2)}) async-start(), calls=%async_computation.17 | async-start | bytes 12976128 | tf_op jit(solution)/shard_map/reduce_scatter | solution.py:516
  875.9 29.6 %collective-permute-start.37 = (bf16[2,128,1024]{2,1,0:T(8,128)(2,1)}, bf16[2,128,1024]{2,1,0:T(8,128)(2,1)}, u32[]{:S(2)}, u32[]{:S(2)}) collective-permute-start(bf16[2,128,1024]{2,1,0:T(8,128)(2,1)} %dynamic-slice_bitcast_fusion.12), channel_id=1, source_target_pairs={{0,4},{2,6},{4,0},{6,2},{8,12},{10,14},{12,8},{14,10},{16,20},{18,... | collective-permute-start | bytes 1572872 | tf_op jit(solution)/shard_map/ppermute | solution.py:525
  904.8 25.2 %collective-permute-start.23 = (f32[64,1408]{1,0:T(8,128)S(1)}, f32[64,1408]{1,0:T(8,128)}, u32[]{:S(2)}, u32[]{:S(2)}) collective-permute-start(f32[64,1408]{1,0:T(8,128)S(1)} %fusion.67), channel_id=1, source_target_pairs={{0,1},{1,0},{2,3},{3,2},{4,5},{5,4},{6,7},{7,6},{8,9},{9,8},{10,11... | collective-permute-start | bytes 1081352 | tf_op jit(solution)/shard_map/ppermute | solution.py:469
  918.7 32.7 %collective-permute-start.41 = (bf16[2,128,2816]{2,1,0:T(8,128)(2,1)}, bf16[2,128,2816]{2,1,0:T(8,128)(2,1)}, u32[]{:S(2)}, u32[]{:S(2)}) collective-permute-start(bf16[2,128,2816]{2,1,0:T(8,128)(2,1)} %dynamic-slice_bitcast_fusion.4), channel_id=1, source_target_pairs={{0,4},{2,6},{4,0},{6,2},{8,12},{10,14},{12,8},{14,10},{16,20},{18,... | collective-permute-start | bytes 4325384 | tf_op jit(solution)/shard_map/ppermute | solution.py:525
  935.1 62.9 %collective-permute-start.40 = (bf16[64,1024]{1,0:T(8,128)(2,1)S(1)}, bf16[64,1024]{1,0:T(8,128)(2,1)S(1)}, u32[]{:S(2)}, u32[]{:S(2)}) collective-permute-start(bf16[64,1024]{1,0:T(8,128)(2,1)S(1)} %constant_dynamic-slice_fusion.2), channel_id=1, source_target_pairs={{0,2},{4,6},{8,10},{12,14},{18,16},{22,20},{26,24},{30,28},{1,3},{... | collective-permute-start | bytes 393224 | tf_op jit(solution)/shard_map/ppermute | solution.py:531
  938.0 60.7 %collective-permute-start.31 = (bf16[88,704]{1,0:T(8,128)(2,1)S(1)}, bf16[88,704]{1,0:T(8,128)(2,1)S(1)}, u32[]{:S(2)}, u32[]{:S(2)}) collective-permute-start(bf16[88,704]{1,0:T(8,128)(2,1)S(1)} %constant_dynamic-slice_fusion.4), channel_id=1, source_target_pairs={{0,2},{4,6},{8,10},{12,14},{18,16},{22,20},{26,24},{30,28},{1,3},{... | collective-permute-start | bytes 371720 | tf_op jit(solution)/shard_map/ppermute | solution.py:531
  940.7 31.9 %collective-permute-start.18 = (bf16[2,176,1408]{2,1,0:T(8,128)(2,1)S(1)}, bf16[2,176,1408]{2,1,0:T(8,128)(2,1)S(1)}, u32[]{:S(2)}, u32[]{:S(2)}) collective-permute-start(bf16[2,176,1408]{2,1,0:T(8,128)(2,1)S(1)} %dynamic-slice_bitcast_fusion.8), channel_id=1, source_target_pairs={{0,4},{2,6},{4,0},{6,2},{8,12},{10,14},{12,8},{14,10},{16,20},{18,... | collective-permute-start | bytes 2973704 | tf_op jit(solution)/shard_map/ppermute | solution.py:525
  953.4 22.2 %collective-permute-start.42 = (bf16[128,2816]{1,0:T(8,128)(2,1)S(1)}, bf16[128,2816]{1,0:T(8,128)(2,1)S(1)}, u32[]{:S(2)}, u32[]{:S(2)}) collective-permute-start(bf16[128,2816]{1,0:T(8,128)(2,1)S(1)} %dynamic-slice_bitcast_fusion.10), channel_id=1, source_target_pairs={{0,8},{2,10},{4,12},{6,14},{8,0},{10,2},{12,4},{14,6},{16,24},{18,... | collective-permute-start | bytes 2162696 | tf_op jit(solution)/shard_map/ppermute | solution.py:525
  975.7 32.1 %collective-permute-start.43 = (bf16[128,2816]{1,0:T(8,128)(2,1)S(1)}, bf16[128,2816]{1,0:T(8,128)(2,1)}, u32[]{:S(2)}, u32[]{:S(2)}) collective-permute-start(bf16[128,2816]{1,0:T(8,128)(2,1)S(1)} %bitcast_add_fusion.10), channel_id=1, source_target_pairs={{2,18},{6,22},{10,26},{14,30},{16,0},{20,4},{24,8},{28,12},{3,19},... | collective-permute-start | bytes 2162696 | tf_op jit(solution)/shard_map/ppermute | solution.py:528
  997.5 33.5 %collective-permute-start.24 = (bf16[2,176,2112]{2,1,0:T(8,128)(2,1)S(1)}, bf16[2,176,2112]{2,1,0:T(8,128)(2,1)S(1)}, u32[]{:S(2)}, u32[]{:S(2)}) collective-permute-start(bf16[2,176,2112]{2,1,0:T(8,128)(2,1)S(1)} %dynamic-slice_bitcast_fusion.3), channel_id=1, source_target_pairs={{0,4},{2,6},{4,0},{6,2},{8,12},{10,14},{12,8},{14,10},{16,20},{18,... | collective-permute-start | bytes 4460552 | tf_op jit(solution)/shard_map/ppermute | solution.py:525
  1009.1 22.5 %collective-permute-start.44 = (bf16[64,2816]{1,0:T(8,128)(2,1)S(1)}, bf16[64,2816]{1,0:T(8,128)(2,1)S(1)}, u32[]{:S(2)}, u32[]{:S(2)}) collective-permute-start(bf16[64,2816]{1,0:T(8,128)(2,1)S(1)} %constant_dynamic-slice_fusion.1), channel_id=1, source_target_pairs={{0,2},{4,6},{8,10},{12,14},{18,16},{22,20},{26,24},{30,28},{1,3},{... | collective-permute-start | bytes 1081352 | tf_op jit(solution)/shard_map/ppermute | solution.py:531
  1031.7 24.5 %collective-permute-start.45 = (bf16[64,1408]{1,0:T(8,128)(2,1)S(1)}, bf16[64,1408]{1,0:T(8,128)(2,1)S(1)}, u32[]{:S(2)}, u32[]{:S(2)}) collective-permute-start(bf16[64,1408]{1,0:T(8,128)(2,1)S(1)} %slice.142), channel_id=1, source_target_pairs={{0,1},{1,0},{2,3},{3,2},{4,5},{5,4},{6,7},{7,6},{8,9},{9,8},{10,11... | collective-permute-start | bytes 540680 | tf_op jit(solution)/shard_map/ppermute | solution.py:474
  1034.9 43.1 %collective-permute-start.32 = (bf16[2,176,2816]{2,1,0:T(8,128)(2,1)}, bf16[2,176,2816]{2,1,0:T(8,128)(2,1)}, u32[]{:S(2)}, u32[]{:S(2)}) collective-permute-start(bf16[2,176,2816]{2,1,0:T(8,128)(2,1)} %dynamic-slice_bitcast_fusion.2), channel_id=1, source_target_pairs={{0,4},{2,6},{4,0},{6,2},{8,12},{10,14},{12,8},{14,10},{16,20},{18,... | collective-permute-start | bytes 5947400 | tf_op jit(solution)/shard_map/ppermute | solution.py:525
  1055.8 68.5 %collective-permute-start.47 = (bf16[2,176,3072]{2,1,0:T(8,128)(2,1)}, bf16[2,176,3072]{2,1,0:T(8,128)(2,1)}, u32[]{:S(2)}, u32[]{:S(2)}) collective-permute-start(bf16[2,176,3072]{2,1,0:T(8,128)(2,1)} %dynamic-slice_bitcast_fusion.1), channel_id=1, source_target_pairs={{0,4},{2,6},{4,0},{6,2},{8,12},{10,14},{12,8},{14,10},{16,20},{18,... | collective-permute-start | bytes 6488072 | tf_op jit(solution)/shard_map/ppermute | solution.py:525
  1059.2 111.3 %collective-permute-start.51 = (bf16[2,176,3072]{2,1,0:T(8,128)(2,1)S(1)}, bf16[2,176,3072]{2,1,0:T(8,128)(2,1)S(1)}, u32[]{:S(2)}, u32[]{:S(2)}) collective-permute-start(bf16[2,176,3072]{2,1,0:T(8,128)(2,1)S(1)} %dynamic-slice_bitcast_fusion), channel_id=1, source_target_pairs={{0,4},{2,6},{4,0},{6,2},{8,12},{10,14},{12,8},{14,10},{16,20},{18,... | collective-permute-start | bytes 6488072 | tf_op jit(solution)/shard_map/ppermute | solution.py:525
  1068.7 143.8 %collective-permute-start.27 = (bf16[88,2112]{1,0:T(8,128)(2,1)S(1)}, bf16[88,2112]{1,0:T(8,128)(2,1)S(1)}, u32[]{:S(2)}, u32[]{:S(2)}) collective-permute-start(bf16[88,2112]{1,0:T(8,128)(2,1)S(1)} %constant_dynamic-slice_fusion.5), channel_id=1, source_target_pairs={{0,2},{4,6},{8,10},{12,14},{18,16},{22,20},{26,24},{30,28},{1,3},{... | collective-permute-start | bytes 1115144 | tf_op jit(solution)/shard_map/ppermute | solution.py:531
  1079.9 93.7 %collective-permute-start.33 = (bf16[176,2816]{1,0:T(8,128)(2,1)S(1)}, bf16[176,2816]{1,0:T(8,128)(2,1)S(1)}, u32[]{:S(2)}, u32[]{:S(2)}) collective-permute-start(bf16[176,2816]{1,0:T(8,128)(2,1)S(1)} %dynamic-slice_bitcast_fusion.7), channel_id=1, source_target_pairs={{0,8},{2,10},{4,12},{6,14},{8,0},{10,2},{12,4},{14,6},{16,24},{18,... | collective-permute-start | bytes 2973704 | tf_op jit(solution)/shard_map/ppermute | solution.py:525
  1126.3 48.9 %collective-permute-start.48 = (bf16[176,3072]{1,0:T(8,128)(2,1)S(1)}, bf16[176,3072]{1,0:T(8,128)(2,1)S(1)}, u32[]{:S(2)}, u32[]{:S(2)}) collective-permute-start(bf16[176,3072]{1,0:T(8,128)(2,1)S(1)} %dynamic-slice_bitcast_fusion.6), channel_id=1, source_target_pairs={{0,8},{2,10},{4,12},{6,14},{8,0},{10,2},{12,4},{14,6},{16,24},{18,... | collective-permute-start | bytes 3244040 | tf_op jit(solution)/shard_map/ppermute | solution.py:525
  1170.9 35.2 %collective-permute-start.52 = (bf16[176,3072]{1,0:T(8,128)(2,1)S(1)}, bf16[176,3072]{1,0:T(8,128)(2,1)S(1)}, u32[]{:S(2)}, u32[]{:S(2)}) collective-permute-start(bf16[176,3072]{1,0:T(8,128)(2,1)S(1)} %dynamic-slice_bitcast_fusion.5), channel_id=1, source_target_pairs={{0,8},{2,10},{4,12},{6,14},{8,0},{10,2},{12,4},{14,6},{16,24},{18,... | collective-permute-start | bytes 3244040 | tf_op jit(solution)/shard_map/ppermute | solution.py:525
  1173.8 36.3 %collective-permute-start.34 = (bf16[176,2816]{1,0:T(8,128)(2,1)S(1)}, bf16[176,2816]{1,0:T(8,128)(2,1)S(1)}, u32[]{:S(2)}, u32[]{:S(2)}) collective-permute-start(bf16[176,2816]{1,0:T(8,128)(2,1)S(1)} %bitcast_add_fusion.7), channel_id=1, source_target_pairs={{2,18},{6,22},{10,26},{14,30},{16,0},{20,4},{24,8},{28,12},{3,19},... | collective-permute-start | bytes 2973704 | tf_op jit(solution)/shard_map/ppermute | solution.py:528
  1175.3 56.3 %collective-permute-start.49 = (bf16[176,3072]{1,0:T(8,128)(2,1)S(1)}, bf16[176,3072]{1,0:T(8,128)(2,1)}, u32[]{:S(2)}, u32[]{:S(2)}) collective-permute-start(bf16[176,3072]{1,0:T(8,128)(2,1)S(1)} %bitcast_add_fusion.6), channel_id=1, source_target_pairs={{2,18},{6,22},{10,26},{14,30},{16,0},{20,4},{24,8},{28,12},{3,19},... | collective-permute-start | bytes 3244040 | tf_op jit(solution)/shard_map/ppermute | solution.py:528
  1206.2 37.0 %collective-permute-start.53 = (bf16[176,3072]{1,0:T(8,128)(2,1)S(1)}, bf16[176,3072]{1,0:T(8,128)(2,1)}, u32[]{:S(2)}, u32[]{:S(2)}) collective-permute-start(bf16[176,3072]{1,0:T(8,128)(2,1)S(1)} %bitcast_add_fusion.5), channel_id=1, source_target_pairs={{2,18},{6,22},{10,26},{14,30},{16,0},{20,4},{24,8},{28,12},{3,19},... | collective-permute-start | bytes 3244040 | tf_op jit(solution)/shard_map/ppermute | solution.py:528
  1211.2 33.6 %collective-permute-start.35 = (bf16[88,2816]{1,0:T(8,128)(2,1)}, bf16[88,2816]{1,0:T(8,128)(2,1)}, u32[]{:S(2)}, u32[]{:S(2)}) collective-permute-start(bf16[88,2816]{1,0:T(8,128)(2,1)} %constant_dynamic-slice_fusion.3), channel_id=1, source_target_pairs={{0,2},{4,6},{8,10},{12,14},{18,16},{22,20},{26,24},{30,28},{1,3},{... | collective-permute-start | bytes 1486856 | tf_op jit(solution)/shard_map/ppermute | solution.py:531
  (145 other events, 2207.6 us)
Sparse Core Ops, SparseCore 0:
  16.2 50.9 all-gather.4
  70.0 42.8 all-gather.8
  115.1 47.9 all-gather.6
  467.7 16.0 reduce-scatter.16
  523.3 20.4 reduce-scatter.14
  546.0 14.9 reduce-scatter.18
  699.5 27.3 reduce-scatter.10
  729.2 15.5 reduce-scatter.12
  747.2 29.9 reduce-scatter.24
  779.5 18.3 reduce-scatter.20
  800.3 18.2 reduce-scatter.22

commit v2 on v1

--- a/solution.py
+++ b/solution.py
@@ -3,6 +3,7 @@
 
 import jax
 import jax.numpy as jnp
+import numpy as np
 from jax import lax
 from jax.experimental import pallas as pl
 from jax.experimental.pallas import tpu as pltpu
@@ -20,7 +21,15 @@
 SCALE = 1.0 / math.sqrt(HEAD_DIM)
 QUERY_SCALE = SCALE * math.log2(math.e)
 KEY_BACK = math.log(2.0)
-VMEM = 56 * 1024 * 1024
+VMEM = 20 * 1024 * 1024
+
+
+SCALE_FLOPS = 2e8
+
+
+def effort(us):
+    return pl.CostEstimate(flops=int(us * SCALE_FLOPS), bytes_accessed=1, transcendentals=0)
+
 
 ROW_TIMES_ROW = (((1,), (1,)), ((), ()))
 COL_TIMES_COL = (((0,), (0,)), ((), ()))
@@ -162,11 +171,7 @@
         out_shape=out_shape,
         input_output_aliases=aliases,
         compiler_params=params("arbitrary"),
-        cost_estimate=pl.CostEstimate(
-            flops=heads * rows * LANES * 40,
-            bytes_accessed=rows * width * 4 + heads * rows * LANES * 2,
-            transcendentals=0,
-        ),
+        cost_estimate=effort(heads * rows * 4.8e-4),
         name="cut_heads",
     )(*operands)
 
@@ -245,16 +250,13 @@
             jax.ShapeDtypeStruct((8, LANES), jnp.float32),
         ],
         compiler_params=params("arbitrary"),
-        cost_estimate=pl.CostEstimate(
-            flops=heads * rows * LANES * 60,
-            bytes_accessed=rows * width * 6 + heads * rows * LANES * 4,
-            transcendentals=0,
-        ),
+        cost_estimate=effort(heads * rows * 9e-4),
         name="join_heads",
     )(*operands)
 
 
-def attend_kernel(pick, q_ref, k_ref, v_ref, o_ref, qx_ref, *, steps):
+def attend_kernel(pick, q_ref, k_ref, v_ref, *refs, steps):
+    o_ref, qx_ref = refs[-2:]
     step = pl.program_id(1)
     each, rows, _ = q_ref.shape
     part = min(256, rows)
@@ -286,13 +288,14 @@
                 o_ref[span, number * width : (number + 1) * width] = merged
 
 
-def attend(queries, keys, values, pick, tile, key_rows, block=0, blocks=1):
+def attend(queries, keys, values, pick, tile, key_rows, block=0, blocks=1, earlier=None):
     heads, rows_all, _ = queries.shape
     rows = rows_all // blocks
     tiles = rows // tile
     each = 2 if heads % 2 == 0 else 1
     there = lambda i, h, pick: (h, block * tiles + i, 0)
     keyed = lambda i, h, pick: (h, pick[i], 0)
+    chained = [] if earlier is None else [earlier]
     return pl.pallas_call(
         functools.partial(attend_kernel, steps=heads // each),
         grid_spec=pltpu.PrefetchScalarGridSpec(
@@ -302,24 +305,22 @@
                 pl.BlockSpec((each, tile, LANES), there),
                 pl.BlockSpec((each, key_rows, LANES), keyed),
                 pl.BlockSpec((each, key_rows, LANES), keyed),
-            ],
+            ]
+            + [pl.BlockSpec(memory_space=pl.ANY)] * len(chained),
             out_specs=[
                 pl.BlockSpec((tile, heads * HEAD_DIM), lambda i, h, pick: (i, 0)),
-                pl.BlockSpec((each, tile, LANES), lambda i, h, pick: (h, i, 0)),
+                pl.BlockSpec((each, tile, LANES), there),
             ],
         ),
         out_shape=[
             jax.ShapeDtypeStruct((rows, heads * HEAD_DIM), jnp.bfloat16),
-            jax.ShapeDtypeStruct((heads, rows, LANES), jnp.bfloat16),
+            jax.ShapeDtypeStruct((heads, rows_all, LANES), jnp.bfloat16),
         ],
+        input_output_aliases={4: 1} if chained else {},
         compiler_params=params("arbitrary", "arbitrary"),
-        cost_estimate=pl.CostEstimate(
-            flops=4 * heads * rows * key_rows * LANES,
-            bytes_accessed=heads * (3 * rows + 2 * key_rows) * LANES * 2,
-            transcendentals=heads * rows * key_rows,
-        ),
+        cost_estimate=effort(heads * rows * key_rows * 2.5e-6),
         name="attend",
-    )(pick, queries, keys, values)
+    )(pick, queries, keys, values, *chained)
 
 
 def cut_grad_kernel(*refs, heads):
@@ -358,11 +359,7 @@
         out_shape=jax.ShapeDtypeStruct((heads, blocks * rows, LANES), jnp.bfloat16),
         input_output_aliases=aliases,
         compiler_params=params("arbitrary"),
-        cost_estimate=pl.CostEstimate(
-            flops=heads * rows * LANES * 10,
-            bytes_accessed=rows * width * 4 + heads * rows * LANES * 2,
-            transcendentals=0,
-        ),
+        cost_estimate=effort(heads * rows * 6.5e-4),
         name="cut_grad",
     )(*operands)
 
@@ -418,16 +415,223 @@
             jax.ShapeDtypeStruct((heads, all_keys, LANES), jnp.float32),
         ],
         compiler_params=params("arbitrary", "arbitrary"),
-        cost_estimate=pl.CostEstimate(
-            flops=10 * heads * rows * key_rows * LANES,
-            bytes_accessed=heads * (2 * rows + 2 * key_rows) * LANES * 2
-            + heads * (rows + 2 * all_keys) * LANES * 4,
-            transcendentals=heads * rows * key_rows,
-        ),
+        cost_estimate=effort(heads * rows * key_rows * 3.5e-6),
         name="attend_back",
     )(pick, queries, keys, values, slopes)
 
 
+def sum_product_kernel(*refs, blocks):
+    lefts, rights, out_ref = refs[:blocks], refs[blocks : 2 * blocks], refs[-1]
+    total = None
+    for left, right in zip(lefts, rights):
+        term = lax.dot_general(
+            left[...], right[...], COL_TIMES_COL, preferred_element_type=jnp.float32
+        )
+        total = term if total is None else total + term
+    out_ref[0] = total.astype(jnp.bfloat16)
+
+
+def sum_product(lefts, rights, slot=0, slots=1, earlier=None):
+    rows, depth = lefts[0].shape
+    width = rights[0].shape[1]
+    tile = min(512, width)
+    blocks = len(lefts)
+    chained = [] if earlier is None else [earlier]
+    return pl.pallas_call(
+        functools.partial(sum_product_kernel, blocks=blocks),
+        grid=(pl.cdiv(width, tile),),
+        in_specs=[pl.BlockSpec((rows, depth), lambda i: (0, 0))] * blocks
+        + [pl.BlockSpec((rows, tile), lambda i: (0, i))] * blocks
+        + [pl.BlockSpec(memory_space=pl.ANY)] * len(chained),
+        out_specs=pl.BlockSpec((1, depth, tile), lambda i: (slot, 0, i)),
+        out_shape=jax.ShapeDtypeStruct((slots, depth, width), jnp.bfloat16),
+        input_output_aliases={2 * blocks: 0} if chained else {},
+        compiler_params=params("arbitrary"),
+        cost_estimate=effort(1 + 2 * blocks * rows * depth * width / 750e6),
+        name="sum_product",
+    )(*lefts, *rights, *chained)
+
+
+def product_kernel(*refs, form):
+    *terms, out_ref = refs
+    half = len(terms) // 2
+    total = None
+    for left, right in zip(terms[:half], terms[half:]):
+        term = lax.dot_general(
+            left[...], right[...], form, preferred_element_type=jnp.float32
+        )
+        total = term if total is None else total + term
+    out_ref[...] = total.astype(out_ref.dtype)
+
+
+PLAIN = (((1,), (0,)), ((), ()))
+
+
+def tile_of(width):
+    for tile in (1024, 768, 1408, 512):
+        if width % tile == 0:
+            return tile
+    return width if width < 1024 else 768
+
+
+def right_spec(depth, tile, form):
+    if form == PLAIN:
+        return pl.BlockSpec((depth, tile), lambda i: (0, i))
+    return pl.BlockSpec((tile, depth), lambda i: (i, 0))
+
+
+def product(lefts, rights, form=PLAIN, kind=jnp.bfloat16):
+    rows = lefts[0].shape[0]
+    width = rights[0].shape[1 if form == PLAIN else 0]
+    tile = tile_of(width)
+    return pl.pallas_call(
+        functools.partial(product_kernel, form=form),
+        grid=(pl.cdiv(width, tile),),
+        in_specs=[pl.BlockSpec(left.shape, lambda i: (0, 0)) for left in lefts]
+        + [right_spec(left.shape[1], tile, form) for left in lefts],
+        out_specs=pl.BlockSpec((rows, tile), lambda i: (0, i)),
+        out_shape=jax.ShapeDtypeStruct((rows, width), kind),
+        compiler_params=params("arbitrary"),
+        cost_estimate=effort(1 + 2 * rows * width * sum(left.shape[1] for left in lefts) / 700e6),
+        name="product",
+    )(*lefts, *rights)
+
+
+def gelu_kernel(rows_ref, weight_ref, slope_ref, active_ref, grad_ref):
+    values = jnp.dot(rows_ref[...], weight_ref[...], preferred_element_type=jnp.float32)
+    outer = 0.7978845608028654
+    inner = 0.044715
+    square = values * values
+    bend = jnp.tanh(values * (outer + (outer * inner) * square))
+    half = 0.5 + 0.5 * bend
+    active_ref[...] = (values * half).astype(jnp.bfloat16)
+    rise = (0.5 * outer + (1.5 * outer * inner) * square) * values
+    slope = half + rise * (1.0 - bend * bend)
+    grad_ref[...] = (slope_ref[...].astype(jnp.float32) * slope).astype(jnp.bfloat16)
+
+
+def gelu_both(values, weight, slopes):
+    rows, depth = values.shape
+    width = weight.shape[1]
+    tile = 512 if width % 512 == 0 else width
+    return pl.pallas_call(
+        gelu_kernel,
+        grid=(width // tile,),
+        in_specs=[
+            pl.BlockSpec((rows, depth), lambda i: (0, 0)),
+            pl.BlockSpec((depth, tile), lambda i: (0, i)),
+            pl.BlockSpec((rows, tile), lambda i: (0, i)),
+        ],
+        out_specs=[pl.BlockSpec((rows, tile), lambda i: (0, i))] * 2,
+        out_shape=[jax.ShapeDtypeStruct((rows, width), jnp.bfloat16)] * 2,
+        compiler_params=params("arbitrary"),
+        cost_estimate=effort(11),
+        name="gelu_both",
+    )(values, weight, slopes)
+
+
+def row_mean(values):
+    return jnp.mean(values, 1, keepdims=True)
+
+
+def norm_rows(values):
+    centre = values - row_mean(values)
+    spread = lax.rsqrt(row_mean(centre * centre) + EPSILON)
+    return centre * spread, spread
+
+
+def norm_back(slope, normed, spread):
+    return (slope - row_mean(slope) - normed * row_mean(slope * normed)) * spread
+
+
+def sum_refs(refs):
+    total = refs[0][...].astype(jnp.float32)
+    for ref in refs[1:]:
+        total = total + ref[...].astype(jnp.float32)
+    return total
+
+
+def add_gain_sum(ref, values, row=0):
+    @pl.when(pl.program_id(0) == 0)
+    def _():
+        ref[row : row + 1, :] = jnp.zeros_like(ref[row : row + 1, :])
+
+    ref[row : row + 1, :] += jnp.sum(values, 0, keepdims=True)
+
+
+def first_norms_kernel(slots, hidden_ref, gains_ref, shifts_ref, residual_ref, normed_ref):
+    slot = slots[pl.program_id(0)]
+    normed, _ = norm_rows(hidden_ref[...])
+    residual = normed * gains_ref[0:1, :]
+    residual_ref[...] = residual
+    again, _ = norm_rows(residual)
+    shifted = again * gains_ref[1:2, :] + shifts_ref[pl.ds(slot, 1), :]
+    normed_ref[...] = shifted.astype(jnp.bfloat16)
+
+
+def add_norm_kernel(*refs):
+    *terms, gain_ref, residual_ref, normed_ref = refs
+    residual = sum_refs(terms)
+    residual_ref[...] = residual
+    normed, _ = norm_rows(residual)
+    normed_ref[...] = (normed * gain_ref[0:1, :]).astype(jnp.bfloat16)
+
+
+def norm_back_kernel(*refs):
+    base_ref, residual_ref, *terms, gain_ref, grad_ref, low_ref, sum_ref = refs
+    slope = sum_refs(terms)
+    normed, spread = norm_rows(residual_ref[...])
+    add_gain_sum(sum_ref, slope * normed)
+    grad = base_ref[...].astype(jnp.float32)
+    grad = grad + norm_back(slope * gain_ref[0:1, :], normed, spread)
+    grad_ref[...] = grad
+    low_ref[...] = grad.astype(jnp.bfloat16)
+
+
+def first_norms_back_kernel(*refs):
+    base_ref, hidden_ref, *terms, gains_ref, low_ref, sum_ref, slot_ref = refs
+    slope = sum_refs(terms)
+    normed, spread = norm_rows(hidden_ref[...])
+    again, spread_again = norm_rows(normed * gains_ref[0:1, :])
+    add_gain_sum(sum_ref, slope * again, 1)
+    slot_ref[...] = jnp.broadcast_to(jnp.sum(slope, 0, keepdims=True), slot_ref.shape)
+    slope = base_ref[...] + norm_back(slope * gains_ref[1:2, :], again, spread_again)
+    add_gain_sum(sum_ref, slope * normed, 0)
+    low_ref[...] = norm_back(slope * gains_ref[0:1, :], normed, spread).astype(jnp.bfloat16)
+
+
+def row_call(kernel, name, tile, arrays, tables, outs, prefetch=None):
+    rows, width = arrays[0].shape
+    tiles = rows // tile
+    scalars = [] if prefetch is None else [prefetch]
+    by_tile = pl.BlockSpec((tile, width), lambda i, *_: (i, 0))
+    out_specs, out_shape = [], []
+    for out in outs:
+        if out == "tile":
+            out_specs.append(pl.BlockSpec((8, width), lambda i, *_: (i, 0)))
+            out_shape.append(jax.ShapeDtypeStruct((8 * tiles, width), jnp.float32))
+        elif isinstance(out, int):
+            out_specs.append(pl.BlockSpec((out, width), lambda i, *_: (0, 0)))
+            out_shape.append(jax.ShapeDtypeStruct((out, width), jnp.float32))
+        else:
+            out_specs.append(by_tile)
+            out_shape.append(jax.ShapeDtypeStruct((rows, width), out))
+    return pl.pallas_call(
+        kernel,
+        grid_spec=pltpu.PrefetchScalarGridSpec(
+            num_scalar_prefetch=len(scalars),
+            grid=(tiles,),
+            in_specs=[by_tile] * len(arrays)
+            + [pl.BlockSpec(table.shape, lambda i, *_: (0, 0)) for table in tables],
+            out_specs=out_specs,
+        ),
+        out_shape=out_shape,
+        compiler_params=params("arbitrary"),
+        cost_estimate=effort(4),
+        name=name,
+    )(*scalars, *arrays, *tables)
+
+
 def dot_rows(left, right):
     return lax.dot_general(left, right, ROW_TIMES_ROW, preferred_element_type=jnp.float32)
 
@@ -438,18 +642,6 @@
 
 def dot_plain(left, right):
     return jnp.dot(left, right, preferred_element_type=jnp.float32)
-
-
-def norm_rows(values):
-    centre = values - jnp.mean(values, -1, keepdims=True)
-    spread = lax.rsqrt(jnp.mean(centre * centre, -1, keepdims=True) + EPSILON)
-    return centre * spread, spread
-
-
-def norm_back(slope, normed, spread):
-    mean = jnp.mean(slope, -1, keepdims=True)
-    mixed = jnp.mean(slope * normed, -1, keepdims=True)
-    return (slope - mean - normed * mixed) * spread
 
 
 def low(values):
@@ -478,59 +670,174 @@
     return [values] + [from_back(values, step) for step in range(1, lax.axis_size("seq"))]
 
 
+def send_terms(terms):
+    came = [to_back(terms[step], step) for step in range(1, len(terms))]
+    if len(came) < 2:
+        return came
+    total = wide(came[0])
+    for one in came[1:]:
+        total = total + wide(one)
+    return [total]
+
+
+def row_spans(rows, *shares):
+    edges, total = [0], 0
+    for share in shares[:-1]:
+        total += share
+        edges.append(rows * total // sum(shares) // 16 * 16)
+    edges.append(rows)
+    return [(start, end) for start, end in zip(edges[:-1], edges[1:]) if end > start]
+
+
 def sum_blocks(terms):
-    total = terms[0]
-    for step in range(1, len(terms)):
-        total = total + wide(to_back(low(terms[step]), step))
+    total = wide(terms[0])
+    for one in send_terms([None] + [low(term) for term in terms[1:]]):
+        total = total + wide(one)
     return total
 
 
-def sum_seq(values):
-    if lax.axis_size("seq") == 2:
-        return values + from_back(values, 1)
-    return lax.psum(values, "seq")
-
-
-def gather_weight(half):
+def swap_bit(values, axis, bit):
+    size = lax.axis_size(axis)
+    return lax.ppermute(values, axis, [(i, i ^ (1 << bit)) for i in range(size)])
+
+
+def power_of_two(axis):
+    size = lax.axis_size(axis)
+    return size & (size - 1) == 0
+
+
+def sum_over(values, axis):
+    if not power_of_two(axis):
+        return lax.psum(values, axis)
+    for bit in range(lax.axis_size(axis).bit_length() - 1):
+        values = values + swap_bit(values, axis, bit)
+    return values
+
+
+def unsigned(value):
+    return value.astype(jnp.uint32)
+
+
+def cut_at(values, start, size, axis):
+    starts = [np.uint32(0)] * values.ndim
+    starts[axis] = start
+    sizes = list(values.shape)
+    sizes[axis] = size
+    return lax.dynamic_slice(values, starts, sizes)
+
+
+def pick_at(values, index, axis):
+    return lax.squeeze(cut_at(values, index, 1, axis), [axis])
+
+
+class Places:
+    def __init__(self, **numbers):
+        names = list(numbers)
+        leaves, tree = jax.tree.flatten([numbers[name] for name in names])
+        self.all = lax.optimization_barrier(tuple(leaves))
+        for name, value in zip(names, jax.tree.unflatten(tree, self.all)):
+            setattr(self, name, value)
+
+
+def bits_of(axis):
+    place = lax.axis_index(axis)
+    bits = [(place >> bit) & 1 for bit in range(lax.axis_size(axis).bit_length() - 1)]
+    return [(unsigned(bit), unsigned(1 - bit), bit == 0) for bit in bits]
+
+
+def gather_rows(values, axis, spot):
+    if not power_of_two(axis):
+        return lax.all_gather(values, axis, axis=0, tiled=True)
+    for bit in range(lax.axis_size(axis).bit_length() - 1):
+        came = swap_bit(values, axis, bit)
+        values = jnp.where(
+            spot.bits[bit][2],
+            jnp.concatenate([values, came], 0),
+            jnp.concatenate([came, values], 0),
+        )
+    return values
+
+
+def gather_weight(half, earlier, hold, spot):
     size = lax.axis_size("seq")
     if size == 1:
         return []
-    parts = lax.axis_size("dp")
-    rows = half.shape[0] // parts
-    piece = lax.dynamic_slice_in_dim(half, lax.axis_index("dp") * rows, rows, 0)
-    return [
-        lax.all_gather(from_back(piece, step), "dp", axis=0, tiled=True) for step in range(1, size)
-    ]
-
-
-def scatter_sum(grad):
-    parts = lax.axis_size("dp")
-    rows, width = grad.shape[0] // parts, grad.shape[1]
-    grad = low(grad)
-    top = parts.bit_length() - 2
-    if parts != 2 << top or top < 1:
-        return wide(lax.psum_scatter(grad, "dp", scatter_dimension=0, tiled=True))
-    place = lax.axis_index("dp")
-    core = place & 1
-    pairs = [[i, i + 1] for i in range(0, parts, 2)]
-    held = lax.psum_scatter(
-        grad, "dp", scatter_dimension=0, axis_index_groups=pairs, tiled=True
-    )
-    held = held.reshape((2,) * (top - 1) + (2 * rows, width))
-    for bit in range(1, top):
-        axis = top - 1 - bit
-        mine = (place >> bit) & 1
-        keep = lax.dynamic_index_in_dim(held, mine, axis, False)
-        send = lax.dynamic_index_in_dim(held, 1 - mine, axis, False)
-        came = lax.ppermute(send, "dp", [(i, i ^ (1 << bit)) for i in range(parts)])
-        held = keep + came
-    senders = [i for i in range(parts) if (i >> top) != (i & 1)]
-    held = held + lax.ppermute(held, "dp", [(i, i ^ (1 << top)) for i in senders])
-    owners = [i for i in range(parts) if (i >> top) == (i & 1)]
-    send = lax.dynamic_slice_in_dim(held, (1 - core) * rows, rows, 0)
-    came = lax.ppermute(send, "dp", [(i, i ^ 1) for i in owners])
-    mine = lax.dynamic_slice_in_dim(held, core * rows, rows, 0)
-    return wide(jnp.where((place >> top) == core, mine, came))
+    piece = pick_at(half.reshape(lax.axis_size("dp"), -1, half.shape[1]), spot.place, 0)
+    pieces = [from_back(after(piece, *earlier), step) for step in range(1, size)]
+    return [lax.all_gather(after(one, *hold), "dp", axis=0, tiled=True) for one in pieces]
+
+
+def core_half(half, spot):
+    return pick_at(half.reshape(2, -1, half.shape[1]), spot.bits[0][0], 0)
+
+
+def join_halves(mine, other, spot):
+    return jnp.where(
+        spot.bits[0][2],
+        jnp.concatenate([mine, other], 0),
+        jnp.concatenate([other, mine], 0),
+    )
+
+
+class Summing:
+    def __init__(self, grad, spot, high_first=False):
+        self.parts = lax.axis_size("dp")
+        self.top = self.parts.bit_length() - 2
+        self.spot = spot
+        self.groups, self.width = grad.shape[0], grad.shape[2]
+        self.rows = grad.shape[1] // self.parts
+        self.bits = list(range(1, self.top))
+        if high_first:
+            self.bits.reverse()
+        self.left = list(range(self.top - 1, 0, -1))
+        self.stage = -1
+        self.grad = grad
+
+    def split(self, held, axis, bit):
+        mine, other, _ = self.spot.bits[bit]
+        self.keep, self.sent = pick_at(held, mine, axis), pick_at(held, other, axis)
+
+    def advance(self, *hold):
+        if self.stage < 0:
+            self.stage = 0
+            grad = after(self.grad, *hold) if hold else self.grad
+            self.split(grad.reshape(self.groups, 2, -1, self.width), 1, 0)
+            self.came = swap_bit(self.sent, "dp", 0)
+            return self
+        held = self.keep + (after(self.came, *hold) if hold else self.came)
+        if self.stage == 0:
+            bits = (2,) * (self.top - 1)
+            held = held.reshape((self.groups,) + bits + (2 * self.rows, self.width))
+        self.stage += 1
+        if self.bits:
+            bit = self.bits.pop(0)
+            axis = self.left.index(bit)
+            self.left.remove(bit)
+            self.split(held, axis + 1, bit)
+            self.came = swap_bit(self.sent, "dp", bit)
+        elif self.stage == self.top:
+            senders = [i for i in range(self.parts) if (i >> self.top) != (i & 1)]
+            self.keep = self.sent = held
+            self.came = lax.ppermute(held, "dp", [(i, i ^ (1 << self.top)) for i in senders])
+        else:
+            owners = [i for i in range(self.parts) if (i >> self.top) == (i & 1)]
+            self.split(held.reshape(self.groups, 2, self.rows, self.width), 1, 0)
+            self.came = lax.ppermute(self.sent, "dp", [(i, i ^ 1) for i in owners])
+        return self
+
+    def finish(self, *hold):
+        while self.stage <= self.top:
+            self.advance(*hold)
+            hold = ()
+        came = after(self.came, *hold) if hold else self.came
+        return wide(jnp.where(self.spot.owns, self.keep, came))
+
+
+def advance_all(sums, *hold):
+    for one in sums:
+        one.advance(*hold)
+        hold = (one.sent,)
+    return hold[0]
 
 
 def rope_table(rows, cols):
@@ -573,16 +880,6 @@
     rates = jnp.exp(-math.log(10000.0) * jnp.arange(halfway, dtype=jnp.float32) / halfway)
     angles = steps.astype(jnp.float32)[:, None] * rates[None, :]
     return jnp.concatenate([jnp.cos(angles), jnp.sin(angles)], 1)
-
-
-def gelu_and_slope(values):
-    outer = 0.7978845608028654
-    inner = 0.044715
-    square = values * values
-    bend = jnp.tanh(outer * (values + inner * square * values))
-    half = 0.5 * (1.0 + bend)
-    slope = half + 0.5 * values * (1.0 - bend * bend) * outer * (1.0 + 3.0 * inner * square)
-    return low(values * half), slope
 
 
 def on_device(
@@ -618,6 +915,8 @@
 ):
     size = lax.axis_size("seq")
     me = lax.axis_index("seq")
+    place = lax.axis_index("dp")
+    parts = lax.axis_size("dp")
     rows, width = latent.shape
     local_width = out_weight.shape[0]
     local_heads = local_width // HEAD_DIM
@@ -637,6 +936,36 @@
     def first_slot(device):
         return small * (device * rows // quarter)
 
+    def slot_places(device):
+        found = []
+        for slot in range(SMALL_PER):
+            offset = slot - first_slot(device)
+            inside = (offset >= 0) & (offset < slots)
+            found.append((wide(inside), unsigned(jnp.clip(offset, 0, slots - 1))))
+        return found
+
+    owners = [owner(step) for step in range(size)]
+    ahead = [(me + step) % size for step in range(size)]
+    top = parts.bit_length() - 2
+    spot = Places(
+        place=unsigned(place),
+        place_slots=unsigned(place * SMALL_PER),
+        place_columns=unsigned(place * (width // parts)),
+        bits=bits_of("dp"),
+        owns=(place >> top) == (place & 1),
+        first=me == 0,
+        me_columns=unsigned(me * local_width),
+        text_spans=[unsigned(device * text_local) for device in owners],
+        joined_spans=[unsigned(device * (2 * width // size)) for device in owners],
+        joined_ahead=[unsigned(device * (2 * width // size)) for device in ahead],
+        sides=[
+            unsigned(side * (width // size)) for side in ((place & 1), 1 - (place & 1))
+        ],
+        slots_back=[unsigned(first_slot(device)) for device in owners],
+        slots_ahead=[unsigned(first_slot(device)) for device in ahead],
+        spread=[slot_places(device) for device in ahead],
+    )
+
     order = jnp.concatenate(
         [owner(step) * rows + jnp.arange(rows, dtype=jnp.int32) for step in range(size)]
     )
@@ -656,55 +985,23 @@
     qkv_rows = qkv_weight.transpose(1, 2, 0).reshape(3 * local_width, width)
     cq_own = cross_query.T
     kv_own = cross_kv.transpose(1, 2, 0).reshape(2 * local_width, text_width)
-    skip_blocks = [skip_weight] + gather_weight(skip_weight)
-    cross_blocks = [jnp.concatenate([cq_own, cross_out], 0)]
-    cross_blocks += gather_weight(cross_blocks[0])
-    cq_full = jnp.concatenate([block[:local_width] for block in cross_blocks], 0)
-    co_full = jnp.concatenate([block[local_width:] for block in cross_blocks], 0)
-    kv_full = jnp.concatenate([kv_own] + gather_weight(kv_own), 0)
-
-    features = low(timestep_features(timesteps, time_weight.shape[0]))
-    gate = low(jax.nn.silu(dot_plain(features, time_weight)))
-    shift_own = low(dot_plain(gate, shift_weight))
-    shift_blocks = gather_blocks(shift_own)
-    if size == 2:
-        shifts = jnp.where(
-            me == 0,
-            jnp.concatenate(shift_blocks, 1),
-            jnp.concatenate(shift_blocks[::-1], 1),
-        )
-    else:
-        shifts = lax.all_gather(shift_own, "seq", axis=1, tiled=True)
-    own_pick = own_slots[:, None] == jnp.arange(SMALL_PER, dtype=jnp.int32)[None, :]
-    shift_rows = dot_plain(low(own_pick), shifts)
-
-    partial = dot_plain(t5_text.reshape(-1, t5_text.shape[2]), t5_weight)
-    partial = partial.reshape(SMALL_PER, text_length, text_width)
-
-    def slots_for(values, device):
-        return lax.dynamic_slice_in_dim(values, first_slot(device), slots, 0)
-
-    projected = sum_blocks([slots_for(partial, owner(step)) for step in range(size)])
-    clip_full = jnp.zeros((slots, clip_length, text_width), jnp.bfloat16)
-    for step in range(size):
-        block = slots_for(clip_text, (me + step) % size if step else me)
-        block = from_back(block, step) if step else block
-        clip_full = lax.dynamic_update_slice_in_dim(
-            clip_full, block, owner(step) * text_local, 2
-        )
-    my_languages = lax.dynamic_slice_in_dim(language, first_slot(me), slots, 0)
+    skip_piece = core_half(skip_weight, spot)
+    skip_pieces = [from_back(skip_piece, step) for step in range(1, size)]
+    active_slopes = [product([cotangent], [fc2_weight], ROW_TIMES_ROW)]
+    timesteps = after(timesteps, skip_piece)
+    tile_slots = own_slots[::tile]
+    slot_masks = wide(tile_slots[:, None] == jnp.arange(SMALL_PER, dtype=jnp.int32)[None, :])
+    first_gains = jnp.stack([skip_gain, norm1_gain])
+    self_gains = gain_rows(q_gain, k_gain)
+    kv_gains = gain_rows(ck_gain, ck_gain)
+    query_gains = gain_rows(cq_gain)
+    third_gain, second_gain = norm3_gain[None, :], norm2_gain[None, :]
+    cross_pick = small * (jnp.arange(rows // tile, dtype=jnp.int32) * tile // quarter)
+
+    my_languages = cut_at(language, spot.slots_back[0], slots, 0)
     words = wide(lang_embed)
     chosen = jnp.where((my_languages == 1)[:, None], words[1][None, :], words[0][None, :])
-    spare = KEY_ROWS - text_length - clip_length
-    context = jnp.concatenate(
-        [
-            low(projected + chosen[:, None, :]),
-            clip_full,
-            jnp.zeros((slots, spare, text_width), jnp.bfloat16),
-        ],
-        1,
-    ).reshape(slots * KEY_ROWS, text_width)
-    my_counts = lax.dynamic_slice_in_dim(counts, first_slot(me), slots, 0)
+    my_counts = cut_at(counts, spot.slots_back[0], slots, 0)
     key_place = jnp.arange(KEY_ROWS, dtype=jnp.int32)[None, :]
     visible = jnp.where(
         key_place < text_length,
@@ -718,47 +1015,102 @@
         q=extra_lanes([jnp.ones((rows,), jnp.float32)]),
         k=extra_lanes([cross_key_extra, zeros_keys, zeros_keys, zeros_keys, ones_keys, ones_keys]),
     )
-    context_kv = dot_rows(context, kv_full)
-    kv_gains = gain_rows(ck_gain, ck_gain)
-    key_columns = [
-        2 * local_width * group + HEAD_DIM * head
-        for group in range(size)
-        for head in range(local_heads)
+    tables = [
+        *spot.all,
+        tile_slots,
+        slot_masks,
+        first_gains,
+        self_gains,
+        kv_gains,
+        query_gains,
+        third_gain,
+        second_gain,
+        cross_pick,
+        chosen,
+        *cross_extras.values(),
+        *self_extras.values(),
+        rope,
     ]
-    kv_columns = [key_columns, [column + local_width for column in key_columns]]
-    cross_keys, cross_values = cut_heads(
-        context_kv, kv_gains, ("k", "v"), kv_columns, cross_extras
-    )
-
+
+    steps_all = gather_rows(timesteps, "dp", spot)
+    features_all = low(timestep_features(steps_all, time_weight.shape[0]))
+    gate_all, silu_pull = jax.vjp(jax.nn.silu, dot_plain(features_all, time_weight))
+    gate_all = low(gate_all)
+    gate = cut_at(gate_all, spot.place_slots, SMALL_PER, 0)
+    shift_own = low(dot_plain(gate, shift_weight))
+    shift_blocks = gather_blocks(shift_own)
+    if size == 2:
+        shifts = jnp.where(
+            spot.first,
+            jnp.concatenate(shift_blocks, 1),
+            jnp.concatenate(shift_blocks[::-1], 1),
+        )
+    else:
+        shifts = lax.all_gather(shift_own, "seq", axis=1, tiled=True)
+
+    partial = product([t5_text.reshape(-1, t5_text.shape[2])], [t5_weight])
+    partial = partial.reshape(SMALL_PER, text_length, text_width)
     if size == 2:
         chunk = [
-            jnp.where(me == 0, latent, skip_input),
-            jnp.where(me == 0, skip_input, latent),
+            jnp.where(spot.first, latent, skip_input),
+            jnp.where(spot.first, skip_input, latent),
         ]
     else:
         joined = jnp.concatenate([latent, skip_input], 1)
         part = 2 * width // size
         chunk = [
-            lax.dynamic_slice_in_dim(joined, owner(step) * part, part, 1) for step in range(size)
+            cut_at(joined, spot.joined_spans[step], part, 1) for step in range(size)
         ]
-    hidden = dot_plain(chunk[0], skip_blocks[0])
+    half_depth = chunk[0].shape[1] // 2
+    lefts, rights = [chunk[0]], [skip_weight]
     for step in range(1, size):
-        hidden = hidden + dot_plain(chunk[step], skip_blocks[step])
-    skip_normed, skip_spread = norm_rows(hidden)
-    residual_one = skip_normed * skip_gain
-    first_normed, first_spread = norm_rows(residual_one)
-    normed = low(first_normed * norm1_gain + shift_rows)
+        lefts += [cut_at(chunk[step], side, half_depth, 1) for side in spot.sides]
+    skip_pieces = [after(block, partial, shifts, active_slopes[0], *tables, *lefts) for block in skip_pieces]
+    skip_others = [swap_bit(piece, "dp", 0) for piece in skip_pieces]
+    for mine, other in zip(skip_pieces, skip_others):
+        rights += [mine, other]
+    spare = width - text_width
+    cross_rows = jnp.concatenate([cq_own, cross_out, jnp.pad(kv_own, ((0, 0), (0, spare)))], 0)
+    cross_blocks = [cross_rows] + gather_weight(cross_rows, skip_pieces, skip_others, spot)
+    cq_full = jnp.concatenate([block[:local_width] for block in cross_blocks], 0)
+    co_full = jnp.concatenate(
+        [block[local_width : 2 * local_width] for block in cross_blocks], 0
+    )
+    kv_full = jnp.concatenate(
+        [block[2 * local_width :, :text_width] for block in cross_blocks], 0
+    )
+
+
+    text_terms = [cut_at(partial, spot.slots_back[step], slots, 0) for step in range(size)]
+    text_came = send_terms([after(term, *skip_pieces) for term in text_terms])
+    clip_came = []
+    for step in range(size):
+        block = cut_at(after(clip_text, *skip_pieces), spot.slots_ahead[step], slots, 0)
+        clip_came.append(from_back(block, step) if step else block)
+
+    hidden = product(lefts, rights, kind=jnp.float32)
+    residual_one, normed = row_call(
+        first_norms_kernel,
+        "first_norms",
+        tile,
+        [hidden],
+        [first_gains, wide(shifts)],
+        [jnp.float32, jnp.bfloat16],
+        tile_slots,
+    )
     normed_blocks = gather_blocks(normed)
+
 
     self_kinds = ("q", "k", "v")
     self_columns = [
         [local_width * which + HEAD_DIM * head for head in range(local_heads)]
         for which in range(3)
     ]
-    self_gains = gain_rows(q_gain, k_gain)
     qkv_blocks, cut = [], None
     for step in range(size):
-        qkv_blocks.append(dot_rows(normed_blocks[step], qkv_rows))
+        qkv_blocks.append(product([normed_blocks[step]], [qkv_rows], ROW_TIMES_ROW))
+        if step == 0 and size > 1:
+            normed_blocks[1] = after(normed_blocks[1], qkv_blocks[0])
         cut = cut_heads(
             qkv_blocks[step],
             self_gains,
@@ -772,66 +1124,149 @@
         )
     queries, keys, values = cut
     no_pick = jnp.zeros((1,), jnp.int32)
-    self_outputs, self_queries = [None] * size, [None] * size
+    self_outputs, self_queries = [None] * size, None
     out_terms = [None] * size
     for step in list(range(1, size)) + [0]:
-        self_outputs[step], self_queries[step] = attend(
-            queries, keys, values, no_pick, rows, tokens, step, size
+        if step == 0:
+            queries = after(queries, *out_terms[1:])
+        self_outputs[step], self_queries = attend(
+            queries, keys, values, no_pick, rows, tokens, step, size, self_queries
         )
-        out_terms[step] = dot_plain(self_outputs[step], out_weight)
-    residual_two = residual_one + sum_blocks(out_terms)
-
-    third_normed, third_spread = norm_rows(residual_two)
-    normed_cross = low(third_normed * norm3_gain)
-    cross_pre = dot_rows(normed_cross, cq_full)
-    query_gains = gain_rows(cq_gain)
+        out_terms[step] = product([self_outputs[step]], [out_weight])
+    out_came = send_terms(out_terms)
+
+    hold = out_terms[1:] + text_came + clip_came[1:]
+    text_came = [after(came, *hold) for came in text_came]
+    clip_came = [after(came, *hold) for came in clip_came]
+    projected = wide(text_terms[0])
+    for came in text_came:
+        projected = projected + wide(came)
+    clip_full = jnp.zeros((slots, clip_length, text_width), jnp.bfloat16)
+    zero = np.uint32(0)
+    for block, span in zip(clip_came, spot.text_spans):
+        clip_full = lax.dynamic_update_slice(clip_full, block, [zero, zero, span])
+    unused = KEY_ROWS - text_length - clip_length
+    context = jnp.concatenate(
+        [
+            low(projected + chosen[:, None, :]),
+            clip_full,
+            jnp.zeros((slots, unused, text_width), jnp.bfloat16),
+        ],
+        1,
+    ).reshape(slots * KEY_ROWS, text_width)
+    context_kv = product([context], [kv_full], ROW_TIMES_ROW)
+    key_columns = [
+        2 * local_width * group + HEAD_DIM * head
+        for group in range(size)
+        for head in range(local_heads)
+    ]
+    kv_columns = [key_columns, [column + local_width for column in key_columns]]
+    cross_keys, cross_values = cut_heads(
+        context_kv, kv_gains, ("k", "v"), kv_columns, cross_extras
+    )
+
+    out_came = [after(came, out_terms[0], cross_keys) for came in out_came]
+    cotangent_blocks = gather_blocks(after(cotangent, *out_came))
+    residual_two, normed_cross = row_call(
+        add_norm_kernel,
+        "cross_norm",
+        tile,
+        [residual_one, out_terms[0], *out_came],
+        [third_gain],
+        [jnp.float32, jnp.bfloat16],
+    )
+
+    cross_pre = product([normed_cross], [cq_full], ROW_TIMES_ROW)
     query_columns = [[HEAD_DIM * head for head in range(all_heads)]]
     (cross_queries,) = cut_heads(cross_pre, query_gains, ("q",), query_columns, cross_extras)
-    cross_pick = small * (jnp.arange(rows // tile, dtype=jnp.int32) * tile // quarter)
     cross_outputs, cross_queries = attend(
         cross_queries, cross_keys, cross_values, cross_pick, tile, KEY_ROWS
     )
-    residual_three = residual_two + dot_plain(cross_outputs, co_full)
-
-    second_normed, second_spread = norm_rows(residual_three)
-    mlp_blocks = gather_blocks(low(second_normed * norm2_gain))
-    cotangent_blocks = gather_blocks(cotangent)
-    active, expanded_grads, fc_terms, mlp_terms = [], [], [], []
+    residual_three, normed_mlp = row_call(
+        add_norm_kernel,
+        "mlp_norm",
+        tile,
+        [residual_two, product([cross_outputs], [co_full])],
+        [second_gain],
+        [jnp.float32, jnp.bfloat16],
+    )
+
+    mlp_blocks = gather_blocks(normed_mlp)
+    active, expanded_grads, mlp_terms = [], [], []
     for step in range(size):
-        gate_out, gate_slope = gelu_and_slope(dot_plain(mlp_blocks[step], fc1_weight))
+        gate_out, gate_grad = gelu_both(mlp_blocks[step], fc1_weight, active_slopes[step])
         active.append(gate_out)
-        expanded_grads.append(low(dot_rows(cotangent_blocks[step], fc2_weight) * gate_slope))
-        mlp_terms.append(dot_rows(expanded_grads[step], fc1_weight))
-    mlp_slope = sum_blocks(mlp_terms)
-    for step in range(size):
-        fc_terms.append(dot_plain(active[step], fc2_weight))
-    block_output = low(residual_three + sum_blocks(fc_terms))
-    active_all = jnp.concatenate(active, 0)
-    expanded_all = jnp.concatenate(expanded_grads, 0)
-    grad_fc2 = scatter_sum(dot_sum(jnp.concatenate(cotangent_blocks, 0), active_all)).T
-    grad_fc1 = scatter_sum(dot_sum(jnp.concatenate(mlp_blocks, 0), expanded_all))
-
-    grad_norm2 = jnp.sum(mlp_slope * second_normed, 0)
-    grad_three = wide(cotangent) + norm_back(
-        mlp_slope * norm2_gain, second_normed, second_spread
-    )
-
-    three_low = low(grad_three)
-    cross_slopes = cut_grad(low(dot_rows(three_low, co_full)), cross_outputs)
+        expanded_grads.append(gate_grad)
+        mlp_terms.append(product([gate_grad], [fc1_weight], ROW_TIMES_ROW))
+        if step == 0:
+            fc_terms = [product([active[0]], [fc2_weight])]
+            active_slopes += [
+                product([block], [fc2_weight], ROW_TIMES_ROW) for block in cotangent_blocks[1:]
+            ]
+            mlp_blocks[1:] = [
+                after(block, mlp_terms[0], fc_terms[0], *active_slopes[1:])
+                for block in mlp_blocks[1:]
+            ]
+    mlp_came = send_terms(mlp_terms)
+    fc_sum = sum_product([after(one, *mlp_terms[1:]) for one in cotangent_blocks], active, 0, 2)
+    fc_sum = sum_product(mlp_blocks, expanded_grads, 1, 2, fc_sum)
+    for step in range(1, size):
+        fc_terms.append(product([after(active[step], fc_sum)], [fc2_weight]))
+    mlp_came = [after(came, fc_sum, *fc_terms) for came in mlp_came]
+    fc_sums = [Summing(fc_sum, spot)]
+    fc_terms[1:] = [after(term, *mlp_came) for term in fc_terms[1:]]
+    fc_came = send_terms(fc_terms)
+
+    sent = advance_all(fc_sums, *mlp_came)
+    mlp_came = [after(came, sent) for came in mlp_came]
+    grad_three, three_low, norm2_sum = row_call(
+        norm_back_kernel,
+        "mlp_norm_back",
+        tile,
+        [cotangent, residual_three, mlp_terms[0], *mlp_came],
+        [second_gain],
+        [jnp.float32, jnp.bfloat16, 8],
+    )
+
+    cross_slopes = cut_grad(product([three_low], [co_full], ROW_TIMES_ROW), cross_outputs)
+    cross_slopes = after(cross_slopes, advance_all(fc_sums, cross_slopes))
     grad_cq, grad_ck, grad_cv = attend_back(
         cross_queries, cross_keys, cross_values, cross_slopes, cross_pick, tile, KEY_ROWS
     )
+    fc_came = [after(came, grad_cq) for came in fc_came]
+    block_output = residual_three + wide(fc_terms[0])
+    for came in fc_came:
+        block_output = block_output + wide(came)
+    block_output = low(block_output)
+    joined_blocks = [chunk[0]]
+    for step in range(1, size):
+        if size == 2:
+            block = chunk[1]
+        else:
+            block = cut_at(joined, spot.joined_ahead[step], part, 1)
+        block = after(block, *fc_terms)
+        joined_blocks.append(from_back(block, step))
+    grad_cq = after(grad_cq, block_output)
     cross_pre_grad, query_sums = join_heads(
         cross_pre, query_gains, ("q",), query_columns, (grad_cq,)
     )
-    cross_slope = dot_plain(cross_pre_grad, cq_full)
-    grad_norm3 = jnp.sum(cross_slope * third_normed, 0)
-    grad_two = grad_three + norm_back(cross_slope * norm3_gain, third_normed, third_spread)
-    two_blocks = gather_blocks(low(grad_two))
+    cross_slope = product([cross_pre_grad], [cq_full])
+    cross_slope = after(cross_slope, *joined_blocks[1:])
+    grad_two, two_low, norm3_sum = row_call(
+        norm_back_kernel,
+        "cross_norm_back",
+        tile,
+        [grad_three, residual_two, cross_slope],
+        [third_gain],
+        [jnp.float32, jnp.bfloat16, 8],
+    )
+    two_blocks = gather_blocks(two_low)
     context_kv_grad, key_sums = join_heads(
-        context_kv, kv_gains, ("k", "v"), kv_columns, (grad_ck, grad_cv)
-    )
-    context_grad = dot_plain(context_kv_grad, kv_full).reshape(slots, KEY_ROWS, text_width)
+        context_kv, kv_gains, ("k", "v"), kv_columns, (after(grad_ck, two_low), grad_cv)
+    )
+    kv_sum = sum_product([context], [context_kv_grad])
+    context_grad = product([context_kv_grad], [kv_full], kind=jnp.float32)
+    context_grad = context_grad.reshape(slots, KEY_ROWS, text_width)
 
     def own_part(summed):
         blocks = [
@@ -840,57 +1275,44 @@
         ]
         return sum_blocks(blocks)
 
-    grad_cross = scatter_sum(
-        jnp.concatenate(
-            [dot_sum(normed_cross, cross_pre_grad), dot_sum(three_low, cross_outputs)], 1
-        )
-    )
-    grad_cross_query = own_part(grad_cross[:, : all_heads * HEAD_DIM])
-    grad_cross_out = own_part(grad_cross[:, all_heads * HEAD_DIM :]).T
-    grad_cross_kv = own_part(scatter_sum(dot_sum(context, context_kv_grad)))
-    grad_cross_kv = grad_cross_kv.reshape(-1, 2, local_width)
+    later = after(three_low, two_low)
+    cross_sum = sum_product([later], [cross_outputs], 0, 2)
+    cross_sum = sum_product([normed_cross], [cross_pre_grad], 1, 2, cross_sum)
+    two_blocks[1:] = [
+        after(block, cross_sum, kv_sum, context_grad) for block in two_blocks[1:]
+    ]
+    cross_sums = [Summing(kv_sum, spot), Summing(cross_sum, spot)]
+    sent = advance_all(fc_sums + cross_sums, *two_blocks[1:])
+    two_blocks[1:] = [after(block, sent) for block in two_blocks[1:]]
 
     def spread_slots(blocks):
         found = []
         for slot in range(SMALL_PER):
             total = 0.0
             for step, block in enumerate(blocks):
-                offset = slot - first_slot((me + step) % size)
-                inside = (offset >= 0) & (offset < slots)
-                part = lax.dynamic_index_in_dim(
-                    block, jnp.clip(offset, 0, slots - 1), 0, False
-                )
-                total = total + jnp.where(inside, wide(part), 0.0)
+                inside, index = spot.spread[step][slot]
+                total = total + inside * wide(pick_at(block, index, 0))
             found.append(total)
         return jnp.stack(found)
 
     text_grad = context_grad[:, :text_length]
-    text_low = low(text_grad)
+    text_low = after(low(text_grad), *two_blocks[1:])
     text_blocks = [text_low] + [to_back(text_low, step) for step in range(1, size)]
-    project_all = low(spread_slots(text_blocks)).reshape(SMALL_PER * text_length, text_width)
     clip_blocks = []
     for step in range(size):
-        block = lax.dynamic_slice_in_dim(
+        block = cut_at(
             context_grad[:, text_length : text_length + clip_length],
-            owner(step) * text_local,
+            spot.text_spans[step],
             text_local,
             2,
         )
-        clip_blocks.append(to_back(low(block), step) if step else block)
-    grad_clip = spread_slots(clip_blocks)
-    grad_t5 = dot_rows(project_all, t5_weight).reshape(t5_text.shape)
-    grad_t5_weight = scatter_sum(
-        dot_sum(project_all, t5_text.reshape(-1, t5_text.shape[2]))
-    ).T
-    tongues = wide(my_languages[None, :] == jnp.arange(2, dtype=jnp.int32)[:, None])
-    grad_lang = jnp.dot(tongues, jnp.sum(text_grad, 1), precision=PRECISE)
-
+        clip_blocks.append(to_back(after(low(block), text_low), step) if step else block)
     slopes = None
     for step in range(size):
         slopes = cut_grad(
-            low(dot_rows(two_blocks[step], out_weight)), self_outputs[step], step, size, slopes
+            product([two_blocks[step]], [out_weight], ROW_TIMES_ROW), self_outputs[step], step, size, slopes
         )
-    self_queries = jnp.concatenate(self_queries, 1)
+    slopes = after(slopes, advance_all(cross_sums, slopes))
     back_tile = min(512, tokens)
     head_grads = attend_back(
         self_queries,
@@ -901,76 +1323,118 @@
         back_tile,
         tokens,
     )
+    sent = advance_all(fc_sums, head_grads[0])
+    head_grads = [
+        after(head_grads[0], sent, *text_blocks[1:], *clip_blocks[1:]),
+        *head_grads[1:],
+    ]
     qkv_grads, normed_terms = [None] * size, [None] * size
     self_sums = 0.0
     for step in list(range(1, size)) + [0]:
+        if step == 0:
+            head_grads = [after(head_grads[0], *normed_terms[1:]), *head_grads[1:]]
         qkv_grads[step], sums = join_heads(
             qkv_blocks[step], self_gains, self_kinds, self_columns, head_grads, rope, step
         )
         self_sums = self_sums + sums
-        normed_terms[step] = dot_plain(qkv_grads[step], qkv_rows)
-    normed_slope = sum_blocks(normed_terms)
-    normed_all = jnp.concatenate(normed_blocks, 0)
-    grad_qkv = scatter_sum(dot_sum(normed_all, jnp.concatenate(qkv_grads, 0)))
-    grad_qkv = grad_qkv.reshape(-1, 3, local_width)
-    grad_out = scatter_sum(
-        dot_sum(jnp.concatenate(two_blocks, 0), jnp.concatenate(self_outputs, 0))
-    ).T
-
-    grad_norm1 = jnp.sum(normed_slope * first_normed, 0)
-    residual_slope = grad_two + norm_back(normed_slope * norm1_gain, first_normed, first_spread)
-    grad_skip_gain = jnp.sum(residual_slope * skip_normed, 0)
-    hidden_low = low(norm_back(residual_slope * skip_gain, skip_normed, skip_spread))
+        normed_terms[step] = product([qkv_grads[step]], [qkv_rows])
+    normed_came = send_terms(normed_terms)
+    qkv_sum = sum_product(normed_blocks, qkv_grads)
+    normed_terms[0] = after(normed_terms[0], qkv_sum)
+    normed_came = [after(came, normed_terms[0]) for came in normed_came]
+    qkv_sums = [Summing(qkv_sum, spot)]
+    sent = advance_all(qkv_sums, *normed_came)
+    normed_came = [after(came, sent) for came in normed_came]
+
+    hidden_low, first_sums, slot_sums = row_call(
+        first_norms_back_kernel,
+        "first_norms_back",
+        tile,
+        [grad_two, hidden, normed_terms[0], *normed_came],
+        [first_gains],
+        [jnp.bfloat16, 8, "tile"],
+    )
     hidden_blocks = gather_blocks(hidden_low)
-    joined_blocks = [chunk[0]]
-    for step in range(1, size):
-        if size == 2:
-            block = chunk[1]
-        else:
-            block = lax.dynamic_slice_in_dim(joined, (me + step) % size * part, part, 1)
-        joined_blocks.append(from_back(block, step))
-    grad_skip_weight = scatter_sum(
-        dot_sum(jnp.concatenate(hidden_blocks, 0), jnp.concatenate(joined_blocks, 0))
-    ).T
-    joined_grads = [dot_rows(hidden_low, block) for block in skip_blocks]
+    sent = advance_all(qkv_sums + fc_sums + cross_sums, hidden_low)
+    out_sum = sum_product(after(two_blocks, sent), self_outputs)
+    text_blocks[0] = after(text_blocks[0], out_sum)
+    project_all = low(spread_slots(text_blocks)).reshape(SMALL_PER * text_length, text_width)
+    t5_sum = sum_product([project_all], [t5_text.reshape(-1, t5_text.shape[2])])
+    out_sums, t5_sums = [Summing(out_sum, spot)], [Summing(t5_sum, spot, True)]
+    hidden_blocks[1:] = [after(block, t5_sum) for block in hidden_blocks[1:]]
+    skip_sum = sum_product(hidden_blocks, joined_blocks)
+    skip_sums = [Summing(skip_sum, spot)]
+    sent = advance_all(skip_sums + out_sums + t5_sums + cross_sums + qkv_sums, skip_sum)
+    sent = advance_all(skip_sums + out_sums + t5_sums, sent)
+
+    tongues = wide(my_languages[None, :] == jnp.arange(2, dtype=jnp.int32)[:, None])
+    grad_lang = jnp.dot(tongues, jnp.sum(text_grad, 1), precision=PRECISE)
+    gains = [
+        first_sums[0],
+        first_sums[1],
+        self_sums[0, :HEAD_DIM],
+        self_sums[1, :HEAD_DIM],
+        norm3_sum[0],
+        query_sums[0, :HEAD_DIM],
+        key_sums[0, :HEAD_DIM],
+        norm2_sum[0],
+        grad_lang.reshape(-1),
+    ]
+    packed = after(jnp.concatenate(gains), t5_sum)
+    packed_came = swap_bit(packed, "dp", 0)
+    shift_terms = jnp.zeros((SMALL_PER, width), jnp.float32)
+    for number in range(rows // tile):
+        shift_terms += slot_masks[number][:, None] * after(slot_sums, t5_sum)[8 * number][None, :]
+    shift_sum = sum_over(shift_terms, "seq")
+    hidden_low = after(hidden_low, sent)
+    skip_blocks = [skip_weight]
+    for mine, other in zip(skip_pieces, skip_others):
+        skip_blocks.append(join_halves(mine, after(other, sent), spot))
+    joined_grads = [
+        product([hidden_low], [block], ROW_TIMES_ROW, jnp.float32) for block in skip_blocks
+    ]
+    fc_total = fc_sums[0].finish(*joined_grads)
+    grad_fc2, grad_fc1 = fc_total[0].T, fc_total[1]
+    sent = advance_all(qkv_sums + skip_sums + cross_sums, fc_total)
+    packed = packed + after(packed_came, sent)
+    shift_low = low(after(shift_sum, sent))
+    project_all = after(project_all, packed, shift_low)
+    grad_t5 = product([project_all], [t5_weight], ROW_TIMES_ROW, jnp.float32)
+    grad_t5 = grad_t5.reshape(t5_text.shape)
+    sent = advance_all(out_sums + t5_sums + skip_sums + qkv_sums, grad_t5)
+    sent = advance_all(out_sums + t5_sums, sent)
+    clip_blocks[0] = after(clip_blocks[0], sent)
+    grad_clip = spread_slots(clip_blocks)
     if size == 2:
-        grad_latent = jnp.where(me == 0, joined_grads[0], joined_grads[1])
-        grad_skip_input = jnp.where(me == 0, joined_grads[1], joined_grads[0])
+        grad_latent = jnp.where(spot.first, joined_grads[0], joined_grads[1])
+        grad_skip_input = jnp.where(spot.first, joined_grads[1], joined_grads[0])
     else:
         joined_grad = jnp.zeros((rows, 2 * width), jnp.float32)
         for step in range(size):
-            joined_grad = lax.dynamic_update_slice_in_dim(
-                joined_grad, joined_grads[step], owner(step) * part, 1
+            joined_grad = lax.dynamic_update_slice(
+                joined_grad, joined_grads[step], [np.uint32(0), spot.joined_spans[step]]
             )
         grad_latent, grad_skip_input = joined_grad[:, :width], joined_grad[:, width:]
 
-    shift_terms = jnp.dot(wide(own_pick).T, normed_slope, precision=PRECISE)
-    shift_low = low(sum_seq(shift_terms))
-    shift_all = lax.all_gather(shift_low, "dp", axis=0, tiled=True)
-    steps_all = lax.all_gather(timesteps, "dp", axis=0, tiled=True)
-    features_all = low(timestep_features(steps_all, time_weight.shape[0]))
-    gate_all, silu_pull = jax.vjp(jax.nn.silu, dot_plain(features_all, time_weight))
-    shift_mine = lax.dynamic_slice_in_dim(shift_all, me * local_width, local_width, 1)
-    parts = lax.axis_size("dp")
-    gate_mine = lax.dynamic_slice_in_dim(
-        low(gate_all), lax.axis_index("dp") * (width // parts), width // parts, 1
-    )
+    shift_all = gather_rows(shift_low, "dp", spot)
+    shift_mine = cut_at(shift_all, spot.me_columns, local_width, 1)
+    gate_mine = cut_at(gate_all, spot.place_columns, width // parts, 1)
     grad_shift = dot_sum(gate_mine, shift_mine)
-    (time_slope,) = silu_pull(sum_seq(dot_rows(shift_mine, shift_weight)))
+    (time_slope,) = silu_pull(sum_over(dot_rows(shift_mine, shift_weight), "seq"))
     grad_time = jnp.dot(wide(features_all).T, time_slope, precision=PRECISE)
 
-    gains = [
-        grad_skip_gain,
-        grad_norm1,
-        self_sums[0, :HEAD_DIM],
-        self_sums[1, :HEAD_DIM],
-        grad_norm3,
-        query_sums[0, :HEAD_DIM],
-        key_sums[0, :HEAD_DIM],
-        grad_norm2,
-        grad_lang.reshape(-1),
-    ]
-    packed = lax.psum(jnp.concatenate(gains), ("dp", "seq"))
+    grad_skip_weight = skip_sums[0].finish()[0].T
+    grad_qkv = qkv_sums[0].finish().reshape(-1, 3, local_width)
+    grad_out = out_sums[0].finish()[0].T
+    grad_t5_weight = t5_sums[0].finish()[0].T
+    kv_total, cross_total = [one.finish() for one in cross_sums]
+    grad_cross_kv = own_part(kv_total[0]).reshape(-1, 2, local_width)
+    grad_cross_out = own_part(cross_total[0]).T
+    grad_cross_query = own_part(cross_total[1])
+
+    for bit in range(1, lax.axis_size("dp").bit_length() - 1):
+        packed = packed + swap_bit(packed, "dp", bit)
+    packed = sum_over(packed, "seq")
     totals, start = [], 0
     for gain in gains:
         totals.append(packed[start : start + gain.shape[0]])

time: 1280 us -> 894 us (0.70)
  matrix products: 289 us -> 6.75 us
  waiting for transfers between devices: 419 us -> 169 us
  Pallas kernels: 218 us -> 364 us
  blocking collectives: 90.4 us -> 0 us
  local copies, waits for them, and re-layouts: 84.6 us -> 137 us
  other arithmetic: 65.8 us -> 96.9 us
    pallas_call x0 -> x42, Pallas kernels: none -> 200 us  [the longest x25 98.5 us: product(): pl.pallas_call(functools.partial(product_kernel, form=form), grid=(pl.cdi...]
    ppermute x32 -> x51, waiting for transfers between devices: 240 us -> 92.5 us  [the longest x37 61.7 us: swap_bit(): return lax.ppermute(values, axis, [(i, i ^ 1 << bit) for i in range(size)])]
    dot_general x17 -> x2, matrix products: 108 us -> 1.63 us  [dot_plain(): return jnp.dot(left, right, preferred_element_type=jnp.float32)]
    dot_general x15 -> x1, matrix products: 97.6 us -> 0.43 us  [dot_rows(): lax.dot_general(left, right, ROW_TIMES_ROW, preferred_element_type=jnp.fl...]
    dot_general x10 -> x1, matrix products: 75.6 us -> 1.85 us  [dot_sum(): lax.dot_general(left, right, COL_TIMES_COL, preferred_element_type=jnp.fl...]
    ppermute x10, waiting for transfers between devices: 84.5 us -> 18.1 us  [to_back(): lax.ppermute(values, 'seq', [(i, (i - step) % size) for i in range(size)])]
    psum x1 -> x0, blocking collectives: 43.3 us -> none  [on_device(): packed = lax.psum(jnp.concatenate(gains), ('dp', 'seq'))]
    unnamed x263 -> x464, local copies, waits for them, and re-layouts: 36.1 us -> 73.9 us
  transfers between devices with their start and end apart: 66 -> 72, of which waited for: 31 -> 24; matrix products, arithmetic and copies ran while one was open for 29% -> 15% of each run, Pallas kernels for 13% -> 36%
where the time goes in v2:
time: 894 us; the launch traced here: 881 us
  Pallas kernels  364 us (41%)
  waiting for transfers between devices  169 us (19%)
  local copies, waits for them, and re-layouts  137 us (15%)
  other arithmetic  96.9 us (11%)
  starting transfers between devices  88.7 us (10%)
  between operations  18.7 us (2%)
    pallas_call x25, Pallas kernels, product(): pl.pallas_call(functools.partial(product_kernel, form=form), grid=(pl.cdi...  98.5 us
    unnamed x464, local copies, waits for them, and re-layouts  73.9 us
    pallas_call x9, Pallas kernels, sum_product(): pl.pallas_call(functools.partial(sum_product_kernel, blocks=blocks), grid...  61.8 us
    ppermute x37, waiting for transfers between devices, swap_bit(): return lax.ppermute(values, axis, [(i, i ^ 1 << bit) for i in range(size)])  61.7 us
    ppermute x10, waiting for transfers between devices, from_back(): lax.ppermute(values, 'seq', [(i, (i + step) % size) for i in range(size)])  58.9 us
    pallas_call x4, Pallas kernels, join_heads(): pl.pallas_call(functools.partial(join_kernel, kinds=kinds, columns=column...  51.8 us
    pallas_call x2, Pallas kernels, attend_back(): pl.pallas_call(functools.partial(attend_back_kernel, key_rows=key_rows),...  45.9 us
    add x28, other arithmetic, advance(): held = self.keep + (after(self.came, *hold) if hold else self.came)  42.7 us
  transfers between devices with their start and end apart: 72, of which 24 were waited for; matrix products, arithmetic and copies ran while one was open for 15% of the time, Pallas kernels for 36%

profile of v2, /device:TPU:15, one launch (start us, length us, event | category | flops | bytes accessed | tf_op | source)
XLA Modules:
  0.0 881.2 jit_solution(7320485239057813412)
XLA Ops:
  24.2 5.7 product.26.slope_ref
  63.0 6.9 fusion.1
  71.3 12.8 %collective-permute-done.11 = bf16[176,1408]{1,0:T(8,128)(2,1)} collective-permute-done((bf16[176,1408]{1,0:T(8,128)(2,1)S(1)}, bf16[176,1408]{1,0:T(8,128)(2,1)}, u32[]{:S(2)}, u32[]{:S(2)}) %collective-permute-start.11) | collective-permute-done | bytes 495648 | tf_op jit(solution)/shard_map/ppermute | solution.py:661
  89.8 7.2 product.27.hidden_ref.refs_1_
  112.9 5.7 cut_heads.4
  118.6 15.2 %collective-permute-done.7.refs_0_.refs_1_ = bf16[512,1408]{1,0:T(8,128)(2,1)S(1)} collective-permute-done((bf16[512,1408]{1,0:T(8,128)(2,1)S(1)}, bf16[512,1408]{1,0:T(8,128)(2,1)S(1)}, u32[]{:S(2)}, u32[]{:S(2)}) %collective-permute-start.7) | collective-permute-done | bytes 1441824 | tf_op jit(solution)/shard_map/ppermute | solution.py:661
  141.1 5.7 cut_heads.5
  146.8 7.9 attend.3
  159.6 7.9 attend.4
  180.1 5.6 product.32.refs_0_
  185.8 7.8 cut_heads.6
  202.7 4.9 cut_heads.7.q_ref
  209.3 15.6 %attend.5 = (bf16[512,1408]{1,0:T(8,128)(2,1)S(1)}, bf16[16,512,128]{2,1,0:T(8,128)(2,1)S(1)}) custom-call(s32[2]{0:T(128)S(1)} %copy-done.119, bf16[16,512,128]{2,1,0:T(8,128)(2,1)S(1)} %cut_heads.7.q_ref, bf16[16,768,128]{2,1,0:T(8,128)(2,1)S(1)} %get-tuple-element.255.k_ref, bf16[16,768,128]{2,1,0:T(8,128)(2,1)S(1)} %get-tuple-element.259.v_ref), custom_call_target="tpu_custom_call" | custom-call | flops 1572864000 | bytes 1 | tf_op jit(solution)/shard_map/attend/pallas_call | solution.py:299
  231.3 10.1 %gelu_both.2 = (bf16[512,3072]{1,0:T(8,128)(2,1)S(1)}, bf16[512,3072]{1,0:T(8,128)(2,1)S(1)}) custom-call(bf16[512,1408]{1,0:T(8,128)(2,1)S(1)} %get-tuple-element.262.rows_ref.refs_0_, bf16[1408,3072]{1,0:T(8,128)(2,1)S(1)} %bitcast.236, bf16[512,3072]{1,0:T(8,128)(2,1)S(1)} %copy-done.40), custom_call_target="tpu_custom_call" | custom-call | flops 2200000000 | bytes 1 | tf_op jit(solution)/shard_map/gelu_both/pallas_call | solution.py:517
  241.4 5.0 product.35
  246.5 5.1 product.36.refs_2_
  251.7 5.7 product.37.slope_ref
  257.4 13.3 %collective-permute-done.12.rows_ref.refs_1_ = bf16[512,1408]{1,0:T(8,128)(2,1)S(1)} collective-permute-done((bf16[512,1408]{1,0:T(8,128)(2,1)S(1)}, bf16[512,1408]{1,0:T(8,128)(2,1)S(1)}, u32[]{:S(2)}, u32[]{:S(2)}) %collective-permute-start.12) | collective-permute-done | bytes 1441824 | tf_op jit(solution)/shard_map/ppermute | solution.py:661
  270.6 10.4 %gelu_both.3 = (bf16[512,3072]{1,0:T(8,128)(2,1)S(1)}, bf16[512,3072]{1,0:T(8,128)(2,1)S(1)}) custom-call(bf16[512,1408]{1,0:T(8,128)(2,1)S(1)} %collective-permute-done.12.rows_ref.refs_1_, bf16[1408,3072]{1,0:T(8,128)(2,1)S(1)} %bitcast.236, bf16[512,3072]{1,0:T(8,128)(2,1)S(1)} %product.37.slope_ref), custom_call_target="tpu_custom_call" | custom-call | flops 2200000000 | bytes 1 | tf_op jit(solution)/shard_map/gelu_both/pallas_call | solution.py:517
  281.1 6.2 product.38
  287.6 11.3 %sum_product.9.refs_4_ = bf16[2,1408,3072]{2,1,0:T(8,128)(2,1)S(1)} custom-call(bf16[512,1408]{1,0:T(8,128)(2,1)S(1)} %copy-done.27, bf16[512,1408]{1,0:T(8,128)(2,1)S(1)} %copy-done.83, bf16[512,3072]{1,0:T(8,128)(2,1)S(1)} %get-tuple-element.263.refs_0_.refs_2_, bf16[512,3072]{1,0:T(8,128)(2,1)S(1)} %get-tuple-element.271.refs_3_.refs_0_), custom_call_target="tpu_custom_call" | custom-call | flops 2562232064 | bytes 1 | tf_op jit(solution)/shard_map/sum_product/pallas_call | solution.py:440
  301.6 11.3 %sum_product.10 = bf16[2,1408,3072]{2,1,0:T(8,128)(2,1)S(1)} custom-call(bf16[512,1408]{1,0:T(8,128)(2,1)S(1)} %copy-done.89, bf16[512,1408]{1,0:T(8,128)(2,1)S(1)} %copy-done.91, bf16[512,3072]{1,0:T(8,128)(2,1)S(1)} %copy-done.42, bf16[512,3072]{1,0:T(8,128)(2,1)S(1)} %copy-done.44, ...), custom_call_target="tpu_custom_call", output_to_operand_aliasing={{}: (4, {})} | custom-call | flops 2562232064 | bytes 1 | tf_op jit(solution)/shard_map/sum_product/pallas_call | solution.py:440
  312.9 5.9 copy-done.1
  318.9 5.0 product.39
  325.0 7.6 dynamic-slice_bitcast_fusion
  350.2 5.4 cut_grad.3.g_ref
  359.7 4.9 dynamic-slice_bitcast_fusion.1
  366.3 18.4 %attend_back.2 = (f32[16,512,128]{2,1,0:T(8,128)S(1)}, f32[16,768,128]{2,1,0:T(8,128)S(1)}, f32[16,768,128]{2,1,0:T(8,128)S(1)}) custom-call(s32[2]{0:T(128)S(1)} %copy-done.119, bf16[16,512,128]{2,1,0:T(8,128)(2,1)S(1)} %copy-done.101, bf16[16,768,128]{2,1,0:T(8,128)(2,1)S(1)} %copy-done.36, bf16[16,768,128]{2,1,0:T(8,128)(2,1)S(1)} %copy-done.38, ...), custom_call_target="tpu_custom_call" | custom-call | flops 2202009600 | bytes 1 | tf_op jit(solution)/shard_map/attend_back/pallas_call | solution.py:395
  389.8 7.9 collective-permute-done.15
  399.4 11.2 %join_heads.4 = (bf16[512,1408]{1,0:T(8,128)(2,1)S(1)}, f32[8,128]{1,0:T(8,128)S(1)}) custom-call(bf16[512,1408]{1,0:T(8,128)(2,1)S(1)} %copy-done.31, f32[8,128]{1,0:T(8,128)S(1)} %copy-done.116, f32[16,512,128]{2,1,0:T(8,128)S(1)} %get-tuple-element.283.refs_2_), custom_call_target="tpu_custom_call" | custom-call | flops 1474560000 | bytes 1 | tf_op jit(solution)/shard_map/join_heads/pallas_call | solution.py:240
  413.2 15.4 %collective-permute-done.17.refs_3_ = bf16[512,1408]{1,0:T(8,128)(2,1)S(1)} collective-permute-done((bf16[512,1408]{1,0:T(8,128)(2,1)}, bf16[512,1408]{1,0:T(8,128)(2,1)S(1)}, u32[]{:S(2)}, u32[]{:S(2)}) %collective-permute-start.17) | collective-permute-done | bytes 1441824 | tf_op jit(solution)/shard_map/ppermute | solution.py:661
  444.1 17.5 %join_heads.5 = (bf16[768,2816]{1,0:T(8,128)(2,1)S(1)}, f32[8,128]{1,0:T(8,128)S(1)}) custom-call(bf16[768,2816]{1,0:T(8,128)(2,1)S(1)} %bitcast.259, f32[8,128]{1,0:T(8,128)S(1)} %copy-done.118, f32[16,768,128]{2,1,0:T(8,128)S(1)} %copy-done.72, f32[16,768,128]{2,1,0:T(8,128)S(1)} %bitcast.276), custom_call_target="tpu_custom_call" | custom-call | flops 4423680000 | bytes 1 | tf_op jit(solution)/shard_map/join_heads/pallas_call | solution.py:240
  461.6 7.1 sum_product.13
  475.0 6.0 bitcast_add_fusion.1
  517.7 27.6 %attend_back.3 = (f32[8,1024,128]{2,1,0:T(8,128)S(1)}, f32[8,1024,128]{2,1,0:T(8,128)S(1)}, f32[8,1024,128]{2,1,0:T(8,128)S(1)}) custom-call(s32[2]{0:T(128)S(1)} %broadcast.628.pick, bf16[8,1024,128]{2,1,0:T(8,128)(2,1)S(1)} %copy-done.103, bf16[8,1024,128]{2,1,0:T(8,128)(2,1)S(1)} %copy-done.62, bf16[8,1024,128]{2,1,0:T(8,128)(2,1)S(1)} %copy-done.64, ...), custom_call_target="tpu_custom_call" | custom-call | flops 5872025600 | bytes 1 | tf_op jit(solution)/shard_map/attend_back/pallas_call | solution.py:395
  548.8 11.5 %join_heads.6 = (bf16[512,2112]{1,0:T(8,128)(2,1)S(1)}, f32[8,128]{1,0:T(8,128)S(1)}) custom-call(bf16[512,2112]{1,0:T(8,128)(2,1)S(1)} %copy-done.20, f32[8,128]{1,0:T(8,128)S(1)} %copy-done.111, f32[1024,384]{1,0:T(8,128)S(1)} %copy-done.8, f32[8,1024,128]{2,1,0:T(8,128)S(1)} %get-tuple-element.311.refs_3_, ...), custom_call_target="tpu_custom_call" | custom-call | flops 2211840000 | bytes 1 | tf_op jit(solution)/shard_map/join_heads/pallas_call | solution.py:240
  564.4 11.5 %join_heads.7 = (bf16[512,2112]{1,0:T(8,128)(2,1)S(1)}, f32[8,128]{1,0:T(8,128)S(1)}) custom-call(bf16[512,2112]{1,0:T(8,128)(2,1)S(1)} %copy-done.22, f32[8,128]{1,0:T(8,128)S(1)} %copy-done.111, f32[1024,384]{1,0:T(8,128)S(1)} %copy-done.8, f32[8,1024,128]{2,1,0:T(8,128)S(1)} %get-tuple-element.311.refs_3_, ...), custom_call_target="tpu_custom_call" | custom-call | flops 2211840000 | bytes 1 | tf_op jit(solution)/shard_map/join_heads/pallas_call | solution.py:240
  579.8 9.6 %sum_product.14 = bf16[1,1408,2112]{2,1,0:T(8,128)(2,1)S(1)} custom-call(bf16[512,1408]{1,0:T(8,128)(2,1)S(1)} %copy-done.75, bf16[512,1408]{1,0:T(8,128)(2,1)S(1)} %copy-done.77, bf16[512,2112]{1,0:T(8,128)(2,1)S(1)} %get-tuple-element.312.refs_0_.refs_2_, bf16[512,2112]{1,0:T(8,128)(2,1)S(1)} %get-tuple-element.310.refs_0_.refs_3_), custom_call_target="tpu_custom_call" | custom-call | flops 1824034560 | bytes 1 | tf_op jit(solution)/shard_map/sum_product/pallas_call | solution.py:440
  589.4 7.0 collective-permute-done.25.refs_3_
  601.5 5.6 collective-permute-start.28
  611.8 5.2 first_norms_back.1
  622.2 30.7 %collective-permute-done.28 = bf16[2,176,3072]{2,1,0:T(8,128)(2,1)} collective-permute-done((bf16[2,176,3072]{2,1,0:T(8,128)(2,1)}, bf16[2,176,3072]{2,1,0:T(8,128)(2,1)}, u32[]{:S(2)}, u32[]{:S(2)}) %collective-permute-start.28) | collective-permute-done | bytes 2162720 | tf_op jit(solution)/shard_map/ppermute | solution.py:821
  660.2 21.9 %collective-permute-done.26 = bf16[2,2,176,1408]{3,2,1,0:T(8,128)(2,1)} collective-permute-done((bf16[2,2,176,1408]{3,2,1,0:T(8,128)(2,1)}, bf16[2,2,176,1408]{3,2,1,0:T(8,128)(2,1)}, u32[]{:S(2)}, u32[]{:S(2)}) %collective-permute-start.26) | collective-permute-done | bytes 1982496 | tf_op jit(solution)/shard_map/ppermute | solution.py:701
  686.7 5.5 sum_product.15
  697.9 7.1 sum_product.17
  719.8 5.1 collective-permute-start.41
  748.4 12.1 %collective-permute-done.43 = bf16[1,176,2112]{2,1,0:T(8,128)(2,1)} collective-permute-done((bf16[1,176,2112]{2,1,0:T(8,128)(2,1)}, bf16[1,176,2112]{2,1,0:T(8,128)(2,1)}, u32[]{:S(2)}, u32[]{:S(2)}) %collective-permute-start.43) | collective-permute-done | bytes 743456 | tf_op jit(solution)/shard_map/ppermute | solution.py:701
  822.5 14.0 %collective-permute-start.62 = (bf16[1,176,704]{2,1,0:T(8,128)(2,1)}, bf16[1,176,704]{2,1,0:T(8,128)(2,1)}, u32[]{:S(2)}, u32[]{:S(2)}) collective-permute-start(bf16[1,176,704]{2,1,0:T(8,128)(2,1)} %bitcast_add_fusion.19), channel_id=1, source_target_pairs={{2,18},{6,22},{10,26},{14,30},{16,0},{20,4},{24,8},{28,12},{3,19},... | collective-permute-start | bytes 743432 | tf_op jit(solution)/shard_map/ppermute | solution.py:821
  (818 shorter events, 388.6 us)
Async XLA Ops:
  7.2 169.4 %all-gather.2.cloned.1.call-start = ((), (), s32[]{:S(2)}) async-start(), calls=%async_computation | async-start | bytes 8425472 | tf_op jit(solution)/shard_map/all_gather | solution.py:767
  11.4 47.9 %collective-permute-start = (bf16[704,1408]{1,0:T(8,128)(2,1)}, bf16[704,1408]{1,0:T(8,128)(2,1)}, u32[]{:S(2)}, u32[]{:S(2)}) collective-permute-start(bf16[704,1408]{1,0:T(8,128)(2,1)} %dynamic-slice_bitcast_fusion.8), channel_id=1, source_target_pairs={{0,1},{1,0},{2,3},{3,2},{4,5},{5,4},{6,7},{7,6},{8,9},{9,8},{10,11... | collective-permute-start | bytes 5947400 | tf_op jit(solution)/shard_map/ppermute | solution.py:661
  11.7 27.7 %collective-permute-start.1 = (s32[4]{0:T(128)}, s32[4]{0:T(128)}, u32[]{:S(2)}, u32[]{:S(2)}) collective-permute-start(s32[4]{0:T(128)} %param.36), channel_id=1, source_target_pairs={{0,2},{2,0},{4,6},{6,4},{8,10},{10,8},{12,14},{14,12},{16,18},{18,... | collective-permute-start | bytes 56 | tf_op jit(solution)/shard_map/ppermute | solution.py:701
  60.1 24.0 %collective-permute-start.6 = (bf16[704,1408]{1,0:T(8,128)(2,1)}, bf16[704,1408]{1,0:T(8,128)(2,1)}, u32[]{:S(2)}, u32[]{:S(2)}) collective-permute-start(bf16[704,1408]{1,0:T(8,128)(2,1)} %collective-permute-done.refs_4_), channel_id=1, source_target_pairs={{0,2},{2,0},{4,6},{6,4},{8,10},{10,8},{12,14},{14,12},{16,18},{18,... | collective-permute-start | bytes 5947400 | tf_op jit(solution)/shard_map/ppermute | solution.py:701
  101.4 32.4 %collective-permute-start.7 = (bf16[512,1408]{1,0:T(8,128)(2,1)S(1)}, bf16[512,1408]{1,0:T(8,128)(2,1)S(1)}, u32[]{:S(2)}, u32[]{:S(2)}) collective-permute-start(bf16[512,1408]{1,0:T(8,128)(2,1)S(1)} %get-tuple-element.236.refs_0_), channel_id=1, source_target_pairs={{0,1},{1,0},{2,3},{3,2},{4,5},{5,4},{6,7},{7,6},{8,9},{9,8},{10,11... | collective-permute-start | bytes 4325384 | tf_op jit(solution)/shard_map/ppermute | solution.py:661
  101.8 57.8 %collective-permute-start.9 = (bf16[2,256,1024]{2,1,0:T(8,128)(2,1)S(1)}, bf16[2,256,1024]{2,1,0:T(8,128)(2,1)S(1)}, u32[]{:S(2)}, u32[]{:S(2)}) collective-permute-start(bf16[2,256,1024]{2,1,0:T(8,128)(2,1)S(1)} %constant_dynamic-slice_fusion.5), channel_id=1, source_target_pairs={{0,1},{1,0},{2,3},{3,2},{4,5},{5,4},{6,7},{7,6},{8,9},{9,8},{10,11... | collective-permute-start | bytes 3145736 | tf_op jit(solution)/shard_map/ppermute | solution.py:666
  105.3 54.3 %collective-permute-start.10 = (bf16[2,77,512]{2,0,1:T(2,128)(2,1)S(1)}, bf16[2,77,512]{2,0,1:T(2,128)(2,1)S(1)}, u32[]{:S(2)}, u32[]{:S(2)}) collective-permute-start(bf16[2,77,512]{2,0,1:T(2,128)(2,1)S(1)} %get-tuple-element.448), channel_id=1, source_target_pairs={{0,1},{1,0},{2,3},{3,2},{4,5},{5,4},{6,7},{7,6},{8,9},{9,8},{10,11... | collective-permute-start | bytes 473096 | tf_op jit(solution)/shard_map/ppermute | solution.py:661
  157.2 36.3 %collective-permute-start.8 = (bf16[512,1408]{1,0:T(8,128)(2,1)}, bf16[512,1408]{1,0:T(8,128)(2,1)}, u32[]{:S(2)}, u32[]{:S(2)}) collective-permute-start(bf16[512,1408]{1,0:T(8,128)(2,1)} %product.30), channel_id=1, source_target_pairs={{0,1},{1,0},{2,3},{3,2},{4,5},{5,4},{6,7},{7,6},{8,9},{9,8},{10,11... | collective-permute-start | bytes 4325384 | tf_op jit(solution)/shard_map/ppermute | solution.py:666
  209.0 42.7 %collective-permute-start.13 = (bf16[512,1408]{1,0:T(8,128)(2,1)S(1)}, bf16[512,1408]{1,0:T(8,128)(2,1)S(1)}, u32[]{:S(2)}, u32[]{:S(2)}) collective-permute-start(bf16[512,1408]{1,0:T(8,128)(2,1)S(1)} %copy-done.27), channel_id=1, source_target_pairs={{0,1},{1,0},{2,3},{3,2},{4,5},{5,4},{6,7},{7,6},{8,9},{9,8},{10,11... | collective-permute-start | bytes 4325384 | tf_op jit(solution)/shard_map/ppermute | solution.py:661
  230.1 40.5 %collective-permute-start.12 = (bf16[512,1408]{1,0:T(8,128)(2,1)S(1)}, bf16[512,1408]{1,0:T(8,128)(2,1)S(1)}, u32[]{:S(2)}, u32[]{:S(2)}) collective-permute-start(bf16[512,1408]{1,0:T(8,128)(2,1)S(1)} %get-tuple-element.262.rows_ref.refs_0_), channel_id=1, source_target_pairs={{0,1},{1,0},{2,3},{3,2},{4,5},{5,4},{6,7},{7,6},{8,9},{9,8},{10,11... | collective-permute-start | bytes 4325384 | tf_op jit(solution)/shard_map/ppermute | solution.py:661
  287.3 37.7 %collective-permute-start.14 = (bf16[512,1408]{1,0:T(8,128)(2,1)}, bf16[512,1408]{1,0:T(8,128)(2,1)}, u32[]{:S(2)}, u32[]{:S(2)}) collective-permute-start(bf16[512,1408]{1,0:T(8,128)(2,1)} %product.38), channel_id=1, source_target_pairs={{0,1},{1,0},{2,3},{3,2},{4,5},{5,4},{6,7},{7,6},{8,9},{9,8},{10,11... | collective-permute-start | bytes 4325384 | tf_op jit(solution)/shard_map/ppermute | solution.py:666
  332.6 22.9 %collective-permute-start.16 = (bf16[2,704,3072]{2,1,0:T(8,128)(2,1)}, bf16[2,704,3072]{2,1,0:T(8,128)(2,1)S(1)}, u32[]{:S(2)}, u32[]{:S(2)}) collective-permute-start(bf16[2,704,3072]{2,1,0:T(8,128)(2,1)} %dynamic-slice_bitcast_fusion), channel_id=1, source_target_pairs={{0,2},{2,0},{4,6},{6,4},{8,10},{10,8},{12,14},{14,12},{16,18},{18,... | collective-permute-start | bytes 25952264 | tf_op jit(solution)/shard_map/ppermute | solution.py:701
  364.5 110.5 %collective-permute-start.19 = (bf16[2,2,176,3072]{3,2,1,0:T(8,128)(2,1)}, bf16[2,2,176,3072]{3,2,1,0:T(8,128)(2,1)}, u32[]{:S(2)}, u32[]{:S(2)}) collective-permute-start(bf16[2,2,176,3072]{3,2,1,0:T(8,128)(2,1)} %dynamic-slice_bitcast_fusion.1), channel_id=1, source_target_pairs={{0,4},{2,6},{4,0},{6,2},{8,12},{10,14},{12,8},{14,10},{16,20},{18,... | collective-permute-start | bytes 12976136 | tf_op jit(solution)/shard_map/ppermute | solution.py:701
  364.8 33.0 %collective-permute-start.15 = (bf16[512,1408]{1,0:T(8,128)(2,1)S(1)}, bf16[512,1408]{1,0:T(8,128)(2,1)S(1)}, u32[]{:S(2)}, u32[]{:S(2)}) collective-permute-start(bf16[512,1408]{1,0:T(8,128)(2,1)S(1)} %copy-done.107), channel_id=1, source_target_pairs={{0,1},{1,0},{2,3},{3,2},{4,5},{5,4},{6,7},{7,6},{8,9},{9,8},{10,11... | collective-permute-start | bytes 4325384 | tf_op jit(solution)/shard_map/ppermute | solution.py:666
  366.0 62.7 %collective-permute-start.17 = (bf16[512,1408]{1,0:T(8,128)(2,1)}, bf16[512,1408]{1,0:T(8,128)(2,1)S(1)}, u32[]{:S(2)}, u32[]{:S(2)}) collective-permute-start(bf16[512,1408]{1,0:T(8,128)(2,1)} %copy-done.135), channel_id=1, source_target_pairs={{0,1},{1,0},{2,3},{3,2},{4,5},{5,4},{6,7},{7,6},{8,9},{9,8},{10,11... | collective-permute-start | bytes 4325384 | tf_op jit(solution)/shard_map/ppermute | solution.py:661
  433.0 42.0 %collective-permute-start.18 = (bf16[512,1408]{1,0:T(8,128)(2,1)}, bf16[512,1408]{1,0:T(8,128)(2,1)}, u32[]{:S(2)}, u32[]{:S(2)}) collective-permute-start(bf16[512,1408]{1,0:T(8,128)(2,1)} %get-tuple-element.322.refs_0_), channel_id=1, source_target_pairs={{0,1},{1,0},{2,3},{3,2},{4,5},{5,4},{6,7},{7,6},{8,9},{9,8},{10,11... | collective-permute-start | bytes 4325384 | tf_op jit(solution)/shard_map/ppermute | solution.py:661
  487.4 19.2 %collective-permute-start.20 = (bf16[2,704,1408]{2,1,0:T(8,128)(2,1)S(1)}, bf16[2,704,1408]{2,1,0:T(8,128)(2,1)}, u32[]{:S(2)}, u32[]{:S(2)}) collective-permute-start(bf16[2,704,1408]{2,1,0:T(8,128)(2,1)S(1)} %dynamic-slice_bitcast_fusion.2), channel_id=1, source_target_pairs={{0,2},{2,0},{4,6},{6,4},{8,10},{10,8},{12,14},{14,12},{16,18},{18,... | collective-permute-start | bytes 11894792 | tf_op jit(solution)/shard_map/ppermute | solution.py:701
  495.8 49.5 %collective-permute-start.22 = (bf16[2,176,3072]{2,1,0:T(8,128)(2,1)}, bf16[2,176,3072]{2,1,0:T(8,128)(2,1)}, u32[]{:S(2)}, u32[]{:S(2)}) collective-permute-start(bf16[2,176,3072]{2,1,0:T(8,128)(2,1)} %dynamic-slice_bitcast_fusion.5), channel_id=1, source_target_pairs={{0,8},{2,10},{4,12},{6,14},{8,0},{10,2},{12,4},{14,6},{16,24},{18,... | collective-permute-start | bytes 6488072 | tf_op jit(solution)/shard_map/ppermute | solution.py:701
  496.0 52.7 %collective-permute-start.23 = (bf16[2,256,1024]{2,1,0:T(8,128)(2,1)S(1)}, bf16[2,256,1024]{2,1,0:T(8,128)(2,1)S(1)}, u32[]{:S(2)}, u32[]{:S(2)}) collective-permute-start(bf16[2,256,1024]{2,1,0:T(8,128)(2,1)S(1)} %slice.231), channel_id=1, source_target_pairs={{0,1},{1,0},{2,3},{3,2},{4,5},{5,4},{6,7},{7,6},{8,9},{9,8},{10,11... | collective-permute-start | bytes 3145736 | tf_op jit(solution)/shard_map/ppermute | solution.py:666
  496.2 52.5 %collective-permute-start.24 = (bf16[2,77,512]{2,0,1:T(2,128)(2,1)S(1)}, bf16[2,77,512]{2,0,1:T(2,128)(2,1)S(1)}, u32[]{:S(2)}, u32[]{:S(2)}) collective-permute-start(bf16[2,77,512]{2,0,1:T(2,128)(2,1)S(1)} %copy.78), channel_id=1, source_target_pairs={{0,1},{1,0},{2,3},{3,2},{4,5},{5,4},{6,7},{7,6},{8,9},{9,8},{10,11... | collective-permute-start | bytes 473096 | tf_op jit(solution)/shard_map/ppermute | solution.py:666
  564.1 32.3 %collective-permute-start.25 = (bf16[512,1408]{1,0:T(8,128)(2,1)S(1)}, bf16[512,1408]{1,0:T(8,128)(2,1)S(1)}, u32[]{:S(2)}, u32[]{:S(2)}) collective-permute-start(bf16[512,1408]{1,0:T(8,128)(2,1)S(1)} %product.45), channel_id=1, source_target_pairs={{0,1},{1,0},{2,3},{3,2},{4,5},{5,4},{6,7},{7,6},{8,9},{9,8},{10,11... | collective-permute-start | bytes 4325384 | tf_op jit(solution)/shard_map/ppermute | solution.py:666
  598.3 20.6 %collective-permute-start.29 = (bf16[1,704,2112]{2,1,0:T(8,128)(2,1)}, bf16[1,704,2112]{2,1,0:T(8,128)(2,1)}, u32[]{:S(2)}, u32[]{:S(2)}) collective-permute-start(bf16[1,704,2112]{2,1,0:T(8,128)(2,1)} %dynamic-slice_bitcast_fusion.3), channel_id=1, source_target_pairs={{0,2},{2,0},{4,6},{6,4},{8,10},{10,8},{12,14},{14,12},{16,18},{18,... | collective-permute-start | bytes 8921096 | tf_op jit(solution)/shard_map/ppermute | solution.py:701
  601.5 51.4 %collective-permute-start.28 = (bf16[2,176,3072]{2,1,0:T(8,128)(2,1)}, bf16[2,176,3072]{2,1,0:T(8,128)(2,1)}, u32[]{:S(2)}, u32[]{:S(2)}) collective-permute-start(bf16[2,176,3072]{2,1,0:T(8,128)(2,1)} %bitcast_add_fusion.5), channel_id=1, source_target_pairs={{2,18},{6,22},{10,26},{14,30},{16,0},{20,4},{24,8},{28,12},{3,19},... | collective-permute-start | bytes 6488072 | tf_op jit(solution)/shard_map/ppermute | solution.py:821
  609.8 48.6 %collective-permute-start.27 = (bf16[1,2,128,2816]{3,2,1,0:T(8,128)(2,1)}, bf16[1,2,128,2816]{3,2,1,0:T(8,128)(2,1)}, u32[]{:S(2)}, u32[]{:S(2)}) collective-permute-start(bf16[1,2,128,2816]{3,2,1,0:T(8,128)(2,1)} %dynamic-slice_bitcast_fusion.10), channel_id=1, source_target_pairs={{0,4},{2,6},{4,0},{6,2},{8,12},{10,14},{12,8},{14,10},{16,20},{18,... | collective-permute-start | bytes 4325384 | tf_op jit(solution)/shard_map/ppermute | solution.py:701
  611.1 71.0 %collective-permute-start.26 = (bf16[2,2,176,1408]{3,2,1,0:T(8,128)(2,1)}, bf16[2,2,176,1408]{3,2,1,0:T(8,128)(2,1)}, u32[]{:S(2)}, u32[]{:S(2)}) collective-permute-start(bf16[2,2,176,1408]{3,2,1,0:T(8,128)(2,1)} %dynamic-slice_bitcast_fusion.7), channel_id=1, source_target_pairs={{0,4},{2,6},{4,0},{6,2},{8,12},{10,14},{12,8},{14,10},{16,20},{18,... | collective-permute-start | bytes 5947400 | tf_op jit(solution)/shard_map/ppermute | solution.py:701
  617.0 80.8 %collective-permute-start.30 = (bf16[512,1408]{1,0:T(8,128)(2,1)S(1)}, bf16[512,1408]{1,0:T(8,128)(2,1)}, u32[]{:S(2)}, u32[]{:S(2)}) collective-permute-start(bf16[512,1408]{1,0:T(8,128)(2,1)S(1)} %get-tuple-element.334.refs_0_), channel_id=1, source_target_pairs={{0,1},{1,0},{2,3},{3,2},{4,5},{5,4},{6,7},{7,6},{8,9},{9,8},{10,11... | collective-permute-start | bytes 4325384 | tf_op jit(solution)/shard_map/ppermute | solution.py:661
  660.2 49.8 %collective-permute-start.36 = (bf16[1,128,2816]{2,1,0:T(8,128)(2,1)S(1)}, bf16[1,128,2816]{2,1,0:T(8,128)(2,1)S(1)}, u32[]{:S(2)}, u32[]{:S(2)}) collective-permute-start(bf16[1,128,2816]{2,1,0:T(8,128)(2,1)S(1)} %dynamic-slice_bitcast_fusion.17), channel_id=1, source_target_pairs={{0,8},{2,10},{4,12},{6,14},{8,0},{10,2},{12,4},{14,6},{16,24},{18,... | collective-permute-start | bytes 2162696 | tf_op jit(solution)/shard_map/ppermute | solution.py:701
  684.1 26.9 %collective-permute-start.35 = (bf16[2,176,1408]{2,1,0:T(8,128)(2,1)S(1)}, bf16[2,176,1408]{2,1,0:T(8,128)(2,1)S(1)}, u32[]{:S(2)}, u32[]{:S(2)}) collective-permute-start(bf16[2,176,1408]{2,1,0:T(8,128)(2,1)S(1)} %dynamic-slice_bitcast_fusion.15), channel_id=1, source_target_pairs={{0,8},{2,10},{4,12},{6,14},{8,0},{10,2},{12,4},{14,6},{16,24},{18,... | collective-permute-start | bytes 2973704 | tf_op jit(solution)/shard_map/ppermute | solution.py:701
  685.5 32.7 %collective-permute-start.34 = (bf16[1,2,176,2112]{3,2,1,0:T(8,128)(2,1)S(1)}, bf16[1,2,176,2112]{3,2,1,0:T(8,128)(2,1)S(1)}, u32[]{:S(2)}, u32[]{:S(2)}) collective-permute-start(bf16[1,2,176,2112]{3,2,1,0:T(8,128)(2,1)S(1)} %dynamic-slice_bitcast_fusion.9), channel_id=1, source_target_pairs={{0,4},{2,6},{4,0},{6,2},{8,12},{10,14},{12,8},{14,10},{16,20},{18,... | collective-permute-start | bytes 4460552 | tf_op jit(solution)/shard_map/ppermute | solution.py:701
  710.0 19.6 %collective-permute-start.31 = (bf16[1,512,1024]{2,1,0:T(8,128)(2,1)S(1)}, bf16[1,512,1024]{2,1,0:T(8,128)(2,1)S(1)}, u32[]{:S(2)}, u32[]{:S(2)}) collective-permute-start(bf16[1,512,1024]{2,1,0:T(8,128)(2,1)S(1)} %dynamic-slice_bitcast_fusion.13), channel_id=1, source_target_pairs={{0,2},{2,0},{4,6},{6,4},{8,10},{10,8},{12,14},{14,12},{16,18},{18,... | collective-permute-start | bytes 3145736 | tf_op jit(solution)/shard_map/ppermute | solution.py:701
  711.0 33.2 %collective-permute-start.44 = (bf16[2,88,3072]{2,1,0:T(8,128)(2,1)}, bf16[2,88,3072]{2,1,0:T(8,128)(2,1)}, u32[]{:S(2)}, u32[]{:S(2)}) collective-permute-start(bf16[2,88,3072]{2,1,0:T(8,128)(2,1)} %dynamic-slice_bitcast_fusion.12), channel_id=1, source_target_pairs={{0,2},{4,6},{8,10},{12,14},{18,16},{22,20},{26,24},{30,28},{1,3},{... | collective-permute-start | bytes 3244040 | tf_op jit(solution)/shard_map/ppermute | solution.py:825
  718.2 61.0 %collective-permute-start.39 = (f32[8032]{0:T(1024)S(1)}, f32[8032]{0:T(1024)S(1)}, u32[]{:S(2)}, u32[]{:S(2)}) collective-permute-start(f32[8032]{0:T(1024)S(1)} %concatenate.228), channel_id=1, source_target_pairs={{0,2},{2,0},{4,6},{6,4},{8,10},{10,8},{12,14},{14,12},{16,18},{18,... | collective-permute-start | bytes 96392 | tf_op jit(solution)/shard_map/ppermute | solution.py:701
  719.8 50.8 %collective-permute-start.41 = (bf16[1,128,2816]{2,1,0:T(8,128)(2,1)}, bf16[1,128,2816]{2,1,0:T(8,128)(2,1)}, u32[]{:S(2)}, u32[]{:S(2)}) collective-permute-start(bf16[1,128,2816]{2,1,0:T(8,128)(2,1)} %bitcast_add_fusion.15), channel_id=1, source_target_pairs={{2,18},{6,22},{10,26},{14,30},{16,0},{20,4},{24,8},{28,12},{3,19},... | collective-permute-start | bytes 2162696 | tf_op jit(solution)/shard_map/ppermute | solution.py:821
  726.3 48.8 %collective-permute-start.40 = (bf16[2,176,1408]{2,1,0:T(8,128)(2,1)}, bf16[2,176,1408]{2,1,0:T(8,128)(2,1)}, u32[]{:S(2)}, u32[]{:S(2)}) collective-permute-start(bf16[2,176,1408]{2,1,0:T(8,128)(2,1)} %bitcast_add_fusion.13), channel_id=1, source_target_pairs={{2,18},{6,22},{10,26},{14,30},{16,0},{20,4},{24,8},{28,12},{3,19},... | collective-permute-start | bytes 2973704 | tf_op jit(solution)/shard_map/ppermute | solution.py:821
  729.5 31.0 %collective-permute-start.43 = (bf16[1,176,2112]{2,1,0:T(8,128)(2,1)}, bf16[1,176,2112]{2,1,0:T(8,128)(2,1)}, u32[]{:S(2)}, u32[]{:S(2)}) collective-permute-start(bf16[1,176,2112]{2,1,0:T(8,128)(2,1)} %dynamic-slice_bitcast_fusion.16), channel_id=1, source_target_pairs={{0,8},{2,10},{4,12},{6,14},{8,0},{10,2},{12,4},{14,6},{16,24},{18,... | collective-permute-start | bytes 2230280 | tf_op jit(solution)/shard_map/ppermute | solution.py:701
  744.3 24.0 %collective-permute-start.42 = (bf16[1,2,176,1408]{3,2,1,0:T(8,128)(2,1)S(1)}, bf16[1,2,176,1408]{3,2,1,0:T(8,128)(2,1)S(1)}, u32[]{:S(2)}, u32[]{:S(2)}) collective-permute-start(bf16[1,2,176,1408]{3,2,1,0:T(8,128)(2,1)S(1)} %copy-done.163), channel_id=1, source_target_pairs={{0,4},{2,6},{4,0},{6,2},{8,12},{10,14},{12,8},{14,10},{16,20},{18,... | collective-permute-start | bytes 2973704 | tf_op jit(solution)/shard_map/ppermute | solution.py:701
  760.5 24.4 %collective-permute-start.38 = (bf16[1,2,176,704]{3,2,1,0:T(8,128)(2,1)S(1)}, bf16[1,2,176,704]{3,2,1,0:T(8,128)(2,1)S(1)}, u32[]{:S(2)}, u32[]{:S(2)}) collective-permute-start(bf16[1,2,176,704]{3,2,1,0:T(8,128)(2,1)S(1)} %copy-done.164), channel_id=1, source_target_pairs={{0,4},{2,6},{4,0},{6,2},{8,12},{10,14},{12,8},{14,10},{16,20},{18,... | collective-permute-start | bytes 1486856 | tf_op jit(solution)/shard_map/ppermute | solution.py:701
  768.3 20.1 %collective-permute-start.37 = (bf16[1,2,128,1024]{3,2,1,0:T(8,128)(2,1)S(1)}, bf16[1,2,128,1024]{3,2,1,0:T(8,128)(2,1)S(1)}, u32[]{:S(2)}, u32[]{:S(2)}) collective-permute-start(bf16[1,2,128,1024]{3,2,1,0:T(8,128)(2,1)S(1)} %copy-done.165), channel_id=1, source_target_pairs={{0,8},{2,10},{4,12},{6,14},{8,0},{10,2},{12,4},{14,6},{16,24},{18,... | collective-permute-start | bytes 1572872 | tf_op jit(solution)/shard_map/ppermute | solution.py:701
  770.6 46.2 %collective-permute-start.48 = (bf16[1,176,2112]{2,1,0:T(8,128)(2,1)}, bf16[1,176,2112]{2,1,0:T(8,128)(2,1)}, u32[]{:S(2)}, u32[]{:S(2)}) collective-permute-start(bf16[1,176,2112]{2,1,0:T(8,128)(2,1)} %bitcast_add_fusion.14), channel_id=1, source_target_pairs={{2,18},{6,22},{10,26},{14,30},{16,0},{20,4},{24,8},{28,12},{3,19},... | collective-permute-start | bytes 2230280 | tf_op jit(solution)/shard_map/ppermute | solution.py:821
  777.9 44.6 %collective-permute-start.64 = (bf16[2,88,1408]{2,1,0:T(8,128)(2,1)}, bf16[2,88,1408]{2,1,0:T(8,128)(2,1)}, u32[]{:S(2)}, u32[]{:S(2)}) collective-permute-start(bf16[2,88,1408]{2,1,0:T(8,128)(2,1)} %dynamic-slice_bitcast_fusion.20), channel_id=1, source_target_pairs={{0,2},{4,6},{8,10},{12,14},{18,16},{22,20},{26,24},{30,28},{1,3},{... | collective-permute-start | bytes 1486856 | tf_op jit(solution)/shard_map/ppermute | solution.py:825
  779.2 33.5 %collective-permute-start.68 = (bf16[1,64,2816]{2,1,0:T(8,128)(2,1)}, bf16[1,64,2816]{2,1,0:T(8,128)(2,1)}, u32[]{:S(2)}, u32[]{:S(2)}) collective-permute-start(bf16[1,64,2816]{2,1,0:T(8,128)(2,1)} %dynamic-slice_bitcast_fusion.24), channel_id=1, source_target_pairs={{0,2},{4,6},{8,10},{12,14},{18,16},{22,20},{26,24},{30,28},{1,3},{... | collective-permute-start | bytes 1081352 | tf_op jit(solution)/shard_map/ppermute | solution.py:825
  812.7 25.1 %collective-permute-start.46 = (bf16[1,128,1024]{2,1,0:T(8,128)(2,1)S(1)}, bf16[1,128,1024]{2,1,0:T(8,128)(2,1)S(1)}, u32[]{:S(2)}, u32[]{:S(2)}) collective-permute-start(bf16[1,128,1024]{2,1,0:T(8,128)(2,1)S(1)} %copy-done.170), channel_id=1, source_target_pairs={{0,4},{2,6},{4,0},{6,2},{8,12},{10,14},{12,8},{14,10},{16,20},{18,... | collective-permute-start | bytes 786440 | tf_op jit(solution)/shard_map/ppermute | solution.py:701
  814.7 29.5 %collective-permute-start.60 = (f32[64,1408]{1,0:T(8,128)S(1)}, f32[64,1408]{1,0:T(8,128)S(1)}, u32[]{:S(2)}, u32[]{:S(2)}) collective-permute-start(f32[64,1408]{1,0:T(8,128)S(1)} %fusion.64), channel_id=1, source_target_pairs={{0,1},{1,0},{2,3},{3,2},{4,5},{5,4},{6,7},{7,6},{8,9},{9,8},{10,11... | collective-permute-start | bytes 1081352 | tf_op jit(solution)/shard_map/ppermute | solution.py:701
  816.8 31.3 %collective-permute-start.69 = (bf16[64,1408]{1,0:T(8,128)(2,1)S(1)}, bf16[64,1408]{1,0:T(8,128)(2,1)S(1)}, u32[]{:S(2)}, u32[]{:S(2)}) collective-permute-start(bf16[64,1408]{1,0:T(8,128)(2,1)S(1)} %slice.195), channel_id=1, source_target_pairs={{0,1},{1,0},{2,3},{3,2},{4,5},{5,4},{6,7},{7,6},{8,9},{9,8},{10,11... | collective-permute-start | bytes 540680 | tf_op jit(solution)/shard_map/ppermute | solution.py:666
  820.5 41.5 %collective-permute-start.61 = (bf16[1,88,2112]{2,1,0:T(8,128)(2,1)}, bf16[1,88,2112]{2,1,0:T(8,128)(2,1)}, u32[]{:S(2)}, u32[]{:S(2)}) collective-permute-start(bf16[1,88,2112]{2,1,0:T(8,128)(2,1)} %dynamic-slice_bitcast_fusion.23), channel_id=1, source_target_pairs={{0,2},{4,6},{8,10},{12,14},{18,16},{22,20},{26,24},{30,28},{1,3},{... | collective-permute-start | bytes 1115144 | tf_op jit(solution)/shard_map/ppermute | solution.py:825
  822.5 34.6 %collective-permute-start.62 = (bf16[1,176,704]{2,1,0:T(8,128)(2,1)}, bf16[1,176,704]{2,1,0:T(8,128)(2,1)}, u32[]{:S(2)}, u32[]{:S(2)}) collective-permute-start(bf16[1,176,704]{2,1,0:T(8,128)(2,1)} %bitcast_add_fusion.19), channel_id=1, source_target_pairs={{2,18},{6,22},{10,26},{14,30},{16,0},{20,4},{24,8},{28,12},{3,19},... | collective-permute-start | bytes 743432 | tf_op jit(solution)/shard_map/ppermute | solution.py:821
  838.6 20.9 %collective-permute-start.66 = (bf16[1,128,1024]{2,1,0:T(8,128)(2,1)S(1)}, bf16[1,128,1024]{2,1,0:T(8,128)(2,1)}, u32[]{:S(2)}, u32[]{:S(2)}) collective-permute-start(bf16[1,128,1024]{2,1,0:T(8,128)(2,1)S(1)} %bitcast_add_fusion.20), channel_id=1, source_target_pairs={{2,18},{6,22},{10,26},{14,30},{16,0},{20,4},{24,8},{28,12},{3,19},... | collective-permute-start | bytes 786440 | tf_op jit(solution)/shard_map/ppermute | solution.py:821
  844.2 19.7 %collective-permute-start.50 = (bf16[1,176,1408]{2,1,0:T(8,128)(2,1)}, bf16[1,176,1408]{2,1,0:T(8,128)(2,1)}, u32[]{:S(2)}, u32[]{:S(2)}) collective-permute-start(bf16[1,176,1408]{2,1,0:T(8,128)(2,1)} %bitcast_add_fusion.18), channel_id=1, source_target_pairs={{2,18},{6,22},{10,26},{14,30},{16,0},{20,4},{24,8},{28,12},{3,19},... | collective-permute-start | bytes 1486856 | tf_op jit(solution)/shard_map/ppermute | solution.py:821
  (255 other events, 2033.2 us)
Sparse Core Ops, SparseCore 0:
  84.2 72.2 all-gather.1

commit v3 on v2

--- a/solution.py
+++ b/solution.py
@@ -1,3 +1,4 @@
+import copy
 import functools
 import math
 
@@ -25,6 +26,7 @@
 
 
 SCALE_FLOPS = 2e8
+EACH_BACK = 2
 
 
 def effort(us):
@@ -99,9 +101,11 @@
         if kind != "v":
             extras[kind] = refs[place]
             place += 1
+    normed_kinds = [number for number, kind in enumerate(kinds) if kind != "v"]
     if chained:
-        place += len(kinds)
-    outs = refs[place:]
+        place += len(kinds) + len(normed_kinds)
+    outs = refs[place : place + len(kinds)]
+    keeps = dict(zip(normed_kinds, refs[place + len(kinds) :]))
     part = min(64, pre_ref.shape[0])
     lane = lanes_of((part, LANES))
     ones = jnp.where((lane == HEAD_DIM) | (lane == HEAD_DIM + 1), 1.0, 0.0)
@@ -115,7 +119,11 @@
                 if kind == "v":
                     outs[number][head, span, :] = (values + ones).astype(jnp.bfloat16)
                     continue
-                normed, _ = head_norm(values)
+                normed, spread = head_norm(values)
+                high = spread.astype(jnp.bfloat16).astype(jnp.float32)
+                kept = jnp.where(lane == HEAD_DIM, high, normed)
+                kept = jnp.where(lane == HEAD_DIM + 1, spread - high, kept)
+                keeps[number][head, span, :] = kept.astype(jnp.bfloat16)
                 normed = normed * gain_ref[number : number + 1, :]
                 if roped:
                     normed = turn(normed, rope)
@@ -149,12 +157,14 @@
             aliases[len(operands)] = number
             operands.append(array)
             in_specs.append(pl.BlockSpec(memory_space=pl.ANY))
+    out_columns = columns + [cols for kind, cols in zip(kinds, columns) if kind != "v"]
     out_shape = [
-        jax.ShapeDtypeStruct((len(cols), blocks * rows, LANES), jnp.bfloat16) for cols in columns
+        jax.ShapeDtypeStruct((len(cols), blocks * rows, LANES), jnp.bfloat16)
+        for cols in out_columns
     ]
     out_specs = [
         pl.BlockSpec((len(cols), tile, LANES), lambda i: (0, block * tiles + i, 0))
-        for cols in columns
+        for cols in out_columns
     ]
     heads = sum(len(cols) for cols in columns)
     return pl.pallas_call(
@@ -177,14 +187,18 @@
 
 
 def join_kernel(*refs, kinds, columns, roped):
-    pre_ref, gain_ref = refs[:2]
-    place = 2
+    gain_ref = refs[0]
+    place = 1
     if roped:
         rope_ref = refs[place]
         place += 1
     grads = refs[place : place + len(kinds)]
-    out_ref, sum_ref = refs[place + len(kinds) :]
-    part = min(256, pre_ref.shape[0])
+    place += len(kinds)
+    normed_kinds = [number for number, kind in enumerate(kinds) if kind != "v"]
+    keeps = dict(zip(normed_kinds, refs[place : place + len(normed_kinds)]))
+    out_ref, sum_ref = refs[place + len(normed_kinds) :]
+    rows = out_ref.shape[0]
+    part = min(256, rows)
     inside = lanes_of((part, LANES)) < HEAD_DIM
 
     @pl.when(pl.program_id(0) == 0)
@@ -197,17 +211,23 @@
         for number, kind in enumerate(kinds):
             total = jnp.zeros((part, LANES), jnp.float32)
             for head, offset in enumerate(columns[number]):
-                slope = jnp.where(inside, grads[number][head, span, :], 0.0)
+                slope = grads[number][head, span, :].astype(jnp.float32)
                 if kind != "v":
+                    slope = jnp.where(inside, slope, 0.0)
                     slope = slope * (SCALE if kind == "q" else KEY_BACK)
                     if roped:
                         slope = turn_back(slope, rope)
-                    values = pre_ref[span, offset : offset + HEAD_DIM].astype(jnp.float32)
-                    normed, spread = head_norm(widen(values))
-                    total = total + slope * normed
-                    slope = slope * gain_ref[number : number + 1, :]
+                    normed = keeps[number][head, span, :].astype(jnp.float32)
+                    spread = (
+                        normed[:, HEAD_DIM : HEAD_DIM + 1]
+                        + normed[:, HEAD_DIM + 1 : HEAD_DIM + 2]
+                    )
+                    product = slope * normed
+                    total = total + product
+                    gain = gain_ref[number : number + 1, :]
+                    slope = slope * gain
                     mean = lane_mean(slope, True)
-                    mixed = lane_mean(slope * normed, False)
+                    mixed = lane_mean(product * gain, False)
                     slope = (slope - mean - normed * mixed) * spread
                 pieces[offset] = slope[:, :HEAD_DIM]
             if kind != "v":
@@ -216,22 +236,20 @@
             [pieces[offset] for offset in sorted(pieces)], 1
         ).astype(jnp.bfloat16)
 
-    by_parts(pre_ref.shape[0], part, rows_of)
-
-
-def join_heads(pre, gains, kinds, columns, grads, rope=None, block=0):
-    rows, width = pre.shape
+    by_parts(rows, part, rows_of)
+
+
+def join_heads(keeps, gains, kinds, columns, grads, rope=None, block=0, blocks=1):
+    rows = keeps[0].shape[1] // blocks
+    width = HEAD_DIM * sum(len(cols) for cols in columns)
     tile = min(256, rows)
     tiles = rows // tile
-    operands = [pre, gains]
-    in_specs = [
-        pl.BlockSpec((tile, width), lambda i: (i, 0)),
-        pl.BlockSpec((8, LANES), lambda i: (0, 0)),
-    ]
+    operands = [gains]
+    in_specs = [pl.BlockSpec((8, LANES), lambda i: (0, 0))]
     if rope is not None:
         operands.append(rope)
         in_specs.append(pl.BlockSpec((tile, 3 * LANES), lambda i: (block * tiles + i, 0)))
-    for array in grads:
+    for array in list(grads) + list(keeps):
         operands.append(array)
         in_specs.append(
             pl.BlockSpec((array.shape[0], tile, LANES), lambda i: (0, block * tiles + i, 0))
@@ -292,7 +310,7 @@
     heads, rows_all, _ = queries.shape
     rows = rows_all // blocks
     tiles = rows // tile
-    each = 2 if heads % 2 == 0 else 1
+    each = 4 if heads % 4 == 0 else 1
     there = lambda i, h, pick: (h, block * tiles + i, 0)
     keyed = lambda i, h, pick: (h, pick[i], 0)
     chained = [] if earlier is None else [earlier]
@@ -364,31 +382,47 @@
     )(*operands)
 
 
-def attend_back_kernel(pick, q_ref, k_ref, v_ref, g_ref, dq_ref, dk_ref, dv_ref, *, key_rows):
+def attend_back_kernel(
+    pick, q_ref, k_ref, v_ref, g_ref, dq_ref, dk_ref, dv_ref, key_sum, value_sum, *, key_rows
+):
     tile = pl.program_id(1)
-    queries, keys, slopes = q_ref[0], k_ref[0], g_ref[0]
-    scores = lax.dot_general(keys, queries, ROW_TIMES_ROW, preferred_element_type=jnp.float32)
-    weights = jnp.exp2(scores)
-    pulls = lax.dot_general(v_ref[0], slopes, ROW_TIMES_ROW, preferred_element_type=jnp.float32)
-    pulls = (weights * pulls).astype(jnp.bfloat16)
-    value_grad = jnp.dot(weights.astype(jnp.bfloat16), slopes, preferred_element_type=jnp.float32)
-    key_grad = jnp.dot(pulls, queries, preferred_element_type=jnp.float32)
-    dq_ref[0] = lax.dot_general(pulls, keys, COL_TIMES_COL, preferred_element_type=jnp.float32)
 
     @pl.when(tile == 0)
     def _():
-        dk_ref[...] = jnp.zeros_like(dk_ref)
-        dv_ref[...] = jnp.zeros_like(dv_ref)
+        key_sum[...] = jnp.zeros_like(key_sum)
+        value_sum[...] = jnp.zeros_like(value_sum)
 
     start = pl.multiple_of(pick[tile] * key_rows, key_rows)
-    dk_ref[0, pl.ds(start, key_rows), :] += key_grad
-    dv_ref[0, pl.ds(start, key_rows), :] += value_grad
+    for head in range(q_ref.shape[0]):
+        queries, keys, slopes = q_ref[head], k_ref[head], g_ref[head]
+        scores = lax.dot_general(keys, queries, ROW_TIMES_ROW, preferred_element_type=jnp.float32)
+        weights = jnp.exp2(scores)
+        pulls = lax.dot_general(
+            v_ref[head], slopes, ROW_TIMES_ROW, preferred_element_type=jnp.float32
+        )
+        pulls = (weights * pulls).astype(jnp.bfloat16)
+        value_sum[head, pl.ds(start, key_rows), :] += jnp.dot(
+            weights.astype(jnp.bfloat16), slopes, preferred_element_type=jnp.float32
+        )
+        key_sum[head, pl.ds(start, key_rows), :] += jnp.dot(
+            pulls, queries, preferred_element_type=jnp.float32
+        )
+        query_grad = lax.dot_general(
+            pulls, keys, COL_TIMES_COL, preferred_element_type=jnp.float32
+        )
+        dq_ref[head] = query_grad.astype(jnp.bfloat16)
+
+    @pl.when(tile == pl.num_programs(1) - 1)
+    def _():
+        dk_ref[...] = key_sum[...].astype(jnp.bfloat16)
+        dv_ref[...] = value_sum[...].astype(jnp.bfloat16)
 
 
 def attend_back(queries, keys, values, slopes, pick, tile, key_rows):
     heads, rows, _ = queries.shape
     all_keys = keys.shape[1]
     tiles = rows // tile
+    each = EACH_BACK if heads % EACH_BACK == 0 else 1
     there = lambda h, i, pick: (h, i, 0)
     keyed = lambda h, i, pick: (h, pick[i], 0)
     whole = lambda h, i, pick: (h, 0, 0)
@@ -396,23 +430,24 @@
         functools.partial(attend_back_kernel, key_rows=key_rows),
         grid_spec=pltpu.PrefetchScalarGridSpec(
             num_scalar_prefetch=1,
-            grid=(heads, tiles),
+            grid=(heads // each, tiles),
             in_specs=[
-                pl.BlockSpec((1, tile, LANES), there),
-                pl.BlockSpec((1, key_rows, LANES), keyed),
-                pl.BlockSpec((1, key_rows, LANES), keyed),
-                pl.BlockSpec((1, tile, LANES), there),
+                pl.BlockSpec((each, tile, LANES), there),
+                pl.BlockSpec((each, key_rows, LANES), keyed),
+                pl.BlockSpec((each, key_rows, LANES), keyed),
+                pl.BlockSpec((each, tile, LANES), there),
             ],
             out_specs=[
-                pl.BlockSpec((1, tile, LANES), there),
-                pl.BlockSpec((1, all_keys, LANES), whole),
-                pl.BlockSpec((1, all_keys, LANES), whole),
+                pl.BlockSpec((each, tile, LANES), there),
+                pl.BlockSpec((each, all_keys, LANES), whole),
+                pl.BlockSpec((each, all_keys, LANES), whole),
             ],
+            scratch_shapes=[pltpu.VMEM((each, all_keys, LANES), jnp.float32)] * 2,
         ),
         out_shape=[
-            jax.ShapeDtypeStruct((heads, rows, LANES), jnp.float32),
-            jax.ShapeDtypeStruct((heads, all_keys, LANES), jnp.float32),
-            jax.ShapeDtypeStruct((heads, all_keys, LANES), jnp.float32),
+            jax.ShapeDtypeStruct((heads, rows, LANES), jnp.bfloat16),
+            jax.ShapeDtypeStruct((heads, all_keys, LANES), jnp.bfloat16),
+            jax.ShapeDtypeStruct((heads, all_keys, LANES), jnp.bfloat16),
         ],
         compiler_params=params("arbitrary", "arbitrary"),
         cost_estimate=effort(heads * rows * key_rows * 3.5e-6),
@@ -745,26 +780,25 @@
     return [(unsigned(bit), unsigned(1 - bit), bit == 0) for bit in bits]
 
 
+def gather_step(values, came, bit, spot):
+    return jnp.where(
+        spot.bits[bit][2],
+        jnp.concatenate([values, came], 0),
+        jnp.concatenate([came, values], 0),
+    )
+
+
 def gather_rows(values, axis, spot):
     if not power_of_two(axis):
         return lax.all_gather(values, axis, axis=0, tiled=True)
     for bit in range(lax.axis_size(axis).bit_length() - 1):
-        came = swap_bit(values, axis, bit)
-        values = jnp.where(
-            spot.bits[bit][2],
-            jnp.concatenate([values, came], 0),
-            jnp.concatenate([came, values], 0),
-        )
+        values = gather_step(values, swap_bit(values, axis, bit), bit, spot)
     return values
 
 
-def gather_weight(half, earlier, hold, spot):
-    size = lax.axis_size("seq")
-    if size == 1:
-        return []
+def send_piece(half, spot):
     piece = pick_at(half.reshape(lax.axis_size("dp"), -1, half.shape[1]), spot.place, 0)
-    pieces = [from_back(after(piece, *earlier), step) for step in range(1, size)]
-    return [lax.all_gather(after(one, *hold), "dp", axis=0, tiled=True) for one in pieces]
+    return [from_back(piece, step) for step in range(1, lax.axis_size("seq"))]
 
 
 def core_half(half, spot):
@@ -777,6 +811,10 @@
         jnp.concatenate([mine, other], 0),
         jnp.concatenate([other, mine], 0),
     )
+
+
+def scatter_rows(grad):
+    return lax.psum_scatter(grad[0], "dp", scatter_dimension=0, tiled=True)
 
 
 class Summing:
@@ -824,6 +862,15 @@
             self.split(held.reshape(self.groups, 2, self.rows, self.width), 1, 0)
             self.came = lax.ppermute(self.sent, "dp", [(i, i ^ 1) for i in owners])
         return self
+
+    def fork(self):
+        forks = []
+        for group in range(self.groups):
+            one = copy.copy(self)
+            one.groups, one.bits, one.left = 1, list(self.bits), list(self.left)
+            one.keep, one.came = self.keep[group : group + 1], self.came[group : group + 1]
+            forks.append(one)
+        return forks
 
     def finish(self, *hold):
         while self.stage <= self.top:
@@ -1065,20 +1112,16 @@
     lefts, rights = [chunk[0]], [skip_weight]
     for step in range(1, size):
         lefts += [cut_at(chunk[step], side, half_depth, 1) for side in spot.sides]
-    skip_pieces = [after(block, partial, shifts, active_slopes[0], *tables, *lefts) for block in skip_pieces]
+    spare = width - text_width
+    cross_rows = jnp.concatenate([cq_own, cross_out, jnp.pad(kv_own, ((0, 0), (0, spare)))], 0)
+    cross_pieces = send_piece(after(cross_rows, rope), spot)
+    skip_pieces = [
+        after(block, partial, shifts, active_slopes[0], cross_rows, *tables, *lefts)
+        for block in skip_pieces
+    ]
     skip_others = [swap_bit(piece, "dp", 0) for piece in skip_pieces]
     for mine, other in zip(skip_pieces, skip_others):
         rights += [mine, other]
-    spare = width - text_width
-    cross_rows = jnp.concatenate([cq_own, cross_out, jnp.pad(kv_own, ((0, 0), (0, spare)))], 0)
-    cross_blocks = [cross_rows] + gather_weight(cross_rows, skip_pieces, skip_others, spot)
-    cq_full = jnp.concatenate([block[:local_width] for block in cross_blocks], 0)
-    co_full = jnp.concatenate(
-        [block[local_width : 2 * local_width] for block in cross_blocks], 0
-    )
-    kv_full = jnp.concatenate(
-        [block[2 * local_width :, :text_width] for block in cross_blocks], 0
-    )
 
 
     text_terms = [cut_at(partial, spot.slots_back[step], slots, 0) for step in range(size)]
@@ -1089,6 +1132,16 @@
         clip_came.append(from_back(block, step) if step else block)
 
     hidden = product(lefts, rights, kind=jnp.float32)
+    cross_blocks = [cross_rows] + [
+        lax.all_gather(after(piece, hidden), "dp", axis=0, tiled=True) for piece in cross_pieces
+    ]
+    cq_full = jnp.concatenate([block[:local_width] for block in cross_blocks], 0)
+    co_full = jnp.concatenate(
+        [block[local_width : 2 * local_width] for block in cross_blocks], 0
+    )
+    kv_full = jnp.concatenate(
+        [block[2 * local_width :, :text_width] for block in cross_blocks], 0
+    )
     residual_one, normed = row_call(
         first_norms_kernel,
         "first_norms",
@@ -1122,7 +1175,7 @@
             size,
             cut,
         )
-    queries, keys, values = cut
+    queries, keys, values, *self_keeps = cut
     no_pick = jnp.zeros((1,), jnp.int32)
     self_outputs, self_queries = [None] * size, None
     out_terms = [None] * size
@@ -1161,7 +1214,7 @@
         for head in range(local_heads)
     ]
     kv_columns = [key_columns, [column + local_width for column in key_columns]]
-    cross_keys, cross_values = cut_heads(
+    cross_keys, cross_values, *kv_keeps = cut_heads(
         context_kv, kv_gains, ("k", "v"), kv_columns, cross_extras
     )
 
@@ -1178,10 +1231,13 @@
 
     cross_pre = product([normed_cross], [cq_full], ROW_TIMES_ROW)
     query_columns = [[HEAD_DIM * head for head in range(all_heads)]]
-    (cross_queries,) = cut_heads(cross_pre, query_gains, ("q",), query_columns, cross_extras)
+    cross_queries, *query_keeps = cut_heads(
+        cross_pre, query_gains, ("q",), query_columns, cross_extras
+    )
     cross_outputs, cross_queries = attend(
         cross_queries, cross_keys, cross_values, cross_pick, tile, KEY_ROWS
     )
+    cross_outputs = after(cross_outputs, *cotangent_blocks[1:])
     residual_three, normed_mlp = row_call(
         add_norm_kernel,
         "mlp_norm",
@@ -1208,14 +1264,22 @@
                 for block in mlp_blocks[1:]
             ]
     mlp_came = send_terms(mlp_terms)
-    fc_sum = sum_product([after(one, *mlp_terms[1:]) for one in cotangent_blocks], active, 0, 2)
-    fc_sum = sum_product(mlp_blocks, expanded_grads, 1, 2, fc_sum)
+    fc2_sum = sum_product([after(one, *mlp_terms[1:]) for one in cotangent_blocks], active)
+    fc1_sum = sum_product([after(one, fc2_sum) for one in mlp_blocks], expanded_grads)
     for step in range(1, size):
-        fc_terms.append(product([after(active[step], fc_sum)], [fc2_weight]))
-    mlp_came = [after(came, fc_sum, *fc_terms) for came in mlp_came]
-    fc_sums = [Summing(fc_sum, spot)]
+        fc_terms.append(product([after(active[step], fc1_sum)], [fc2_weight]))
+    mlp_came = [after(came, fc1_sum, *fc_terms) for came in mlp_came]
+    fc2_total = scatter_rows(after(fc2_sum, *mlp_came))
+    fc_sums = [Summing(fc1_sum, spot)]
     fc_terms[1:] = [after(term, *mlp_came) for term in fc_terms[1:]]
     fc_came = send_terms(fc_terms)
+    joined_blocks = [chunk[0]]
+    for step in range(1, size):
+        if size == 2:
+            block = chunk[1]
+        else:
+            block = cut_at(joined, spot.joined_ahead[step], part, 1)
+        joined_blocks.append(from_back(after(block, *fc_terms), step))
 
     sent = advance_all(fc_sums, *mlp_came)
     mlp_came = [after(came, sent) for came in mlp_came]
@@ -1233,25 +1297,12 @@
     grad_cq, grad_ck, grad_cv = attend_back(
         cross_queries, cross_keys, cross_values, cross_slopes, cross_pick, tile, KEY_ROWS
     )
-    fc_came = [after(came, grad_cq) for came in fc_came]
-    block_output = residual_three + wide(fc_terms[0])
-    for came in fc_came:
-        block_output = block_output + wide(came)
-    block_output = low(block_output)
-    joined_blocks = [chunk[0]]
-    for step in range(1, size):
-        if size == 2:
-            block = chunk[1]
-        else:
-            block = cut_at(joined, spot.joined_ahead[step], part, 1)
-        block = after(block, *fc_terms)
-        joined_blocks.append(from_back(block, step))
-    grad_cq = after(grad_cq, block_output)
     cross_pre_grad, query_sums = join_heads(
-        cross_pre, query_gains, ("q",), query_columns, (grad_cq,)
+        query_keeps, query_gains, ("q",), query_columns, (grad_cq,)
     )
     cross_slope = product([cross_pre_grad], [cq_full])
-    cross_slope = after(cross_slope, *joined_blocks[1:])
+    fc_came = [after(came, cross_slope) for came in fc_came]
+    cross_slope = after(cross_slope, *fc_came, *joined_blocks[1:])
     grad_two, two_low, norm3_sum = row_call(
         norm_back_kernel,
         "cross_norm_back",
@@ -1261,8 +1312,12 @@
         [jnp.float32, jnp.bfloat16, 8],
     )
     two_blocks = gather_blocks(two_low)
+    block_output = residual_three + wide(fc_terms[0])
+    for came in fc_came:
+        block_output = block_output + wide(after(came, two_low))
+    block_output = low(block_output)
     context_kv_grad, key_sums = join_heads(
-        context_kv, kv_gains, ("k", "v"), kv_columns, (after(grad_ck, two_low), grad_cv)
+        kv_keeps, kv_gains, ("k", "v"), kv_columns, (after(grad_ck, two_low), grad_cv)
     )
     kv_sum = sum_product([context], [context_kv_grad])
     context_grad = product([context_kv_grad], [kv_full], kind=jnp.float32)
@@ -1281,7 +1336,8 @@
     two_blocks[1:] = [
         after(block, cross_sum, kv_sum, context_grad) for block in two_blocks[1:]
     ]
-    cross_sums = [Summing(kv_sum, spot), Summing(cross_sum, spot)]
+    cross_sums = [Summing(cross_sum, spot)]
+    kv_total = scatter_rows(after(kv_sum, *two_blocks[1:]))
     sent = advance_all(fc_sums + cross_sums, *two_blocks[1:])
     two_blocks[1:] = [after(block, sent) for block in two_blocks[1:]]
 
@@ -1306,7 +1362,7 @@
             text_local,
             2,
         )
-        clip_blocks.append(to_back(after(low(block), text_low), step) if step else block)
+        clip_blocks.append(low(block) if step else block)
     slopes = None
     for step in range(size):
         slopes = cut_grad(
@@ -1324,27 +1380,32 @@
         tokens,
     )
     sent = advance_all(fc_sums, head_grads[0])
-    head_grads = [
-        after(head_grads[0], sent, *text_blocks[1:], *clip_blocks[1:]),
-        *head_grads[1:],
-    ]
+    head_grads = [after(head_grads[0], sent, fc2_total, *text_blocks[1:]), *head_grads[1:]]
+    clip_came = [to_back(after(block, sent), step) for step, block in enumerate(clip_blocks)][1:]
     qkv_grads, normed_terms = [None] * size, [None] * size
     self_sums = 0.0
     for step in list(range(1, size)) + [0]:
         if step == 0:
-            head_grads = [after(head_grads[0], *normed_terms[1:]), *head_grads[1:]]
+            sent = advance_all(cross_sums, *normed_terms[1:])
+            head_grads = [after(head_grads[0], sent), *head_grads[1:]]
         qkv_grads[step], sums = join_heads(
-            qkv_blocks[step], self_gains, self_kinds, self_columns, head_grads, rope, step
+            self_keeps, self_gains, self_kinds, self_columns, head_grads, rope, step, size
         )
         self_sums = self_sums + sums
         normed_terms[step] = product([qkv_grads[step]], [qkv_rows])
     normed_came = send_terms(normed_terms)
+    text_blocks[0] = after(text_blocks[0], *normed_terms[1:])
+    project_all = low(spread_slots(text_blocks)).reshape(SMALL_PER * text_length, text_width)
+    t5_sum = sum_product([project_all], [t5_text.reshape(-1, t5_text.shape[2])])
+    out_sum = sum_product(after(two_blocks, t5_sum), self_outputs)
     qkv_sum = sum_product(normed_blocks, qkv_grads)
-    normed_terms[0] = after(normed_terms[0], qkv_sum)
+    normed_terms[0] = after(normed_terms[0], qkv_sum, out_sum)
     normed_came = [after(came, normed_terms[0]) for came in normed_came]
-    qkv_sums = [Summing(qkv_sum, spot)]
-    sent = advance_all(qkv_sums, *normed_came)
-    normed_came = [after(came, sent) for came in normed_came]
+    clip_blocks[1:] = [after(came, normed_terms[0]) for came in clip_came]
+    t5_sums, out_sums = [Summing(t5_sum, spot, True)], [Summing(out_sum, spot)]
+    qkv_total = scatter_rows(after(qkv_sum, *normed_came))
+    sent = advance_all(t5_sums + out_sums + fc_sums, *normed_came)
+    normed_came = [after(came, sent, *clip_blocks[1:]) for came in normed_came]
 
     hidden_low, first_sums, slot_sums = row_call(
         first_norms_back_kernel,
@@ -1355,18 +1416,6 @@
         [jnp.bfloat16, 8, "tile"],
     )
     hidden_blocks = gather_blocks(hidden_low)
-    sent = advance_all(qkv_sums + fc_sums + cross_sums, hidden_low)
-    out_sum = sum_product(after(two_blocks, sent), self_outputs)
-    text_blocks[0] = after(text_blocks[0], out_sum)
-    project_all = low(spread_slots(text_blocks)).reshape(SMALL_PER * text_length, text_width)
-    t5_sum = sum_product([project_all], [t5_text.reshape(-1, t5_text.shape[2])])
-    out_sums, t5_sums = [Summing(out_sum, spot)], [Summing(t5_sum, spot, True)]
-    hidden_blocks[1:] = [after(block, t5_sum) for block in hidden_blocks[1:]]
-    skip_sum = sum_product(hidden_blocks, joined_blocks)
-    skip_sums = [Summing(skip_sum, spot)]
-    sent = advance_all(skip_sums + out_sums + t5_sums + cross_sums + qkv_sums, skip_sum)
-    sent = advance_all(skip_sums + out_sums + t5_sums, sent)
-
     tongues = wide(my_languages[None, :] == jnp.arange(2, dtype=jnp.int32)[:, None])
     grad_lang = jnp.dot(tongues, jnp.sum(text_grad, 1), precision=PRECISE)
     gains = [
@@ -1380,12 +1429,36 @@
         norm2_sum[0],
         grad_lang.reshape(-1),
     ]
-    packed = after(jnp.concatenate(gains), t5_sum)
-    packed_came = swap_bit(packed, "dp", 0)
     shift_terms = jnp.zeros((SMALL_PER, width), jnp.float32)
     for number in range(rows // tile):
-        shift_terms += slot_masks[number][:, None] * after(slot_sums, t5_sum)[8 * number][None, :]
-    shift_sum = sum_over(shift_terms, "seq")
+        shift_terms += slot_masks[number][:, None] * after(slot_sums, hidden_low)[8 * number][None, :]
+    flat = jnp.concatenate(gains)
+    lines = -(-flat.shape[0] // width)
+    flat = jnp.pad(flat, (0, lines * width - flat.shape[0])).reshape(lines, width)
+    sent = advance_all(cross_sums + out_sums + t5_sums, shift_terms)
+    grad_fc1 = fc_sums[0].finish(sent)[0]
+    packed = after(jnp.concatenate([flat, shift_terms], 0), sent, grad_fc1)
+    packed_came = swap_bit(packed, "dp", 0)
+
+    def take(packed, came, bit):
+        rest = gather_step(packed[lines:], came[lines:], bit, spot)
+        return jnp.concatenate([packed[:lines] + came[:lines], rest], 0)
+
+    def next_step(packed, came, bit, hold):
+        packed = take(packed, after(came, hold), bit - 1)
+        return packed, swap_bit(packed, "dp", bit)
+
+    sent = advance_all(cross_sums + out_sums, packed)
+    packed, packed_came = next_step(packed, packed_came, 1, sent)
+    hidden_blocks[1:] = [after(block, packed) for block in hidden_blocks[1:]]
+    skip_sum = sum_product(hidden_blocks, joined_blocks)
+    last_sums = [Summing(skip_sum, spot)]
+    sent = advance_all(last_sums, skip_sum)
+    packed, packed_came = next_step(packed, packed_came, 2, sent)
+    sent = advance_all(last_sums, packed)
+    cross_total = cross_sums[0].finish(sent)
+    sent = cross_total
+
     hidden_low = after(hidden_low, sent)
     skip_blocks = [skip_weight]
     for mine, other in zip(skip_pieces, skip_others):
@@ -1393,16 +1466,18 @@
     joined_grads = [
         product([hidden_low], [block], ROW_TIMES_ROW, jnp.float32) for block in skip_blocks
     ]
-    fc_total = fc_sums[0].finish(*joined_grads)
-    grad_fc2, grad_fc1 = fc_total[0].T, fc_total[1]
-    sent = advance_all(qkv_sums + skip_sums + cross_sums, fc_total)
-    packed = packed + after(packed_came, sent)
-    shift_low = low(after(shift_sum, sent))
-    project_all = after(project_all, packed, shift_low)
+    for bit in range(3, lax.axis_size("dp").bit_length() - 1):
+        packed, packed_came = next_step(packed, packed_came, bit, joined_grads)
+        joined_grads[0] = after(joined_grads[0], packed)
+    sent = advance_all(last_sums + out_sums + t5_sums, *joined_grads)
+    project_all = after(project_all, sent)
     grad_t5 = product([project_all], [t5_weight], ROW_TIMES_ROW, jnp.float32)
     grad_t5 = grad_t5.reshape(t5_text.shape)
-    sent = advance_all(out_sums + t5_sums + skip_sums + qkv_sums, grad_t5)
-    sent = advance_all(out_sums + t5_sums, sent)
+    sent = grad_t5
+    packed = take(packed, after(packed_came, sent), lax.axis_size("dp").bit_length() - 2)
+    sent = advance_all(last_sums + out_sums + t5_sums, packed)
+    packed = sum_over(after(packed, sent), "seq")
+    sent = advance_all(last_sums + t5_sums, packed)
     clip_blocks[0] = after(clip_blocks[0], sent)
     grad_clip = spread_slots(clip_blocks)
     if size == 2:
@@ -1416,29 +1491,26 @@
             )
         grad_latent, grad_skip_input = joined_grad[:, :width], joined_grad[:, width:]
 
-    shift_all = gather_rows(shift_low, "dp", spot)
+    flat, totals, start = packed[:lines].reshape(-1), [], 0
+    for gain in gains:
+        totals.append(flat[start : start + gain.shape[0]])
+        start += gain.shape[0]
+    shift_all = low(packed[lines:])
     shift_mine = cut_at(shift_all, spot.me_columns, local_width, 1)
     gate_mine = cut_at(gate_all, spot.place_columns, width // parts, 1)
     grad_shift = dot_sum(gate_mine, shift_mine)
     (time_slope,) = silu_pull(sum_over(dot_rows(shift_mine, shift_weight), "seq"))
     grad_time = jnp.dot(wide(features_all).T, time_slope, precision=PRECISE)
 
-    grad_skip_weight = skip_sums[0].finish()[0].T
-    grad_qkv = qkv_sums[0].finish().reshape(-1, 3, local_width)
-    grad_out = out_sums[0].finish()[0].T
-    grad_t5_weight = t5_sums[0].finish()[0].T
-    kv_total, cross_total = [one.finish() for one in cross_sums]
-    grad_cross_kv = own_part(kv_total[0]).reshape(-1, 2, local_width)
+    grad_out = out_sums[0].finish(grad_shift)[0].T
+    grad_t5_weight = t5_sums[0].finish(grad_out)[0].T
+    grad_skip_weight = last_sums[0].finish(grad_t5_weight)[0].T
+    grad_qkv = wide(after(qkv_total, grad_skip_weight, kv_total)).reshape(-1, 3, local_width)
+    grad_fc2 = wide(after(fc2_total, grad_skip_weight)).T
+    grad_cross_kv = own_part(wide(after(kv_total, grad_out))).reshape(-1, 2, local_width)
     grad_cross_out = own_part(cross_total[0]).T
     grad_cross_query = own_part(cross_total[1])
 
-    for bit in range(1, lax.axis_size("dp").bit_length() - 1):
-        packed = packed + swap_bit(packed, "dp", bit)
-    packed = sum_over(packed, "seq")
-    totals, start = [], 0
-    for gain in gains:
-        totals.append(packed[start : start + gain.shape[0]])
-        start += gain.shape[0]
     return (
         block_output,
         grad_latent,

time: 894 us -> 797 us (0.89)
  waiting for transfers between devices: 169 us -> 89.8 us
  Pallas kernels: 364 us -> 335 us
  starting transfers between devices: 88.7 us -> 102 us
    ppermute x37 -> x26, waiting for transfers between devices: 61.7 us -> 23.5 us  [swap_bit(): return lax.ppermute(values, axis, [(i, i ^ 1 << bit) for i in range(size)])]
    pallas_call x4, Pallas kernels: 51.8 us -> 29.4 us  [join_heads(): pl.pallas_call(functools.partial(join_kernel, kinds=kinds, columns=column...]
    ppermute x10, waiting for transfers between devices: 58.9 us -> 38.1 us  [from_back(): lax.ppermute(values, 'seq', [(i, (i + step) % size) for i in range(size)])]
    ppermute x10, waiting for transfers between devices: 18.1 us -> 0.03 us  [to_back(): lax.ppermute(values, 'seq', [(i, (i - step) % size) for i in range(size)])]
    squeeze x30 -> x22, local copies, waits for them, and re-layouts: 37.5 us -> 21.6 us  [pick_at(): return lax.squeeze(cut_at(values, index, 1, axis), [axis])]
    unnamed x464 -> x508, local copies, waits for them, and re-layouts: 73.9 us -> 87 us
    add x28 -> x20, other arithmetic: 42.7 us -> 29.9 us  [advance(): held = self.keep + (after(self.came, *hold) if hold else self.came)]
    ppermute x7 -> x5, starting transfers between devices: 33.3 us -> 43.5 us  [advance(): lax.ppermute(held, 'dp', [(i, i ^ 1 << self.top) for i in senders])]
  transfers between devices with their start and end apart: 72 -> 60, of which waited for: 24 -> 17; matrix products, arithmetic and copies ran while one was open for 15% -> 19% of each run, Pallas kernels for 36% -> 39%
where the time goes in v3:
time: 797 us; the launch traced here: 786 us
  Pallas kernels  335 us (42%)
  local copies, waits for them, and re-layouts  141 us (18%)
  starting transfers between devices  102 us (13%)
  other arithmetic  89.8 us (11%)
  waiting for transfers between devices  89.8 us (11%)
  between operations  18.2 us (2%)
  matrix products  9.66 us (1%)
    pallas_call x25, Pallas kernels, product(): pl.pallas_call(functools.partial(product_kernel, form=form), grid=(pl.cdi...  95.7 us
    unnamed x508, local copies, waits for them, and re-layouts  87 us
    pallas_call x9, Pallas kernels, sum_product(): pl.pallas_call(functools.partial(sum_product_kernel, blocks=blocks), grid...  62 us
    ppermute x5, starting transfers between devices, advance(): lax.ppermute(held, 'dp', [(i, i ^ 1 << self.top) for i in senders])  43.5 us
    pallas_call x2, Pallas kernels, attend_back(): pl.pallas_call(functools.partial(attend_back_kernel, key_rows=key_rows),...  41.9 us
    ppermute x26, starting transfers between devices, swap_bit(): return lax.ppermute(values, axis, [(i, i ^ 1 << bit) for i in range(size)])  39.8 us
    ppermute x10, waiting for transfers between devices, from_back(): lax.ppermute(values, 'seq', [(i, (i + step) % size) for i in range(size)])  38.1 us
    add x20, other arithmetic, advance(): held = self.keep + (after(self.came, *hold) if hold else self.came)  29.9 us
  transfers between devices with their start and end apart: 60, of which 17 were waited for; matrix products, arithmetic and copies ran while one was open for 19% of the time, Pallas kernels for 39%

profile of v3, /device:TPU:15, one launch (start us, length us, event | category | flops | bytes accessed | tf_op | source)
XLA Modules:
  0.0 785.8 jit_solution(3094678738818988725)
XLA Ops:
  24.1 5.6 product.26.slope_ref
  35.5 6.9 fusion.1
  75.5 7.3 product.27.hidden_ref.refs_1_
  100.6 4.5 product.28.refs_0_
  105.2 6.1 cut_heads.4
  111.3 14.9 %collective-permute-done.7.refs_0_.refs_1_ = bf16[512,1408]{1,0:T(8,128)(2,1)S(1)} collective-permute-done((bf16[512,1408]{1,0:T(8,128)(2,1)S(1)}, bf16[512,1408]{1,0:T(8,128)(2,1)S(1)}, u32[]{:S(2)}, u32[]{:S(2)}) %collective-permute-start.7) | collective-permute-done | bytes 1441824 | tf_op jit(solution)/shard_map/ppermute | solution.py:696
  129.0 4.5 product.29.refs_0_
  133.5 6.1 cut_heads.5
  141.0 6.4 attend.3
  152.8 6.8 attend.4
  180.5 5.6 product.32.refs_0_
  186.2 8.9 %cut_heads.6 = (bf16[16,768,128]{2,1,0:T(8,128)(2,1)S(1)}, bf16[16,768,128]{2,1,0:T(8,128)(2,1)S(1)}, bf16[16,768,128]{2,1,0:T(8,128)(2,1)S(1)}) custom-call(bf16[768,2816]{1,0:T(8,128)(2,1)S(1)} %product.32.refs_0_, f32[8,128]{1,0:T(8,128)S(1)} %copy-done.140, f32[768,128]{1,0:T(8,128)S(1)} %copy-done.126), custom_call_target="tpu_custom_call" | custom-call | flops 2359296000 | bytes 1 | tf_op jit(solution)/shard_map/cut_heads/pallas_call | solution.py:170
  206.8 5.2 cut_heads.7
  212.1 11.3 %attend.5 = (bf16[512,1408]{1,0:T(8,128)(2,1)S(1)}, bf16[16,512,128]{2,1,0:T(8,128)(2,1)S(1)}) custom-call(s32[2]{0:T(128)S(1)} %copy-done.142, bf16[16,512,128]{2,1,0:T(8,128)(2,1)S(1)} %get-tuple-element.279.q_ref, bf16[16,768,128]{2,1,0:T(8,128)(2,1)S(1)} %get-tuple-element.275.k_ref, bf16[16,768,128]{2,1,0:T(8,128)(2,1)S(1)} %get-tuple-element.280.v_ref), custom_call_target="tpu_custom_call" | custom-call | flops 1572864000 | bytes 1 | tf_op jit(solution)/shard_map/attend/pallas_call | solution.py:317
  225.1 6.9 collective-permute-done.12.refs_0_.refs_1_
  238.1 12.8 %gelu_both.2 = (bf16[512,3072]{1,0:T(8,128)(2,1)S(1)}, bf16[512,3072]{1,0:T(8,128)(2,1)S(1)}) custom-call(bf16[512,1408]{1,0:T(8,128)(2,1)} %get-tuple-element.293.rows_ref.refs_0_, bf16[1408,3072]{1,0:T(8,128)(2,1)S(1)} %bitcast.191, bf16[512,3072]{1,0:T(8,128)(2,1)S(1)} %copy-done.44), custom_call_target="tpu_custom_call" | custom-call | flops 2200000000 | bytes 1 | tf_op jit(solution)/shard_map/gelu_both/pallas_call | solution.py:552
  251.0 5.0 product.35
  256.1 5.1 product.36.refs_2_
  261.2 5.7 product.37.slope_ref
  268.2 11.7 %gelu_both.3 = (bf16[512,3072]{1,0:T(8,128)(2,1)S(1)}, bf16[512,3072]{1,0:T(8,128)(2,1)S(1)}) custom-call(bf16[512,1408]{1,0:T(8,128)(2,1)} %collective-permute-done.13.rows_ref.refs_1_, bf16[1408,3072]{1,0:T(8,128)(2,1)S(1)} %bitcast.191, bf16[512,3072]{1,0:T(8,128)(2,1)S(1)} %product.37.slope_ref), custom_call_target="tpu_custom_call" | custom-call | flops 2200000000 | bytes 1 | tf_op jit(solution)/shard_map/gelu_both/pallas_call | solution.py:552
  279.9 6.2 product.38
  286.1 11.4 %sum_product.9 = bf16[1,1408,3072]{2,1,0:T(8,128)(2,1)S(1)} custom-call(bf16[512,1408]{1,0:T(8,128)(2,1)S(1)} %copy-done.32, bf16[512,1408]{1,0:T(8,128)(2,1)S(1)} %copy-done.100, bf16[512,3072]{1,0:T(8,128)(2,1)S(1)} %get-tuple-element.286.refs_0_.refs_2_, bf16[512,3072]{1,0:T(8,128)(2,1)S(1)} %get-tuple-element.295.refs_3_.refs_0_), custom_call_target="tpu_custom_call" | custom-call | flops 2562232064 | bytes 1 | tf_op jit(solution)/shard_map/sum_product/pallas_call | solution.py:475
  302.9 13.0 %sum_product.10 = bf16[1,1408,3072]{2,1,0:T(8,128)(2,1)S(1)} custom-call(bf16[512,1408]{1,0:T(8,128)(2,1)} %get-tuple-element.293.rows_ref.refs_0_, bf16[512,1408]{1,0:T(8,128)(2,1)} %collective-permute-done.13.rows_ref.refs_1_, bf16[512,3072]{1,0:T(8,128)(2,1)S(1)} %get-tuple-element.287.refs_0_.refs_2_, bf16[512,3072]{1,0:T(8,128)(2,1)S(1)} %copy-done.46), custom_call_target="tpu_custom_call" | custom-call | flops 2562232064 | bytes 1 | tf_op jit(solution)/shard_map/sum_product/pallas_call | solution.py:475
  315.9 5.0 product.39
  342.6 5.4 cut_grad.3.g_ref
  348.0 5.4 bitcast_add_fusion
  356.8 16.6 %attend_back.2 = (bf16[16,512,128]{2,1,0:T(8,128)(2,1)S(1)}, bf16[16,768,128]{2,1,0:T(8,128)(2,1)S(1)}, bf16[16,768,128]{2,1,0:T(8,128)(2,1)S(1)}) custom-call(s32[2]{0:T(128)S(1)} %copy-done.143, bf16[16,512,128]{2,1,0:T(8,128)(2,1)S(1)} %copy-done.122, bf16[16,768,128]{2,1,0:T(8,128)(2,1)S(1)} %copy-done.40, bf16[16,768,128]{2,1,0:T(8,128)(2,1)S(1)} %copy-done.42, ...), custom_call_target="tpu_custom_call" | custom-call | flops 2202009600 | bytes 1 | tf_op jit(solution)/shard_map/attend_back/pallas_call | solution.py:429
  375.0 4.5 join_heads.4
  382.2 10.0 %collective-permute-done.17.refs_3_ = bf16[512,1408]{1,0:T(8,128)(2,1)} collective-permute-done((bf16[512,1408]{1,0:T(8,128)(2,1)}, bf16[512,1408]{1,0:T(8,128)(2,1)}, u32[]{:S(2)}, u32[]{:S(2)}) %collective-permute-start.17) | collective-permute-done | bytes 1441824 | tf_op jit(solution)/shard_map/ppermute | solution.py:696
  405.2 7.9 %join_heads.5 = (bf16[768,2816]{1,0:T(8,128)(2,1)S(1)}, f32[8,128]{1,0:T(8,128)S(1)}) custom-call(f32[8,128]{1,0:T(8,128)S(1)} %copy-done.141, bf16[16,768,128]{2,1,0:T(8,128)(2,1)S(1)} %copy-done.145, bf16[16,768,128]{2,1,0:T(8,128)(2,1)S(1)} %copy-done.147, bf16[16,768,128]{2,1,0:T(8,128)(2,1)S(1)} %copy-done.153), custom_call_target="tpu_custom_call" | custom-call | flops 4423680000 | bytes 1 | tf_op jit(solution)/shard_map/join_heads/pallas_call | solution.py:258
  413.2 7.1 sum_product.13
  422.7 4.6 product.42
  463.8 25.4 %attend_back.3 = (bf16[8,1024,128]{2,1,0:T(8,128)(2,1)S(1)}, bf16[8,1024,128]{2,1,0:T(8,128)(2,1)S(1)}, bf16[8,1024,128]{2,1,0:T(8,128)(2,1)S(1)}) custom-call(s32[2]{0:T(128)S(1)} %broadcast.630.pick, bf16[8,1024,128]{2,1,0:T(8,128)(2,1)S(1)} %copy-done.124, bf16[8,1024,128]{2,1,0:T(8,128)(2,1)S(1)} %copy-done.78, bf16[8,1024,128]{2,1,0:T(8,128)(2,1)S(1)} %copy-done.80, ...), custom_call_target="tpu_custom_call" | custom-call | flops 5872025600 | bytes 1 | tf_op jit(solution)/shard_map/attend_back/pallas_call | solution.py:429
  495.6 5.1 collective-permute-start.25
  509.4 8.4 %join_heads.6 = (bf16[512,2112]{1,0:T(8,128)(2,1)S(1)}, f32[8,128]{1,0:T(8,128)S(1)}) custom-call(f32[8,128]{1,0:T(8,128)S(1)} %copy-done.129, f32[1024,384]{1,0:T(8,128)S(1)} %fusion.2.refs_2_.refs_1_, bf16[8,1024,128]{2,1,0:T(8,128)(2,1)S(1)} %copy-done.69, bf16[8,1024,128]{2,1,0:T(8,128)(2,1)S(1)} %copy-done.72, bf16[8,1024,128]{2,1,0:T(8,128)(2,1)S(1)} %copy-done.75, ...), custom_call_target="tpu_custom_call" | custom-call | flops 2211840000 | bytes 1 | tf_op jit(solution)/shard_map/join_heads/pallas_call | solution.py:258
  542.2 8.6 %join_heads.7 = (bf16[512,2112]{1,0:T(8,128)(2,1)S(1)}, f32[8,128]{1,0:T(8,128)S(1)}) custom-call(f32[8,128]{1,0:T(8,128)S(1)} %copy-done.130, f32[1024,384]{1,0:T(8,128)S(1)} %fusion.2.refs_2_.refs_1_, bf16[8,1024,128]{2,1,0:T(8,128)(2,1)S(1)} %copy-done.70, bf16[8,1024,128]{2,1,0:T(8,128)(2,1)S(1)} %copy-done.73, bf16[8,1024,128]{2,1,0:T(8,128)(2,1)S(1)} %copy-done.76, ...), custom_call_target="tpu_custom_call" | custom-call | flops 2211840000 | bytes 1 | tf_op jit(solution)/shard_map/join_heads/pallas_call | solution.py:258
  554.7 9.6 %sum_product.14 = bf16[1,1408,2112]{2,1,0:T(8,128)(2,1)S(1)} custom-call(bf16[512,1408]{1,0:T(8,128)(2,1)S(1)} %copy-done.91, bf16[512,1408]{1,0:T(8,128)(2,1)S(1)} %copy-done.93, bf16[512,2112]{1,0:T(8,128)(2,1)S(1)} %get-tuple-element.339.refs_0_.refs_2_, bf16[512,2112]{1,0:T(8,128)(2,1)S(1)} %get-tuple-element.336.refs_0_.refs_3_), custom_call_target="tpu_custom_call" | custom-call | flops 1824034560 | bytes 1 | tf_op jit(solution)/shard_map/sum_product/pallas_call | solution.py:475
  574.3 4.8 first_norms_back.1
  582.2 5.3 collective-permute-start.28
  595.2 14.0 %collective-permute-done.28 = bf16[2,176,1408]{2,1,0:T(8,128)(2,1)S(1)} collective-permute-done((bf16[2,176,1408]{2,1,0:T(8,128)(2,1)S(1)}, bf16[2,176,1408]{2,1,0:T(8,128)(2,1)S(1)}, u32[]{:S(2)}, u32[]{:S(2)}) %collective-permute-start.28) | collective-permute-done | bytes 991264 | tf_op jit(solution)/shard_map/ppermute | solution.py:859
  611.8 7.3 sum_product.17
  650.7 6.1 collective-permute-start.45
  660.0 13.9 %collective-permute-done.41 = bf16[1,2,176,1408]{3,2,1,0:T(8,128)(2,1)S(1)} collective-permute-done((bf16[1,2,176,1408]{3,2,1,0:T(8,128)(2,1)S(1)}, bf16[1,2,176,1408]{3,2,1,0:T(8,128)(2,1)S(1)}, u32[]{:S(2)}, u32[]{:S(2)}) %collective-permute-start.41) | collective-permute-done | bytes 991264 | tf_op jit(solution)/shard_map/ppermute | solution.py:736
  679.8 4.4 product.49
  684.2 17.7 %collective-permute-start.43 = (bf16[1,176,704]{2,1,0:T(8,128)(2,1)S(1)}, bf16[1,176,704]{2,1,0:T(8,128)(2,1)S(1)}, u32[]{:S(2)}, u32[]{:S(2)}) collective-permute-start(bf16[1,176,704]{2,1,0:T(8,128)(2,1)S(1)} %bitcast_add_fusion.13), channel_id=1, source_target_pairs={{2,18},{6,22},{10,26},{14,30},{16,0},{20,4},{24,8},{28,12},{3,19},... | collective-permute-start | bytes 743432 | tf_op jit(solution)/shard_map/ppermute | solution.py:859
  707.9 7.8 collective-permute-start.48
  718.4 13.4 %collective-permute-start.47 = (bf16[1,176,1408]{2,1,0:T(8,128)(2,1)S(1)}, bf16[1,176,1408]{2,1,0:T(8,128)(2,1)}, u32[]{:S(2)}, u32[]{:S(2)}) collective-permute-start(bf16[1,176,1408]{2,1,0:T(8,128)(2,1)S(1)} %bitcast_add_fusion.12), channel_id=1, source_target_pairs={{2,18},{6,22},{10,26},{14,30},{16,0},{20,4},{24,8},{28,12},{3,19},... | collective-permute-start | bytes 1486856 | tf_op jit(solution)/shard_map/ppermute | solution.py:859
  745.8 8.7 %collective-permute-done.47 = bf16[1,176,1408]{2,1,0:T(8,128)(2,1)} collective-permute-done((bf16[1,176,1408]{2,1,0:T(8,128)(2,1)S(1)}, bf16[1,176,1408]{2,1,0:T(8,128)(2,1)}, u32[]{:S(2)}, u32[]{:S(2)}) %collective-permute-start.47) | collective-permute-done | bytes 495648 | tf_op jit(solution)/shard_map/ppermute | solution.py:859
  (835 shorter events, 362.5 us)
Async XLA Ops:
  7.2 166.9 %all-gather.2.cloned.1.call-start = ((), (), s32[]{:S(2)}) async-start(), calls=%async_computation.3 | async-start | bytes 8425472 | tf_op jit(solution)/shard_map/all_gather | solution.py:1136
  11.4 56.5 %collective-permute-start = (bf16[704,1408]{1,0:T(8,128)(2,1)}, bf16[704,1408]{1,0:T(8,128)(2,1)}, u32[]{:S(2)}, u32[]{:S(2)}) collective-permute-start(bf16[704,1408]{1,0:T(8,128)(2,1)} %dynamic-slice_bitcast_fusion.5), channel_id=1, source_target_pairs={{0,1},{1,0},{2,3},{3,2},{4,5},{5,4},{6,7},{7,6},{8,9},{9,8},{10,11... | collective-permute-start | bytes 5947400 | tf_op jit(solution)/shard_map/ppermute | solution.py:696
  11.7 36.3 %collective-permute-start.1 = (s32[4]{0:T(128)}, s32[4]{0:T(128)}, u32[]{:S(2)}, u32[]{:S(2)}) collective-permute-start(s32[4]{0:T(128)} %param.36), channel_id=1, source_target_pairs={{0,2},{2,0},{4,6},{6,4},{8,10},{10,8},{12,14},{14,12},{16,18},{18,... | collective-permute-start | bytes 56 | tf_op jit(solution)/shard_map/ppermute | solution.py:736
  85.8 414.9 %reduce-scatter.6.cloned.1.call-start = ((), (), s32[]{:S(2)}) async-start(), calls=%async_computation.4 | async-start | bytes 9191424 | tf_op jit(solution)/shard_map/reduce_scatter | solution.py:817
  93.8 32.4 %collective-permute-start.7 = (bf16[512,1408]{1,0:T(8,128)(2,1)S(1)}, bf16[512,1408]{1,0:T(8,128)(2,1)S(1)}, u32[]{:S(2)}, u32[]{:S(2)}) collective-permute-start(bf16[512,1408]{1,0:T(8,128)(2,1)S(1)} %get-tuple-element.254.refs_0_), channel_id=1, source_target_pairs={{0,1},{1,0},{2,3},{3,2},{4,5},{5,4},{6,7},{7,6},{8,9},{9,8},{10,11... | collective-permute-start | bytes 4325384 | tf_op jit(solution)/shard_map/ppermute | solution.py:696
  94.1 57.9 %collective-permute-start.9 = (bf16[2,256,1024]{2,1,0:T(8,128)(2,1)S(1)}, bf16[2,256,1024]{2,1,0:T(8,128)(2,1)S(1)}, u32[]{:S(2)}, u32[]{:S(2)}) collective-permute-start(bf16[2,256,1024]{2,1,0:T(8,128)(2,1)S(1)} %constant_dynamic-slice_fusion.5), channel_id=1, source_target_pairs={{0,1},{1,0},{2,3},{3,2},{4,5},{5,4},{6,7},{7,6},{8,9},{9,8},{10,11... | collective-permute-start | bytes 3145736 | tf_op jit(solution)/shard_map/ppermute | solution.py:701
  97.6 54.4 %collective-permute-start.10 = (bf16[2,77,512]{2,0,1:T(2,128)(2,1)S(1)}, bf16[2,77,512]{2,0,1:T(2,128)(2,1)S(1)}, u32[]{:S(2)}, u32[]{:S(2)}) collective-permute-start(bf16[2,77,512]{2,0,1:T(2,128)(2,1)S(1)} %get-tuple-element.534), channel_id=1, source_target_pairs={{0,1},{1,0},{2,3},{3,2},{4,5},{5,4},{6,7},{7,6},{8,9},{9,8},{10,11... | collective-permute-start | bytes 473096 | tf_op jit(solution)/shard_map/ppermute | solution.py:696
  149.9 47.0 %collective-permute-start.8 = (bf16[512,1408]{1,0:T(8,128)(2,1)}, bf16[512,1408]{1,0:T(8,128)(2,1)}, u32[]{:S(2)}, u32[]{:S(2)}) collective-permute-start(bf16[512,1408]{1,0:T(8,128)(2,1)} %product.30), channel_id=1, source_target_pairs={{0,1},{1,0},{2,3},{3,2},{4,5},{5,4},{6,7},{7,6},{8,9},{9,8},{10,11... | collective-permute-start | bytes 4325384 | tf_op jit(solution)/shard_map/ppermute | solution.py:701
  200.9 31.2 %collective-permute-start.12 = (bf16[512,1408]{1,0:T(8,128)(2,1)S(1)}, bf16[512,1408]{1,0:T(8,128)(2,1)S(1)}, u32[]{:S(2)}, u32[]{:S(2)}) collective-permute-start(bf16[512,1408]{1,0:T(8,128)(2,1)S(1)} %copy-done.32), channel_id=1, source_target_pairs={{0,1},{1,0},{2,3},{3,2},{4,5},{5,4},{6,7},{7,6},{8,9},{9,8},{10,11... | collective-permute-start | bytes 4325384 | tf_op jit(solution)/shard_map/ppermute | solution.py:696
  237.6 30.6 %collective-permute-start.13 = (bf16[512,1408]{1,0:T(8,128)(2,1)}, bf16[512,1408]{1,0:T(8,128)(2,1)}, u32[]{:S(2)}, u32[]{:S(2)}) collective-permute-start(bf16[512,1408]{1,0:T(8,128)(2,1)} %get-tuple-element.293.rows_ref.refs_0_), channel_id=1, source_target_pairs={{0,1},{1,0},{2,3},{3,2},{4,5},{5,4},{6,7},{7,6},{8,9},{9,8},{10,11... | collective-permute-start | bytes 4325384 | tf_op jit(solution)/shard_map/ppermute | solution.py:696
  286.1 34.9 %collective-permute-start.14 = (bf16[512,1408]{1,0:T(8,128)(2,1)}, bf16[512,1408]{1,0:T(8,128)(2,1)}, u32[]{:S(2)}, u32[]{:S(2)}) collective-permute-start(bf16[512,1408]{1,0:T(8,128)(2,1)} %product.38), channel_id=1, source_target_pairs={{0,1},{1,0},{2,3},{3,2},{4,5},{5,4},{6,7},{7,6},{8,9},{9,8},{10,11... | collective-permute-start | bytes 4325384 | tf_op jit(solution)/shard_map/ppermute | solution.py:701
  323.5 24.5 %collective-permute-start.16 = (bf16[1,704,3072]{2,1,0:T(8,128)(2,1)}, bf16[1,704,3072]{2,1,0:T(8,128)(2,1)}, u32[]{:S(2)}, u32[]{:S(2)}) collective-permute-start(bf16[1,704,3072]{2,1,0:T(8,128)(2,1)} %dynamic-slice_bitcast_fusion), channel_id=1, source_target_pairs={{0,2},{2,0},{4,6},{6,4},{8,10},{10,8},{12,14},{14,12},{16,18},{18,... | collective-permute-start | bytes 12976136 | tf_op jit(solution)/shard_map/ppermute | solution.py:736
  327.6 414.5 %reduce-scatter.8.cloned.1.call-start = ((), (), s32[]{:S(2)}) async-start(), calls=%async_computation.5 | async-start | bytes 6127616 | tf_op jit(solution)/shard_map/reduce_scatter | solution.py:817
  327.6 54.5 %collective-permute-start.15 = (bf16[512,1408]{1,0:T(8,128)(2,1)}, bf16[512,1408]{1,0:T(8,128)(2,1)}, u32[]{:S(2)}, u32[]{:S(2)}) collective-permute-start(bf16[512,1408]{1,0:T(8,128)(2,1)} %copy-done.125), channel_id=1, source_target_pairs={{0,1},{1,0},{2,3},{3,2},{4,5},{5,4},{6,7},{7,6},{8,9},{9,8},{10,11... | collective-permute-start | bytes 4325384 | tf_op jit(solution)/shard_map/ppermute | solution.py:701
  329.1 63.0 %collective-permute-start.17 = (bf16[512,1408]{1,0:T(8,128)(2,1)}, bf16[512,1408]{1,0:T(8,128)(2,1)}, u32[]{:S(2)}, u32[]{:S(2)}) collective-permute-start(bf16[512,1408]{1,0:T(8,128)(2,1)} %copy-done.166), channel_id=1, source_target_pairs={{0,1},{1,0},{2,3},{3,2},{4,5},{5,4},{6,7},{7,6},{8,9},{9,8},{10,11... | collective-permute-start | bytes 4325384 | tf_op jit(solution)/shard_map/ppermute | solution.py:696
  356.7 72.2 %collective-permute-start.19 = (bf16[1,2,176,3072]{3,2,1,0:T(8,128)(2,1)}, bf16[1,2,176,3072]{3,2,1,0:T(8,128)(2,1)}, u32[]{:S(2)}, u32[]{:S(2)}) collective-permute-start(bf16[1,2,176,3072]{3,2,1,0:T(8,128)(2,1)} %dynamic-slice_bitcast_fusion.2), channel_id=1, source_target_pairs={{0,4},{2,6},{4,0},{6,2},{8,12},{10,14},{12,8},{14,10},{16,20},{18,... | collective-permute-start | bytes 6488072 | tf_op jit(solution)/shard_map/ppermute | solution.py:736
  396.5 32.4 %collective-permute-start.18 = (bf16[512,1408]{1,0:T(8,128)(2,1)S(1)}, bf16[512,1408]{1,0:T(8,128)(2,1)S(1)}, u32[]{:S(2)}, u32[]{:S(2)}) collective-permute-start(bf16[512,1408]{1,0:T(8,128)(2,1)S(1)} %get-tuple-element.341.refs_0_), channel_id=1, source_target_pairs={{0,1},{1,0},{2,3},{3,2},{4,5},{5,4},{6,7},{7,6},{8,9},{9,8},{10,11... | collective-permute-start | bytes 4325384 | tf_op jit(solution)/shard_map/ppermute | solution.py:696
  434.0 15.3 %collective-permute-start.20 = (bf16[2,704,1408]{2,1,0:T(8,128)(2,1)S(1)}, bf16[2,704,1408]{2,1,0:T(8,128)(2,1)}, u32[]{:S(2)}, u32[]{:S(2)}) collective-permute-start(bf16[2,704,1408]{2,1,0:T(8,128)(2,1)S(1)} %dynamic-slice_bitcast_fusion.1), channel_id=1, source_target_pairs={{0,2},{2,0},{4,6},{6,4},{8,10},{10,8},{12,14},{14,12},{16,18},{18,... | collective-permute-start | bytes 11894792 | tf_op jit(solution)/shard_map/ppermute | solution.py:736
  445.0 48.2 %collective-permute-start.21 = (bf16[1,176,3072]{2,1,0:T(8,128)(2,1)}, bf16[1,176,3072]{2,1,0:T(8,128)(2,1)}, u32[]{:S(2)}, u32[]{:S(2)}) collective-permute-start(bf16[1,176,3072]{2,1,0:T(8,128)(2,1)} %dynamic-slice_bitcast_fusion.7), channel_id=1, source_target_pairs={{0,8},{2,10},{4,12},{6,14},{8,0},{10,2},{12,4},{14,6},{16,24},{18,... | collective-permute-start | bytes 3244040 | tf_op jit(solution)/shard_map/ppermute | solution.py:736
  454.2 71.6 %collective-permute-start.23 = (bf16[2,2,176,1408]{3,2,1,0:T(8,128)(2,1)}, bf16[2,2,176,1408]{3,2,1,0:T(8,128)(2,1)}, u32[]{:S(2)}, u32[]{:S(2)}) collective-permute-start(bf16[2,2,176,1408]{3,2,1,0:T(8,128)(2,1)} %dynamic-slice_bitcast_fusion.4), channel_id=1, source_target_pairs={{0,4},{2,6},{4,0},{6,2},{8,12},{10,14},{12,8},{14,10},{16,20},{18,... | collective-permute-start | bytes 5947400 | tf_op jit(solution)/shard_map/ppermute | solution.py:736
  455.6 320.7 %reduce-scatter.10.cloned.1.call-start = ((), (), s32[]{:S(2)}) async-start(), calls=%async_computation.6 | async-start | bytes 6510592
  455.7 45.0 %collective-permute-start.22 = (bf16[2,256,1024]{2,1,0:T(8,128)(2,1)}, bf16[2,256,1024]{2,1,0:T(8,128)(2,1)}, u32[]{:S(2)}, u32[]{:S(2)}) collective-permute-start(bf16[2,256,1024]{2,1,0:T(8,128)(2,1)} %slice.285), channel_id=1, source_target_pairs={{0,1},{1,0},{2,3},{3,2},{4,5},{5,4},{6,7},{7,6},{8,9},{9,8},{10,11... | collective-permute-start | bytes 3145736 | tf_op jit(solution)/shard_map/ppermute | solution.py:701
  495.6 74.1 %collective-permute-start.25 = (bf16[1,176,3072]{2,1,0:T(8,128)(2,1)}, bf16[1,176,3072]{2,1,0:T(8,128)(2,1)}, u32[]{:S(2)}, u32[]{:S(2)}) collective-permute-start(bf16[1,176,3072]{2,1,0:T(8,128)(2,1)} %bitcast_add_fusion.6), channel_id=1, source_target_pairs={{2,18},{6,22},{10,26},{14,30},{16,0},{20,4},{24,8},{28,12},{3,19},... | collective-permute-start | bytes 3244040 | tf_op jit(solution)/shard_map/ppermute | solution.py:859
  500.7 66.3 %collective-permute-start.26 = (bf16[2,77,512]{2,0,1:T(2,128)(2,1)}, bf16[2,77,512]{2,0,1:T(2,128)(2,1)}, u32[]{:S(2)}, u32[]{:S(2)}) collective-permute-start(bf16[2,77,512]{2,0,1:T(2,128)(2,1)} %copy.84), channel_id=1, source_target_pairs={{0,1},{1,0},{2,3},{3,2},{4,5},{5,4},{6,7},{7,6},{8,9},{9,8},{10,11... | collective-permute-start | bytes 473096 | tf_op jit(solution)/shard_map/ppermute | solution.py:701
  524.2 42.8 %collective-permute-start.24 = (bf16[512,1408]{1,0:T(8,128)(2,1)S(1)}, bf16[512,1408]{1,0:T(8,128)(2,1)S(1)}, u32[]{:S(2)}, u32[]{:S(2)}) collective-permute-start(bf16[512,1408]{1,0:T(8,128)(2,1)S(1)} %product.45), channel_id=1, source_target_pairs={{0,1},{1,0},{2,3},{3,2},{4,5},{5,4},{6,7},{7,6},{8,9},{9,8},{10,11... | collective-permute-start | bytes 4325384 | tf_op jit(solution)/shard_map/ppermute | solution.py:701
  527.8 51.6 %collective-permute-start.27 = (bf16[2,176,1408]{2,1,0:T(8,128)(2,1)S(1)}, bf16[2,176,1408]{2,1,0:T(8,128)(2,1)S(1)}, u32[]{:S(2)}, u32[]{:S(2)}) collective-permute-start(bf16[2,176,1408]{2,1,0:T(8,128)(2,1)S(1)} %dynamic-slice_bitcast_fusion.10), channel_id=1, source_target_pairs={{0,8},{2,10},{4,12},{6,14},{8,0},{10,2},{12,4},{14,6},{16,24},{18,... | collective-permute-start | bytes 2973704 | tf_op jit(solution)/shard_map/ppermute | solution.py:736
  568.1 22.6 %collective-permute-start.29 = (bf16[1,512,1024]{2,1,0:T(8,128)(2,1)}, bf16[1,512,1024]{2,1,0:T(8,128)(2,1)}, u32[]{:S(2)}, u32[]{:S(2)}) collective-permute-start(bf16[1,512,1024]{2,1,0:T(8,128)(2,1)} %dynamic-slice_bitcast_fusion.8), channel_id=1, source_target_pairs={{0,2},{2,0},{4,6},{6,4},{8,10},{10,8},{12,14},{14,12},{16,18},{18,... | collective-permute-start | bytes 3145736 | tf_op jit(solution)/shard_map/ppermute | solution.py:736
  569.1 18.4 %collective-permute-start.30 = (bf16[1,704,704]{2,1,0:T(8,128)(2,1)}, bf16[1,704,704]{2,1,0:T(8,128)(2,1)}, u32[]{:S(2)}, u32[]{:S(2)}) collective-permute-start(bf16[1,704,704]{2,1,0:T(8,128)(2,1)} %dynamic-slice_bitcast_fusion.6), channel_id=1, source_target_pairs={{0,2},{2,0},{4,6},{6,4},{8,10},{10,8},{12,14},{14,12},{16,18},{18,... | collective-permute-start | bytes 2973704 | tf_op jit(solution)/shard_map/ppermute | solution.py:736
  572.9 20.1 %collective-permute-start.31 = (bf16[1,88,3072]{2,1,0:T(8,128)(2,1)}, bf16[1,88,3072]{2,1,0:T(8,128)(2,1)}, u32[]{:S(2)}, u32[]{:S(2)}) collective-permute-start(bf16[1,88,3072]{2,1,0:T(8,128)(2,1)} %dynamic-slice_bitcast_fusion.12), channel_id=1, source_target_pairs={{0,2},{4,6},{8,10},{12,14},{18,16},{22,20},{26,24},{30,28},{1,3},{... | collective-permute-start | bytes 1622024 | tf_op jit(solution)/shard_map/ppermute | solution.py:863
  579.1 32.7 %collective-permute-start.33 = (bf16[512,1408]{1,0:T(8,128)(2,1)S(1)}, bf16[512,1408]{1,0:T(8,128)(2,1)}, u32[]{:S(2)}, u32[]{:S(2)}) collective-permute-start(bf16[512,1408]{1,0:T(8,128)(2,1)S(1)} %get-tuple-element.373.refs_0_), channel_id=1, source_target_pairs={{0,1},{1,0},{2,3},{3,2},{4,5},{5,4},{6,7},{7,6},{8,9},{9,8},{10,11... | collective-permute-start | bytes 4325384 | tf_op jit(solution)/shard_map/ppermute | solution.py:696
  582.2 27.0 %collective-permute-start.28 = (bf16[2,176,1408]{2,1,0:T(8,128)(2,1)S(1)}, bf16[2,176,1408]{2,1,0:T(8,128)(2,1)S(1)}, u32[]{:S(2)}, u32[]{:S(2)}) collective-permute-start(bf16[2,176,1408]{2,1,0:T(8,128)(2,1)S(1)} %bitcast_add_fusion.9), channel_id=1, source_target_pairs={{2,18},{6,22},{10,26},{14,30},{16,0},{20,4},{24,8},{28,12},{3,19},... | collective-permute-start | bytes 2973704 | tf_op jit(solution)/shard_map/ppermute | solution.py:859
  589.2 21.1 %collective-permute-start.35 = (bf16[1,2,176,704]{3,2,1,0:T(8,128)(2,1)S(1)}, bf16[1,2,176,704]{3,2,1,0:T(8,128)(2,1)S(1)}, u32[]{:S(2)}, u32[]{:S(2)}) collective-permute-start(bf16[1,2,176,704]{3,2,1,0:T(8,128)(2,1)S(1)} %dynamic-slice_bitcast_fusion.11), channel_id=1, source_target_pairs={{0,4},{2,6},{4,0},{6,2},{8,12},{10,14},{12,8},{14,10},{16,20},{18,... | collective-permute-start | bytes 1486856 | tf_op jit(solution)/shard_map/ppermute | solution.py:736
  595.1 16.0 %collective-permute-start.34 = (f32[10,1408]{1,0:T(8,128)S(1)}, f32[10,1408]{1,0:T(8,128)S(1)}, u32[]{:S(2)}, u32[]{:S(2)}) collective-permute-start(f32[10,1408]{1,0:T(8,128)S(1)} %pad_maximum_fusion.8), channel_id=1, source_target_pairs={{0,2},{2,0},{4,6},{6,4},{8,10},{10,8},{12,14},{14,12},{16,18},{18,... | collective-permute-start | bytes 168968 | tf_op jit(solution)/shard_map/ppermute | solution.py:736
  630.0 48.6 %collective-permute-start.39 = (bf16[1,2,128,1024]{3,2,1,0:T(8,128)(2,1)}, bf16[1,2,128,1024]{3,2,1,0:T(8,128)(2,1)}, u32[]{:S(2)}, u32[]{:S(2)}) collective-permute-start(bf16[1,2,128,1024]{3,2,1,0:T(8,128)(2,1)} %dynamic-slice_bitcast_fusion.13), channel_id=1, source_target_pairs={{0,8},{2,10},{4,12},{6,14},{8,0},{10,2},{12,4},{14,6},{16,24},{18,... | collective-permute-start | bytes 1572872 | tf_op jit(solution)/shard_map/ppermute | solution.py:736
  631.3 44.0 %collective-permute-start.40 = (bf16[1,176,704]{2,1,0:T(8,128)(2,1)}, bf16[1,176,704]{2,1,0:T(8,128)(2,1)}, u32[]{:S(2)}, u32[]{:S(2)}) collective-permute-start(bf16[1,176,704]{2,1,0:T(8,128)(2,1)} %dynamic-slice_bitcast_fusion.17), channel_id=1, source_target_pairs={{0,8},{2,10},{4,12},{6,14},{8,0},{10,2},{12,4},{14,6},{16,24},{18,... | collective-permute-start | bytes 743432 | tf_op jit(solution)/shard_map/ppermute | solution.py:736
  634.1 16.0 %collective-permute-start.38 = (f32[22,1408]{1,0:T(8,128)S(1)}, f32[22,1408]{1,0:T(8,128)S(1)}, u32[]{:S(2)}, u32[]{:S(2)}) collective-permute-start(f32[22,1408]{1,0:T(8,128)S(1)} %pad_maximum_fusion.7), channel_id=1, source_target_pairs={{0,8},{2,10},{4,12},{6,14},{8,0},{10,2},{12,4},{14,6},{16,24},{18,... | collective-permute-start | bytes 371720 | tf_op jit(solution)/shard_map/ppermute | solution.py:736
  650.2 23.7 %collective-permute-start.41 = (bf16[1,2,176,1408]{3,2,1,0:T(8,128)(2,1)S(1)}, bf16[1,2,176,1408]{3,2,1,0:T(8,128)(2,1)S(1)}, u32[]{:S(2)}, u32[]{:S(2)}) collective-permute-start(bf16[1,2,176,1408]{3,2,1,0:T(8,128)(2,1)S(1)} %copy-done.189), channel_id=1, source_target_pairs={{0,4},{2,6},{4,0},{6,2},{8,12},{10,14},{12,8},{14,10},{16,20},{18,... | collective-permute-start | bytes 2973704 | tf_op jit(solution)/shard_map/ppermute | solution.py:736
  650.7 33.5 %collective-permute-start.45 = (f32[38,1408]{1,0:T(8,128)S(1)}, f32[38,1408]{1,0:T(8,128)S(1)}, u32[]{:S(2)}, u32[]{:S(2)}) collective-permute-start(f32[38,1408]{1,0:T(8,128)S(1)} %pad_maximum_fusion.6), channel_id=1, source_target_pairs={{0,16},{2,18},{4,20},{6,22},{8,24},{10,26},{12,28},{14,30},{16,0},... | collective-permute-start | bytes 642056 | tf_op jit(solution)/shard_map/ppermute | solution.py:736
  656.9 58.8 %collective-permute-start.55 = (bf16[88,704]{1,0:T(8,128)(2,1)S(1)}, bf16[88,704]{1,0:T(8,128)(2,1)S(1)}, u32[]{:S(2)}, u32[]{:S(2)}) collective-permute-start(bf16[88,704]{1,0:T(8,128)(2,1)S(1)} %slice.286), channel_id=1, source_target_pairs={{0,1},{1,0},{2,3},{3,2},{4,5},{5,4},{6,7},{7,6},{8,9},{9,8},{10,11... | collective-permute-start | bytes 371720 | tf_op jit(solution)/shard_map/ppermute | solution.py:701
  673.9 43.8 %collective-permute-start.53 = (bf16[88,704]{1,0:T(8,128)(2,1)S(1)}, bf16[88,704]{1,0:T(8,128)(2,1)S(1)}, u32[]{:S(2)}, u32[]{:S(2)}) collective-permute-start(bf16[88,704]{1,0:T(8,128)(2,1)S(1)} %slice.287), channel_id=1, source_target_pairs={{0,1},{1,0},{2,3},{3,2},{4,5},{5,4},{6,7},{7,6},{8,9},{9,8},{10,11... | collective-permute-start | bytes 371720 | tf_op jit(solution)/shard_map/ppermute | solution.py:701
  675.3 26.8 %collective-permute-start.44 = (bf16[1,176,1408]{2,1,0:T(8,128)(2,1)S(1)}, bf16[1,176,1408]{2,1,0:T(8,128)(2,1)S(1)}, u32[]{:S(2)}, u32[]{:S(2)}) collective-permute-start(bf16[1,176,1408]{2,1,0:T(8,128)(2,1)S(1)} %dynamic-slice_bitcast_fusion.14), channel_id=1, source_target_pairs={{0,8},{2,10},{4,12},{6,14},{8,0},{10,2},{12,4},{14,6},{16,24},{18,... | collective-permute-start | bytes 1486856 | tf_op jit(solution)/shard_map/ppermute | solution.py:736
  684.2 22.0 %collective-permute-start.43 = (bf16[1,176,704]{2,1,0:T(8,128)(2,1)S(1)}, bf16[1,176,704]{2,1,0:T(8,128)(2,1)S(1)}, u32[]{:S(2)}, u32[]{:S(2)}) collective-permute-start(bf16[1,176,704]{2,1,0:T(8,128)(2,1)S(1)} %bitcast_add_fusion.13), channel_id=1, source_target_pairs={{2,18},{6,22},{10,26},{14,30},{16,0},{20,4},{24,8},{28,12},{3,19},... | collective-permute-start | bytes 743432 | tf_op jit(solution)/shard_map/ppermute | solution.py:859
  707.9 25.9 %collective-permute-start.48 = (f32[70,1408]{1,0:T(8,128)S(1)}, f32[70,1408]{1,0:T(8,128)S(1)}, u32[]{:S(2)}, u32[]{:S(2)}) collective-permute-start(f32[70,1408]{1,0:T(8,128)S(1)} %pad_maximum_fusion.5), channel_id=1, source_target_pairs={{0,1},{1,0},{2,3},{3,2},{4,5},{5,4},{6,7},{7,6},{8,9},{9,8},{10,11... | collective-permute-start | bytes 1182728 | tf_op jit(solution)/shard_map/ppermute | solution.py:736
  716.4 20.0 %collective-permute-start.51 = (bf16[1,88,704]{2,1,0:T(8,128)(2,1)S(1)}, bf16[1,88,704]{2,1,0:T(8,128)(2,1)S(1)}, u32[]{:S(2)}, u32[]{:S(2)}) collective-permute-start(bf16[1,88,704]{2,1,0:T(8,128)(2,1)S(1)} %dynamic-slice_bitcast_fusion.20), channel_id=1, source_target_pairs={{0,2},{4,6},{8,10},{12,14},{18,16},{22,20},{26,24},{30,28},{1,3},{... | collective-permute-start | bytes 371720 | tf_op jit(solution)/shard_map/ppermute | solution.py:863
  718.4 36.1 %collective-permute-start.47 = (bf16[1,176,1408]{2,1,0:T(8,128)(2,1)S(1)}, bf16[1,176,1408]{2,1,0:T(8,128)(2,1)}, u32[]{:S(2)}, u32[]{:S(2)}) collective-permute-start(bf16[1,176,1408]{2,1,0:T(8,128)(2,1)S(1)} %bitcast_add_fusion.12), channel_id=1, source_target_pairs={{2,18},{6,22},{10,26},{14,30},{16,0},{20,4},{24,8},{28,12},{3,19},... | collective-permute-start | bytes 1486856 | tf_op jit(solution)/shard_map/ppermute | solution.py:859
  731.8 27.4 %collective-permute-start.46 = (bf16[1,128,1024]{2,1,0:T(8,128)(2,1)S(1)}, bf16[1,128,1024]{2,1,0:T(8,128)(2,1)}, u32[]{:S(2)}, u32[]{:S(2)}) collective-permute-start(bf16[1,128,1024]{2,1,0:T(8,128)(2,1)S(1)} %bitcast_add_fusion.14), channel_id=1, source_target_pairs={{2,18},{6,22},{10,26},{14,30},{16,0},{20,4},{24,8},{28,12},{3,19},... | collective-permute-start | bytes 786440 | tf_op jit(solution)/shard_map/ppermute | solution.py:859
  743.7 22.0 %collective-permute-start.54 = (bf16[64,1408]{1,0:T(8,128)(2,1)}, bf16[64,1408]{1,0:T(8,128)(2,1)}, u32[]{:S(2)}, u32[]{:S(2)}) collective-permute-start(bf16[64,1408]{1,0:T(8,128)(2,1)} %slice.222), channel_id=1, source_target_pairs={{0,1},{1,0},{2,3},{3,2},{4,5},{5,4},{6,7},{7,6},{8,9},{9,8},{10,11... | collective-permute-start | bytes 540680 | tf_op jit(solution)/shard_map/ppermute | solution.py:701
  743.7 29.6 %collective-permute-start.52 = (f32[64,1408]{1,0:T(8,128)}, f32[64,1408]{1,0:T(8,128)}, u32[]{:S(2)}, u32[]{:S(2)}) collective-permute-start(f32[64,1408]{1,0:T(8,128)} %fusion.20), channel_id=1, source_target_pairs={{0,1},{1,0},{2,3},{3,2},{4,5},{5,4},{6,7},{7,6},{8,9},{9,8},{10,11... | collective-permute-start | bytes 1081352 | tf_op jit(solution)/shard_map/ppermute | solution.py:736
  (265 other events, 1809.0 us)
Sparse Core Ops, SparseCore 0:
  85.9 72.2 all-gather.1
  327.7 127.0 reduce-scatter.5
  458.7 108.6 reduce-scatter.7
  628.6 129.7 reduce-scatter.9
